TPU v7x, 32 devices: a whole 2x2x4 slice. The times are simulated.
32 devices in a mesh: grp: 4 (over y, core), dev: 8 (over z, x).
Axes of the slice: x: 2, y: 2, z: 4, core: 2. Of those that a mesh axis runs over, the one named last changes fastest.
Arguments:
- a_blocks: bfloat16 [1024, 7, 128, 128], P(('grp', 'dev')), may hold values from -0.5 to 0.5
- p_blocks: bfloat16 [1024, 128, 128], P(('grp', 'dev')), may hold values from -0.5 to 0.5
- neighbours: int32 [1024, 6], P(('grp', 'dev')), may hold values from 0 to 31
- coarse_slot: int32 [1024, 7], P(('grp', 'dev')), may hold values from 0 to 6
- owner: int32 [1024, 1], P(('grp', 'dev')), may hold values from 0 to 7; in each aligned block of 32 rows (0 to 31, 32 to 63, ...) at most 8 rows name the same one
- agg_local: int32 [1024], P(('grp', 'dev')), may hold values from 0 to 7
Outputs:
- coarse: bfloat16 [256, 7, 128, 128], P(('grp', 'dev'))
Inputs may be any that keep to these rules, and one draw needn't show every extreme that they name: Among the elements of one device at most 8 have the same owner, and in every draw some device has exactly 8 elements with one owner.
All inputs are finite; a program needn't handle non-finite values.
Results may differ from a plain program's by a relative error of at most 0.008.
Values may be sent and summed in bfloat16 or wider, within the bound.
No kernel may reach another device: no remote copies, remote signals or barrier semaphores. Data moves between devices by JAX's collectives and lax.ppermute only.
A program may use at most 128 MiB of HBM per device.

v0:
```python
import jax
import jax.numpy as jnp
from jax import lax
from jax.sharding import PartitionSpec as P

KC = 7


def with_halo(block, sides, width):
    for axis, dim in sides:
        count = lax.axis_size(axis)
        forward = [(i, i + 1) for i in range(count - 1)]
        backward = [(target, source) for source, target in forward]
        low = lax.ppermute(
            lax.slice_in_dim(block, block.shape[dim] - width, None, axis=dim), axis, forward
        )
        high = lax.ppermute(lax.slice_in_dim(block, 0, width, axis=dim), axis, backward)
        block = jnp.concatenate([low, block, high], axis=dim)
    return block


def slot_table(slot_rows):
    return (slot_rows[:, :, None] == jnp.arange(KC, dtype=jnp.int32)[None, None, :]).astype(
        jnp.float32
    )


def on_device(a_blocks, p_blocks, neighbours, coarse_slot, owner, agg_local):
    elems = p_blocks.shape[0]
    width = p_blocks.shape[1]
    groups = lax.axis_size("dev")
    cap = max(2, 2 * elems // groups)
    rows = groups * cap
    aggs = elems // 4
    lifted = p_blocks.reshape(1, 1, elems, width, width)
    padded = with_halo(lifted, (("grp", 0), ("dev", 1)), 1)
    sources = (
        p_blocks,
        p_blocks,
        padded[1, 0, :],
        padded[1, 2, :],
        padded[0, 1, :],
        padded[2, 1, :],
    )
    faces = [p_blocks] + [jnp.take(sources[face], neighbours[:, face], axis=0) for face in range(6)]
    facing = jnp.stack(faces, 1)
    applied = jnp.einsum(
        "efik,efkj->efij", a_blocks, facing, preferred_element_type=jnp.float32
    ).astype(jnp.bfloat16)
    targets = owner[:, 0]
    order = jnp.arange(elems, dtype=jnp.int32)
    same_owner = targets[:, None] == targets[None, :]
    slot_rows = jnp.arange(rows, dtype=jnp.int32)[:, None]
    keys = targets * aggs + agg_local
    same_key = keys[:, None] == keys[None, :]
    firstidx = jnp.min(jnp.where(same_key, order[None, :], elems), 1)
    first = firstidx == order
    before = first[None, :] & same_owner & (order[None, :] < firstidx[:, None])
    position = targets * cap + jnp.sum(before.astype(jnp.int32), 1)
    placing = slot_rows == position[None, :]
    leading = (placing & first[None, :]).astype(jnp.int32)
    labels = jnp.sum(leading * (agg_local[None, :] + 1), 1) - 1
    weighted = jnp.einsum("eki,efkj->efij", p_blocks, applied, preferred_element_type=jnp.float32)
    mixing = (
        placing.astype(jnp.float32)[:, None, :, None]
        * jnp.transpose(slot_table(coarse_slot), (2, 0, 1))[None, :, :, :]
    )
    send_terms = jnp.einsum(
        "rsef,efij->rsij", mixing, weighted, precision=lax.Precision.HIGHEST
    ).astype(jnp.bfloat16)
    got_terms, got_labels = (
        lax.all_to_all(send_terms, "dev", split_axis=0, concat_axis=0, tiled=True),
        lax.all_to_all(labels, "dev", split_axis=0, concat_axis=0, tiled=True),
    )
    matching = (got_labels[:, None] == jnp.arange(aggs, dtype=jnp.int32)[None, :]).astype(
        jnp.bfloat16
    )
    coarse = jnp.einsum("ra,rsij->asij", matching, got_terms, preferred_element_type=jnp.float32)
    return coarse.astype(jnp.bfloat16)


def solution(mesh):
    placed = (
        P(("grp", "dev"), None, None, None),
        P(("grp", "dev"), None, None),
        P(("grp", "dev"), None),
        P(("grp", "dev"), None),
        P(("grp", "dev"), None),
        P(("grp", "dev")),
    )
    return jax.shard_map(
        on_device,
        mesh=mesh,
        in_specs=placed,
        out_specs=P(("grp", "dev"), None, None, None),
        check_vma=False,
    )
```

profile of v0, /device:TPU:0, one launch (start us, length us, event | category | flops | bytes accessed | tf_op | source)
XLA Modules:
  0.0 573.1 jit_solution(8157755177344992589)
XLA Ops:
  0.0 1.4 collective-permute-start.1
  1.4 3.1 collective-permute-start
  5.4 1.5 collective-permute-done
  7.9 3.2 pad_maximum_fusion
  13.3 7.2 %collective-permute-start.2 = (bf16[3,1,32,128,128]{4,3,2,1,0:T(8,128)(2,1)}, bf16[3,1,32,128,128]{4,3,2,1,0:T(8,128)(2,1)}, u32[]{:S(2)}, u32[]{:S(2)}) collective-permute-start(bf16[3,1,32,128,128]{4,3,2,1,0:T(8,128)(2,1)} %pad_maximum_fusion), channel_id=1, source_target_pairs={{0,1},{1,2},{2,3},{3,4},{4,5},{5,6},{6,7},{8,9},{9,10},{10,11},{11... | collective-permute-start | bytes 9437192 | tf_op jit(solution)/shard_map/ppermute | solution.py:14
  21.9 5.4 all-to-all-start
  27.3 2.3 copy.20
  31.1 1.7 gather_fusion
  32.8 1.6 copy.21
  35.7 2.5 bitcast_dynamic-update-slice_fusion.6
  40.8 2.0 gather_fusion.5
  43.5 2.9 gather_fusion.4
  46.3 1.6 copy.25
  48.0 27.0 %collective-permute-done.3 = bf16[3,1,32,128,128]{4,3,2,1,0:T(8,128)(2,1)} collective-permute-done((bf16[3,1,32,128,128]{4,3,2,1,0:T(8,128)(2,1)}, bf16[3,1,32,128,128]{4,3,2,1,0:T(8,128)(2,1)}, u32[]{:S(2)}, u32[]{:S(2)}) %collective-permute-start.3) | collective-permute-done | bytes 3145760 | tf_op jit(solution)/shard_map/ppermute | solution.py:17
  74.9 2.3 slice_bitcast_fusion
  77.3 2.9 gather_fusion.3
  80.2 2.3 copy.24
  82.4 70.6 %collective-permute-done.2 = bf16[3,1,32,128,128]{4,3,2,1,0:T(8,128)(2,1)} collective-permute-done((bf16[3,1,32,128,128]{4,3,2,1,0:T(8,128)(2,1)}, bf16[3,1,32,128,128]{4,3,2,1,0:T(8,128)(2,1)}, u32[]{:S(2)}, u32[]{:S(2)}) %collective-permute-start.2) | collective-permute-done | bytes 3145760 | tf_op jit(solution)/shard_map/ppermute | solution.py:14
  153.0 2.3 slice_bitcast_fusion.1
  155.3 2.9 gather_fusion.2
  158.2 2.3 copy.23
  160.5 2.5 bitcast_dynamic-update-slice_fusion.3
  163.0 2.5 bitcast_dynamic-update-slice_fusion.2
  165.4 1.3 bitcast_dynamic-update-slice_fusion.1
  168.0 13.4 %convolution_bitcast_fusion = f32[32,7,128,128]{2,3,1,0:T(8,128)} fusion(bf16[32,7,128,128]{2,3,1,0:T(8,128)(2,1)} %bitcast_dynamic-update-slice_fusion, bf16[32,7,128,128]{3,2,1,0:T(8,128)(2,1)} %param.8, bf16[32,128,128]{2,1,0:T(8,128)(2,1)S(1)} %copy-done), kind=kOutput, calls=%fused_computation.11 | convolution fusion | flops 1882718208 | bytes 30408704 | tf_op jit(solution)/shard_map/eki,efkj->efij/dot_general | solution.py:63
  181.5 16.5 %copy.27 = f32[32,7,128,128]{3,0,1,2:T(8,128)} copy(f32[32,7,128,128]{2,3,1,0:T(8,128)} %convolution_bitcast_fusion) | data formatting | bytes 29360128 | tf_op jit(solution)/shard_map/eki,efkj->efij/transpose | solution.py:63
  198.0 26.8 %bitcast_convert_fusion = bf16[64,7,128,128]{3,0,2,1:T(8,128)(2,1)S(1)} fusion(f32[32,7,128,128]{3,0,1,2:T(8,128)} %copy.27, f32[64,7,32,7,1]{0,2,3,4,1:T(8,128)S(1)} %copy-done.3), kind=kOutput, calls=%fused_computation.6 | convolution fusion | flops 19737346048 | bytes 29761536 | tf_op jit(solution)/shard_map/rsef,efij->rsij/dot_general | solution.py:68
  224.8 10.6 %copy.28 = bf16[64,7,128,128]{3,2,1,0:T(8,128)(2,1)} copy(bf16[64,7,128,128]{3,0,2,1:T(8,128)(2,1)S(1)} %bitcast_convert_fusion) | data formatting | bytes 29360128 | tf_op jit(solution)/shard_map/convert_element_type | solution.py:70
  235.3 7.3 %all-to-all-start.1 = ((bf16[64,7,128,128]{3,2,1,0:T(8,128)(2,1)}), bf16[64,7,128,128]{3,2,1,0:T(8,128)(2,1)}, u32[]{:S(2)}, u32[]{:S(2)}) async-start(bf16[64,7,128,128]{3,2,1,0:T(8,128)(2,1)} %copy.28), calls=%async_computation.1 | async-start | bytes 29360128 | tf_op jit(solution)/shard_map/all_to_all | solution.py:72
  243.9 314.5 %all-to-all-done.1 = bf16[64,7,128,128]{3,2,1,0:T(8,128)(2,1)} async-done(((bf16[64,7,128,128]{3,2,1,0:T(8,128)(2,1)}), bf16[64,7,128,128]{3,2,1,0:T(8,128)(2,1)}, u32[]{:S(2)}, u32[]{:S(2)}) %all-to-all-start.1) | async-done | bytes 14680096 | tf_op jit(solution)/shard_map/all_to_all | solution.py:72
  558.4 13.0 %fusion.10 = bf16[8,7,128,128]{3,0,2,1:T(8,128)(2,1)S(1)} fusion(bf16[64,7,128,128]{3,2,1,0:T(8,128)(2,1)} %all-to-all-done.1, s32[64]{0:T(128)S(1)} %eq.93), kind=kOutput, calls=%fused_computation.16 | convolution fusion | flops 118358528 | bytes 16515328 | tf_op jit(solution)/shard_map/ra,rsij->asij/dot_general | solution.py:78
  571.4 1.7 copy.30
  (41 shorter events, 14.0 us)
Async XLA Ops:
  0.0 29.6 %copy-start = (bf16[32,128,128]{2,1,0:T(8,128)(2,1)S(1)}, bf16[32,128,128]{2,1,0:T(8,128)(2,1)}, u32[]{:S(2)}) copy-start(bf16[32,128,128]{2,1,0:T(8,128)(2,1)} %param.9) | copy-start | bytes 3145732
  0.0 29.6 %copy-start.5 = (s32[32,6]{0,1:T(8,128)S(1)}, s32[32,6]{0,1:T(8,128)}, u32[]{:S(2)}) copy-start(s32[32,6]{0,1:T(8,128)} %param.10) | copy-start | bytes 2308
  0.0 5.4 collective-permute-start.1
  1.4 5.5 collective-permute-start
  5.4 29.1 %copy-start.4 = (s32[32,7]{0,1:T(8,128)S(1)}, s32[32,7]{0,1:T(8,128)}, u32[]{:S(2)}) copy-start(s32[32,7]{0,1:T(8,128)} %param.11) | copy-start | bytes 2692
  5.4 5.7 copy-start.2
  6.9 1.0 copy-start.1
  11.1 63.8 %collective-permute-start.3 = (bf16[3,1,32,128,128]{4,3,2,1,0:T(8,128)(2,1)}, bf16[3,1,32,128,128]{4,3,2,1,0:T(8,128)(2,1)}, u32[]{:S(2)}, u32[]{:S(2)}) collective-permute-start(bf16[3,1,32,128,128]{4,3,2,1,0:T(8,128)(2,1)} %pad_maximum_fusion), channel_id=1, source_target_pairs={{1,0},{2,1},{3,2},{4,3},{5,4},{6,5},{7,6},{9,8},{10,9},{11,10},{12... | collective-permute-start | bytes 9437192 | tf_op jit(solution)/shard_map/ppermute | solution.py:17
  13.3 139.7 %collective-permute-start.2 = (bf16[3,1,32,128,128]{4,3,2,1,0:T(8,128)(2,1)}, bf16[3,1,32,128,128]{4,3,2,1,0:T(8,128)(2,1)}, u32[]{:S(2)}, u32[]{:S(2)}) collective-permute-start(bf16[3,1,32,128,128]{4,3,2,1,0:T(8,128)(2,1)} %pad_maximum_fusion), channel_id=1, source_target_pairs={{0,1},{1,2},{2,3},{3,4},{4,5},{5,6},{6,7},{8,9},{9,10},{10,11},{11... | collective-permute-start | bytes 9437192 | tf_op jit(solution)/shard_map/ppermute | solution.py:14
  21.9 213.4 %all-to-all-start = ((s32[8,8,1]{1,2,0:T(1,128)}), s32[8,8,1]{1,2,0:T(1,128)S(1)}, u32[]{:S(2)}, u32[]{:S(2)}) async-start(s32[8,8,1]{1,2,0:T(1,128)} %bitcast.1), calls=%async_computation | async-start | bytes 8192 | tf_op jit(solution)/shard_map/all_to_all | solution.py:73
  181.5 16.5 %copy-start.3 = (f32[64,7,32,7,1]{0,2,3,4,1:T(8,128)S(1)}, f32[64,7,32,7,1]{0,2,3,4,1:T(8,128)}, u32[]{:S(2)}) copy-start(f32[64,7,32,7,1]{0,2,3,4,1:T(8,128)} %fusion.30) | copy-start | bytes 1204228
  235.3 323.0 %all-to-all-start.1 = ((bf16[64,7,128,128]{3,2,1,0:T(8,128)(2,1)}), bf16[64,7,128,128]{3,2,1,0:T(8,128)(2,1)}, u32[]{:S(2)}, u32[]{:S(2)}) async-start(bf16[64,7,128,128]{3,2,1,0:T(8,128)(2,1)} %copy.28), calls=%async_computation.1 | async-start | bytes 29360128 | tf_op jit(solution)/shard_map/all_to_all | solution.py:72
where the time goes:
time: 578 us; the launch traced here: 573 us
  waiting for transfers between devices  414 us (72%)
  local copies, waits for them, and re-layouts  62.6 us (11%)
  matrix products  53.3 us (9%)
  starting transfers between devices  25.6 us (4%)
  other arithmetic  17.8 us (3%)
    all_to_all x1, waiting for transfers between devices, on_device(): lax.all_to_all(send_terms, 'dev', split_axis=0, concat_axis=0, tiled=True)  314 us
    ppermute x2, waiting for transfers between devices, with_halo(): lax.ppermute(lax.slice_in_dim(block, block.shape[dim] - width, None, axis...  72.1 us
    ppermute x2, waiting for transfers between devices, with_halo(): lax.ppermute(lax.slice_in_dim(block, 0, width, axis=dim), axis, backward)  27 us
    dot_general x1, matrix products, on_device(): jnp.einsum('rsef,efij->rsij', mixing, weighted, precision=lax.Precision.H...  26.8 us
    gather x12, local copies, waits for them, and re-layouts, on_device(): jnp.take(sources[face], neighbours[:, face], axis=0)  22.1 us
    transpose x1, local copies, waits for them, and re-layouts, on_device(): jnp.einsum('eki,efkj->efij', p_blocks, applied, preferred_element_type=jn...  16.5 us
    dot_general x1, matrix products, on_device(): jnp.einsum('eki,efkj->efij', p_blocks, applied, preferred_element_type=jn...  13.4 us
    dot_general x1, matrix products, on_device(): jnp.einsum('ra,rsij->asij', matching, got_terms, preferred_element_type=j...  13 us
  transfers between devices with their start and end apart: 6, of which 4 were waited for; matrix products, arithmetic and copies ran while one was open for 20% of the time, Pallas kernels for 0%

commit v1 on v0

v1 whole, which is shorter than its diff:
```python
import functools

import jax
import jax.numpy as jnp
from jax import lax
from jax.experimental import pallas as pl
from jax.experimental.pallas import tpu as pltpu
from jax.sharding import PartitionSpec as P

KC = 7
FACES = 6
VMEM_BYTES = 40 * 1024 * 1024


def ring_order(count):
    nx = 1 << ((count.bit_length() - 1) // 2)
    nz = count // nx
    if nx < 2 or nz < 2 or nz % 2 or nx * nz != count:
        return list(range(count))
    walk = [(z, 0) for z in range(nz)]
    for step, z in enumerate(reversed(range(nz))):
        xs = range(1, nx)
        walk += [(z, x) for x in (xs if step % 2 == 0 else reversed(xs))]
    return [z * nx + x for z, x in walk]


def chunk_kernel(
    distance, rel, agg, near, slot, a_ref, own, below, above, left, right,
    low, high, acc, a_buf, t_buf, picked, sems,
):
    elems = rel.shape[0]
    half = low.shape[0]
    width = own.shape[1]

    def pick(e, count):
        hit = rel[e] == distance

        @pl.when(hit)
        def _():
            picked[count] = e

        return count + hit.astype(jnp.int32)

    count = lax.fori_loop(0, elems, pick, jnp.int32(0))

    def fetch(i, buf):
        return pltpu.make_async_copy(a_ref.at[picked[i]], a_buf.at[buf], sems.at[buf])

    @pl.when(count > 0)
    def _():
        fetch(0, 0).start()

    acc[...] = jnp.zeros_like(acc)
    sources = (own, own, below, above, left, right)

    def element(i, carry):
        buf = lax.rem(i, 2)

        @pl.when(i + 1 < count)
        def _():
            fetch(i + 1, 1 - buf).start()

        e = picked[i]
        fetch(i, buf).wait()
        p_e = own[e]
        for f in range(KC):
            facing = p_e if f == 0 else sources[f - 1][near[e * FACES + f - 1]]
            t_buf[:, f * width : (f + 1) * width] = jnp.dot(
                a_buf[buf, f], facing, preferred_element_type=jnp.float32
            ).astype(jnp.bfloat16)
        weighted = lax.dot_general(
            p_e, t_buf[...], (((0,), (0,)), ((), ())), preferred_element_type=jnp.float32
        )
        a = agg[e]
        for f in range(KC):
            row = a * KC + slot[e * KC + f]
            acc[row] = acc[row] + weighted[:, f * width : (f + 1) * width]
        return carry

    lax.fori_loop(0, count, element, 0)
    for r in range(2 * half):
        out = low if r < half else high
        for s in range(KC):
            out[r % half, s] = acc[r * KC + s].astype(jnp.bfloat16)


def chunk(distance, aggs, tables, a_blocks, blocks):
    elems, _, width, _ = a_blocks.shape
    half = aggs // 2
    out = jax.ShapeDtypeStruct((half, KC, width, width), jnp.bfloat16)
    smem = pl.BlockSpec(memory_space=pltpu.SMEM)
    vmem = pl.BlockSpec(memory_space=pltpu.VMEM)
    return pl.pallas_call(
        functools.partial(chunk_kernel, distance),
        out_shape=(out, out),
        in_specs=[smem] * 4 + [pl.BlockSpec(memory_space=pl.ANY)] + [vmem] * 5,
        out_specs=(vmem, vmem),
        scratch_shapes=[
            pltpu.VMEM((aggs * KC, width, width), jnp.float32),
            pltpu.VMEM((2, KC, width, width), jnp.bfloat16),
            pltpu.VMEM((width, KC * width), jnp.bfloat16),
            pltpu.SMEM((elems,), jnp.int32),
            pltpu.SemaphoreType.DMA((2,)),
        ],
        compiler_params=pltpu.CompilerParams(vmem_limit_bytes=VMEM_BYTES),
        cost_estimate=pl.CostEstimate(
            flops=4 * KC * width**3 * 4, bytes_accessed=12 * 1024 * 1024, transcendentals=0
        ),
    )(*tables, a_blocks, *blocks)


def add(*terms):
    return sum(t.astype(jnp.float32) for t in terms).astype(jnp.bfloat16)


def on_device(a_blocks, p_blocks, neighbours, coarse_slot, owner, agg_local):
    elems = p_blocks.shape[0]
    aggs = elems // 4
    count = lax.axis_size("dev")

    halo = []
    for axis in ("dev", "grp"):
        size = lax.axis_size(axis)
        forward = [(i, i + 1) for i in range(size - 1)]
        backward = [(b, a) for a, b in forward]
        halo += [lax.ppermute(p_blocks, axis, forward), lax.ppermute(p_blocks, axis, backward)]
    blocks = (p_blocks, *halo)

    order = ring_order(count)
    place = [order.index(d) for d in range(count)]
    index = jnp.arange(count, dtype=jnp.int32)
    places = jnp.array(place, jnp.int32)
    mine = jnp.sum(jnp.where(index == lax.axis_index("dev"), places, 0))
    theirs = jnp.sum(jnp.where(owner == index[None, :], places[None, :], 0), 1)
    rel = lax.rem(theirs - mine + count, count)
    tables = (rel, agg_local, neighbours.reshape(-1), coarse_slot.reshape(-1))

    chunks = {}

    def part(distance, side):
        distance %= count
        if distance not in chunks:
            chunks[distance] = chunk(distance, aggs, tables, a_blocks, blocks)
        return chunks[distance][side]

    right = [(order[i], order[(i + 1) % count]) for i in range(count)]
    left = [(b, a) for a, b in right]
    far = count // 2
    got = {}
    for n in range(2 * far - 1):
        distance = far - (n + 1) // 2
        for sign, perm in ((1, right), (-1, left)):
            side = n % 2 if sign > 0 else 1 - n % 2
            terms = [part(sign * distance, side)]
            if n >= 2:
                terms.append(got[sign, n - 2])
            got[sign, n] = lax.ppermute(terms[0] if n < 2 else add(*terms), "dev", perm)
    last = 2 * far - 2
    low = add(part(0, 0), got[1, last], got[-1, last - 1])
    high = add(part(0, 1), got[1, last - 1], got[-1, last])
    return jnp.concatenate([low, high], 0)


def solution(mesh):
    placed = (
        P(("grp", "dev"), None, None, None),
        P(("grp", "dev"), None, None),
        P(("grp", "dev"), None),
        P(("grp", "dev"), None),
        P(("grp", "dev"), None),
        P(("grp", "dev")),
    )
    return jax.shard_map(
        on_device,
        mesh=mesh,
        in_specs=placed,
        out_specs=P(("grp", "dev"), None, None, None),
        check_vma=False,
    )
```

time: 578 us -> 214 us (0.37)
  waiting for transfers between devices: 414 us -> 128 us
  local copies, waits for them, and re-layouts: 62.6 us -> 6.7 us
  matrix products: 53.3 us -> 0 us
  Pallas kernels: 0 us -> 38 us
  other arithmetic: 17.8 us -> 8.91 us
  starting transfers between devices: 25.6 us -> 31.7 us
    all_to_all x2 -> x0, waiting for transfers between devices: 314 us -> none  [the longest x1 314 us: on_device(): lax.all_to_all(send_terms, 'dev', split_axis=0, concat_axis=0, tiled=True)]
    dot_general x3 -> x0, matrix products: 53.3 us -> none  [the longest x1 26.8 us: on_device(): jnp.einsum('rsef,efij->rsij', mixing, weighted, precision=lax.Precision.H...]
    pallas_call x0 -> x8, Pallas kernels: none -> 38 us  [chunk(): pl.pallas_call(functools.partial(chunk_kernel, distance), out_shape=(out,...]
    ppermute x4 -> x18, waiting for transfers between devices: 99.1 us -> 128 us  [the longest x14 88.3 us: on_device(): got[sign, n] = lax.ppermute(terms[0] if n < 2 else add(*terms), 'dev', perm)]
    gather x12 -> x0, local copies, waits for them, and re-layouts: 22.1 us -> none  [on_device(): jnp.take(sources[face], neighbours[:, face], axis=0)]
    ppermute x4 -> x18, starting transfers between devices: 12.9 us -> 31.7 us  [the longest x14 19.6 us: on_device(): got[sign, n] = lax.ppermute(terms[0] if n < 2 else add(*terms), 'dev', perm)]
    transpose x1 -> x0, local copies, waits for them, and re-layouts: 16.5 us -> none  [on_device(): jnp.einsum('eki,efkj->efij', p_blocks, applied, preferred_element_type=jn...]
    all_to_all x2 -> x0, starting transfers between devices: 12.7 us -> none  [the longest x1 7.27 us: on_device(): lax.all_to_all(send_terms, 'dev', split_axis=0, concat_axis=0, tiled=True)]
  transfers between devices with their start and end apart: 6 -> 18, of which waited for: 4 -> 12; matrix products, arithmetic and copies ran while one was open for 20% -> 4% of each run, Pallas kernels for 0% -> 16%
where the time goes in v1:
time: 214 us
  waiting for transfers between devices  128 us (60%)
  Pallas kernels  38 us (18%)
  starting transfers between devices  31.7 us (15%)
  other arithmetic  8.91 us (4%)
  local copies, waits for them, and re-layouts  6.7 us (3%)
    ppermute x14, waiting for transfers between devices, on_device(): got[sign, n] = lax.ppermute(terms[0] if n < 2 else add(*terms), 'dev', perm)  88.3 us
    pallas_call x8, Pallas kernels, chunk(): pl.pallas_call(functools.partial(chunk_kernel, distance), out_shape=(out,...  38 us
    ppermute x2, waiting for transfers between devices, on_device(): lax.ppermute(p_blocks, axis, forward)  23.6 us
    ppermute x14, starting transfers between devices, on_device(): got[sign, n] = lax.ppermute(terms[0] if n < 2 else add(*terms), 'dev', perm)  19.6 us
    ppermute x2, waiting for transfers between devices, on_device(): lax.ppermute(p_blocks, axis, backward)  16.2 us
    ppermute x2, starting transfers between devices, on_device(): lax.ppermute(p_blocks, axis, forward)  9.58 us
    unnamed x8, local copies, waits for them, and re-layouts  6.5 us
    convert_element_type x12, other arithmetic, add(): return sum((t.astype(jnp.float32) for t in terms)).astype(jnp.bfloat16)  4.82 us
  transfers between devices with their start and end apart: 18, of which 12 were waited for; matrix products, arithmetic and copies ran while one was open for 4% of the time, Pallas kernels for 16%

profile of v1, /device:TPU:0, one launch (start us, length us, event | category | flops | bytes accessed | tf_op | source)
XLA Modules:
  0.0 213.7 jit_solution(17801900648216225664)
XLA Ops:
  0.0 1.3 collective-permute-start.3
  1.3 3.1 %collective-permute-start.2 = (bf16[32,128,128]{2,1,0:T(8,128)(2,1)}, bf16[32,128,128]{2,1,0:T(8,128)(2,1)S(1)}, u32[]{:S(2)}, u32[]{:S(2)}) collective-permute-start(bf16[32,128,128]{2,1,0:T(8,128)(2,1)} %own.15), channel_id=1, source_target_pairs={{0,8},{8,16},{16,24},{1,9},{9,17},{17,25},{2,10},{10,18},{18,26},{... | collective-permute-start | bytes 3145736 | tf_op jit(solution)/shard_map/ppermute | solution.py:126
  4.4 1.3 collective-permute-start.1
  5.7 6.5 %collective-permute-start = (bf16[32,128,128]{2,1,0:T(8,128)(2,1)}, bf16[32,128,128]{2,1,0:T(8,128)(2,1)}, u32[]{:S(2)}, u32[]{:S(2)}) collective-permute-start(bf16[32,128,128]{2,1,0:T(8,128)(2,1)} %own.15), channel_id=1, source_target_pairs={{0,1},{1,2},{2,3},{3,4},{4,5},{5,6},{6,7},{8,9},{9,10},{10,11},{11... | collective-permute-start | bytes 3145736 | tf_op jit(solution)/shard_map/ppermute | solution.py:126
  13.9 1.3 fusion
  16.7 16.2 %collective-permute-done.1.above = bf16[32,128,128]{2,1,0:T(8,128)(2,1)S(1)} collective-permute-done((bf16[32,128,128]{2,1,0:T(8,128)(2,1)}, bf16[32,128,128]{2,1,0:T(8,128)(2,1)S(1)}, u32[]{:S(2)}, u32[]{:S(2)}) %collective-permute-start.1) | collective-permute-done | bytes 1048608 | tf_op jit(solution)/shard_map/ppermute | solution.py:126
  32.9 23.5 %collective-permute-done.below = bf16[32,128,128]{2,1,0:T(8,128)(2,1)} collective-permute-done((bf16[32,128,128]{2,1,0:T(8,128)(2,1)}, bf16[32,128,128]{2,1,0:T(8,128)(2,1)}, u32[]{:S(2)}, u32[]{:S(2)}) %collective-permute-start) | collective-permute-done | bytes 1048608 | tf_op jit(solution)/shard_map/ppermute | solution.py:126
  56.4 3.1 %copy-done = bf16[32,7,128,128]{3,2,1,0:T(8,128)(2,1)S(1)} copy-done((bf16[32,7,128,128]{3,2,1,0:T(8,128)(2,1)S(1)}, bf16[32,7,128,128]{3,2,1,0:T(8,128)(2,1)}, u32[]{:S(2)}) %copy-start) | copy-done | bytes 7340056
  61.4 4.7 %shard_map.77 = (bf16[4,7,128,128]{3,2,1,0:T(8,128)(2,1)S(1)}, bf16[4,7,128,128]{3,2,1,0:T(8,128)(2,1)S(1)}) custom-call(s32[32]{0:T(128)S(1)} %compare_select_fusion.rel, s32[32]{0:T(128)S(1)} %copy-done.2, s32[192]{0:T(256)S(1)} %reshape.7.near, s32[224]{0:T(256)S(1)} %reshape.8.slot, bf16[32,7,128,128]{3,2,1,0:T(8,128)(2,1)S(1)} %copy-done, ...), custom_call_target="tpu_custom_call" | custom-call | flops 234881024 | bytes 12582912 | tf_op jit(solution)/shard_map/pallas_call | solution.py:93
  66.2 1.9 collective-permute-start.14
  68.0 2.6 %collective-permute-start.4 = (bf16[4,7,128,128]{3,2,1,0:T(8,128)(2,1)S(1)}, bf16[4,7,128,128]{3,2,1,0:T(8,128)(2,1)S(1)}, u32[]{:S(2)}, u32[]{:S(2)}) collective-permute-start(bf16[4,7,128,128]{3,2,1,0:T(8,128)(2,1)S(1)} %get-tuple-element.25), channel_id=1, source_target_pairs={{0,2},{2,4},{4,6},{6,7},{7,5},{5,3},{3,1},{1,0},{8,10},{10,12},{12... | collective-permute-start | bytes 2752520 | tf_op jit(solution)/shard_map/ppermute | solution.py:157
  70.6 3.4 %shard_map.76 = (bf16[4,7,128,128]{3,2,1,0:T(8,128)(2,1)S(1)}, bf16[4,7,128,128]{3,2,1,0:T(8,128)(2,1)S(1)}) custom-call(s32[32]{0:T(128)S(1)} %compare_select_fusion.rel, s32[32]{0:T(128)S(1)} %copy-done.2, s32[192]{0:T(256)S(1)} %reshape.7.near, s32[224]{0:T(256)S(1)} %reshape.8.slot, bf16[32,7,128,128]{3,2,1,0:T(8,128)(2,1)S(1)} %copy-done, ...), custom_call_target="tpu_custom_call" | custom-call | flops 234881024 | bytes 12582912 | tf_op jit(solution)/shard_map/pallas_call | solution.py:93
  74.0 3.4 %collective-permute-start.11 = (bf16[4,7,128,128]{3,2,1,0:T(8,128)(2,1)S(1)}, bf16[4,7,128,128]{3,2,1,0:T(8,128)(2,1)S(1)}, u32[]{:S(2)}, u32[]{:S(2)}) collective-permute-start(bf16[4,7,128,128]{3,2,1,0:T(8,128)(2,1)S(1)} %get-tuple-element.32), channel_id=1, source_target_pairs={{0,2},{2,4},{4,6},{6,7},{7,5},{5,3},{3,1},{1,0},{8,10},{10,12},{12... | collective-permute-start | bytes 2752520 | tf_op jit(solution)/shard_map/ppermute | solution.py:157
  77.4 7.5 %shard_map.80 = (bf16[4,7,128,128]{3,2,1,0:T(8,128)(2,1)S(1)}, bf16[4,7,128,128]{3,2,1,0:T(8,128)(2,1)S(1)}) custom-call(s32[32]{0:T(128)S(1)} %compare_select_fusion.rel, s32[32]{0:T(128)S(1)} %copy-done.2, s32[192]{0:T(256)S(1)} %reshape.7.near, s32[224]{0:T(256)S(1)} %reshape.8.slot, bf16[32,7,128,128]{3,2,1,0:T(8,128)(2,1)S(1)} %copy-done, ...), custom_call_target="tpu_custom_call" | custom-call | flops 234881024 | bytes 12582912 | tf_op jit(solution)/shard_map/pallas_call | solution.py:93
  84.9 6.3 %collective-permute-done.14 = bf16[4,7,128,128]{3,2,1,0:T(8,128)(2,1)S(1)} collective-permute-done((bf16[4,7,128,128]{3,2,1,0:T(8,128)(2,1)S(1)}, bf16[4,7,128,128]{3,2,1,0:T(8,128)(2,1)S(1)}, u32[]{:S(2)}, u32[]{:S(2)}) %collective-permute-start.14) | collective-permute-done | bytes 917536 | tf_op jit(solution)/shard_map/ppermute | solution.py:157
  94.3 6.1 %shard_map.79 = (bf16[4,7,128,128]{3,2,1,0:T(8,128)(2,1)S(1)}, bf16[4,7,128,128]{3,2,1,0:T(8,128)(2,1)S(1)}) custom-call(s32[32]{0:T(128)S(1)} %compare_select_fusion.rel, s32[32]{0:T(128)S(1)} %copy-done.2, s32[192]{0:T(256)S(1)} %reshape.7.near, s32[224]{0:T(256)S(1)} %reshape.8.slot, bf16[32,7,128,128]{3,2,1,0:T(8,128)(2,1)S(1)} %copy-done, ...), custom_call_target="tpu_custom_call" | custom-call | flops 234881024 | bytes 12582912 | tf_op jit(solution)/shard_map/pallas_call | solution.py:93
  100.4 3.4 %shard_map.75 = (bf16[4,7,128,128]{3,2,1,0:T(8,128)(2,1)S(1)}, bf16[4,7,128,128]{3,2,1,0:T(8,128)(2,1)S(1)}) custom-call(s32[32]{0:T(128)S(1)} %compare_select_fusion.rel, s32[32]{0:T(128)S(1)} %copy-done.2, s32[192]{0:T(256)S(1)} %reshape.7.near, s32[224]{0:T(256)S(1)} %reshape.8.slot, bf16[32,7,128,128]{3,2,1,0:T(8,128)(2,1)S(1)} %copy-done, ...), custom_call_target="tpu_custom_call" | custom-call | flops 234881024 | bytes 12582912 | tf_op jit(solution)/shard_map/pallas_call | solution.py:93
  103.8 7.2 %collective-permute-done.11 = bf16[4,7,128,128]{3,2,1,0:T(8,128)(2,1)S(1)} collective-permute-done((bf16[4,7,128,128]{3,2,1,0:T(8,128)(2,1)S(1)}, bf16[4,7,128,128]{3,2,1,0:T(8,128)(2,1)S(1)}, u32[]{:S(2)}, u32[]{:S(2)}) %collective-permute-start.11) | collective-permute-done | bytes 917536 | tf_op jit(solution)/shard_map/ppermute | solution.py:157
  111.4 2.5 %collective-permute-start.12 = (bf16[4,7,128,128]{3,2,1,0:T(8,128)(2,1)S(1)}, bf16[4,7,128,128]{3,2,1,0:T(8,128)(2,1)S(1)}, u32[]{:S(2)}, u32[]{:S(2)}) collective-permute-start(bf16[4,7,128,128]{3,2,1,0:T(8,128)(2,1)S(1)} %add_convert_fusion.5), channel_id=1, source_target_pairs={{0,2},{2,4},{4,6},{6,7},{7,5},{5,3},{3,1},{1,0},{8,10},{10,12},{12... | collective-permute-start | bytes 2752520 | tf_op jit(solution)/shard_map/ppermute | solution.py:157
  115.3 19.2 %collective-permute-done.8 = bf16[4,7,128,128]{3,2,1,0:T(8,128)(2,1)S(1)} collective-permute-done((bf16[4,7,128,128]{3,2,1,0:T(8,128)(2,1)S(1)}, bf16[4,7,128,128]{3,2,1,0:T(8,128)(2,1)S(1)}, u32[]{:S(2)}, u32[]{:S(2)}) %collective-permute-start.8) | collective-permute-done | bytes 917536 | tf_op jit(solution)/shard_map/ppermute | solution.py:157
  135.4 2.1 collective-permute-start.6
  137.5 4.1 %shard_map.78 = (bf16[4,7,128,128]{3,2,1,0:T(8,128)(2,1)S(1)}, bf16[4,7,128,128]{3,2,1,0:T(8,128)(2,1)S(1)}) custom-call(s32[32]{0:T(128)S(1)} %compare_select_fusion.rel, s32[32]{0:T(128)S(1)} %copy-done.2, s32[192]{0:T(256)S(1)} %reshape.7.near, s32[224]{0:T(256)S(1)} %reshape.8.slot, bf16[32,7,128,128]{3,2,1,0:T(8,128)(2,1)S(1)} %copy-done, ...), custom_call_target="tpu_custom_call" | custom-call | flops 234881024 | bytes 12582912 | tf_op jit(solution)/shard_map/pallas_call | solution.py:93
  141.5 5.4 %shard_map.74 = (bf16[4,7,128,128]{3,2,1,0:T(8,128)(2,1)S(1)}, bf16[4,7,128,128]{3,2,1,0:T(8,128)(2,1)S(1)}) custom-call(s32[32]{0:T(128)S(1)} %compare_select_fusion.rel, s32[32]{0:T(128)S(1)} %copy-done.2, s32[192]{0:T(256)S(1)} %reshape.7.near, s32[224]{0:T(256)S(1)} %reshape.8.slot, bf16[32,7,128,128]{3,2,1,0:T(8,128)(2,1)S(1)} %copy-done, ...), custom_call_target="tpu_custom_call" | custom-call | flops 234881024 | bytes 12582912 | tf_op jit(solution)/shard_map/pallas_call | solution.py:93
  147.0 3.3 %collective-permute-done.12 = bf16[4,7,128,128]{3,2,1,0:T(8,128)(2,1)S(1)} collective-permute-done((bf16[4,7,128,128]{3,2,1,0:T(8,128)(2,1)S(1)}, bf16[4,7,128,128]{3,2,1,0:T(8,128)(2,1)S(1)}, u32[]{:S(2)}, u32[]{:S(2)}) %collective-permute-start.12) | collective-permute-done | bytes 917536 | tf_op jit(solution)/shard_map/ppermute | solution.py:157
  150.7 2.5 %collective-permute-start.13 = (bf16[4,7,128,128]{3,2,1,0:T(8,128)(2,1)S(1)}, bf16[4,7,128,128]{3,2,1,0:T(8,128)(2,1)S(1)}, u32[]{:S(2)}, u32[]{:S(2)}) collective-permute-start(bf16[4,7,128,128]{3,2,1,0:T(8,128)(2,1)S(1)} %add_convert_fusion.4), channel_id=1, source_target_pairs={{0,2},{2,4},{4,6},{6,7},{7,5},{5,3},{3,1},{1,0},{8,10},{10,12},{12... | collective-permute-start | bytes 2752520 | tf_op jit(solution)/shard_map/ppermute | solution.py:157
  154.7 19.2 %collective-permute-done.9 = bf16[4,7,128,128]{3,2,1,0:T(8,128)(2,1)S(1)} collective-permute-done((bf16[4,7,128,128]{3,2,1,0:T(8,128)(2,1)S(1)}, bf16[4,7,128,128]{3,2,1,0:T(8,128)(2,1)S(1)}, u32[]{:S(2)}, u32[]{:S(2)}) %collective-permute-start.9) | collective-permute-done | bytes 917536 | tf_op jit(solution)/shard_map/ppermute | solution.py:157
  174.7 2.1 collective-permute-start.7
  176.8 3.4 %shard_map.73 = (bf16[4,7,128,128]{3,2,1,0:T(8,128)(2,1)S(1)}, bf16[4,7,128,128]{3,2,1,0:T(8,128)(2,1)S(1)}) custom-call(s32[32]{0:T(128)S(1)} %compare_select_fusion.rel, s32[32]{0:T(128)S(1)} %copy-done.2, s32[192]{0:T(256)S(1)} %reshape.7.near, s32[224]{0:T(256)S(1)} %reshape.8.slot, bf16[32,7,128,128]{3,2,1,0:T(8,128)(2,1)S(1)} %copy-done, ...), custom_call_target="tpu_custom_call" | custom-call | flops 234881024 | bytes 12582912 | tf_op jit(solution)/shard_map/pallas_call | solution.py:93
  180.2 9.5 %collective-permute-done.13 = bf16[4,7,128,128]{3,2,1,0:T(8,128)(2,1)S(1)} collective-permute-done((bf16[4,7,128,128]{3,2,1,0:T(8,128)(2,1)S(1)}, bf16[4,7,128,128]{3,2,1,0:T(8,128)(2,1)S(1)}, u32[]{:S(2)}, u32[]{:S(2)}) %collective-permute-start.13) | collective-permute-done | bytes 917536 | tf_op jit(solution)/shard_map/ppermute | solution.py:157
  189.7 3.9 %collective-permute-done.17 = bf16[4,7,128,128]{3,2,1,0:T(8,128)(2,1)S(1)} collective-permute-done((bf16[4,7,128,128]{3,2,1,0:T(8,128)(2,1)S(1)}, bf16[4,7,128,128]{3,2,1,0:T(8,128)(2,1)S(1)}, u32[]{:S(2)}, u32[]{:S(2)}) %collective-permute-start.17) | collective-permute-done | bytes 917536 | tf_op jit(solution)/shard_map/ppermute | solution.py:157
  194.0 17.7 %collective-permute-done.10 = bf16[4,7,128,128]{3,2,1,0:T(8,128)(2,1)S(1)} collective-permute-done((bf16[4,7,128,128]{3,2,1,0:T(8,128)(2,1)S(1)}, bf16[4,7,128,128]{3,2,1,0:T(8,128)(2,1)S(1)}, u32[]{:S(2)}, u32[]{:S(2)}) %collective-permute-start.10) | collective-permute-done | bytes 917536 | tf_op jit(solution)/shard_map/ppermute | solution.py:157
  212.3 1.4 pad_maximum_fusion
  (38 shorter events, 14.3 us)
Async XLA Ops:
  0.0 16.6 %collective-permute-start.3 = (bf16[32,128,128]{2,1,0:T(8,128)(2,1)}, bf16[32,128,128]{2,1,0:T(8,128)(2,1)S(1)}, u32[]{:S(2)}, u32[]{:S(2)}) collective-permute-start(bf16[32,128,128]{2,1,0:T(8,128)(2,1)} %own.15), channel_id=1, source_target_pairs={{8,0},{16,8},{24,16},{9,1},{17,9},{25,17},{10,2},{18,10},{26,18},{... | collective-permute-start | bytes 3145736 | tf_op jit(solution)/shard_map/ppermute | solution.py:126
  1.3 15.4 %collective-permute-start.2 = (bf16[32,128,128]{2,1,0:T(8,128)(2,1)}, bf16[32,128,128]{2,1,0:T(8,128)(2,1)S(1)}, u32[]{:S(2)}, u32[]{:S(2)}) collective-permute-start(bf16[32,128,128]{2,1,0:T(8,128)(2,1)} %own.15), channel_id=1, source_target_pairs={{0,8},{8,16},{16,24},{1,9},{9,17},{17,25},{2,10},{10,18},{18,26},{... | collective-permute-start | bytes 3145736 | tf_op jit(solution)/shard_map/ppermute | solution.py:126
  4.4 28.5 %collective-permute-start.1 = (bf16[32,128,128]{2,1,0:T(8,128)(2,1)}, bf16[32,128,128]{2,1,0:T(8,128)(2,1)S(1)}, u32[]{:S(2)}, u32[]{:S(2)}) collective-permute-start(bf16[32,128,128]{2,1,0:T(8,128)(2,1)} %own.15), channel_id=1, source_target_pairs={{1,0},{2,1},{3,2},{4,3},{5,4},{6,5},{7,6},{9,8},{10,9},{11,10},{12... | collective-permute-start | bytes 3145736 | tf_op jit(solution)/shard_map/ppermute | solution.py:126
  5.7 50.7 %collective-permute-start = (bf16[32,128,128]{2,1,0:T(8,128)(2,1)}, bf16[32,128,128]{2,1,0:T(8,128)(2,1)}, u32[]{:S(2)}, u32[]{:S(2)}) collective-permute-start(bf16[32,128,128]{2,1,0:T(8,128)(2,1)} %own.15), channel_id=1, source_target_pairs={{0,1},{1,2},{2,3},{3,4},{4,5},{5,6},{6,7},{8,9},{9,10},{10,11},{11... | collective-permute-start | bytes 3145736 | tf_op jit(solution)/shard_map/ppermute | solution.py:126
  56.4 3.1 %copy-start = (bf16[32,7,128,128]{3,2,1,0:T(8,128)(2,1)S(1)}, bf16[32,7,128,128]{3,2,1,0:T(8,128)(2,1)}, u32[]{:S(2)}) copy-start(bf16[32,7,128,128]{3,2,1,0:T(8,128)(2,1)} %a_ref.15) | copy-start | bytes 22020100
  59.5 1.2 copy-start.1
  60.7 0.7 copy-start.2
  66.2 25.0 %collective-permute-start.14 = (bf16[4,7,128,128]{3,2,1,0:T(8,128)(2,1)S(1)}, bf16[4,7,128,128]{3,2,1,0:T(8,128)(2,1)S(1)}, u32[]{:S(2)}, u32[]{:S(2)}) collective-permute-start(bf16[4,7,128,128]{3,2,1,0:T(8,128)(2,1)S(1)} %get-tuple-element.36), channel_id=1, source_target_pairs={{2,0},{4,2},{6,4},{7,6},{5,7},{3,5},{1,3},{0,1},{10,8},{12,10},{14... | collective-permute-start | bytes 2752520 | tf_op jit(solution)/shard_map/ppermute | solution.py:157
  68.0 24.9 %collective-permute-start.4 = (bf16[4,7,128,128]{3,2,1,0:T(8,128)(2,1)S(1)}, bf16[4,7,128,128]{3,2,1,0:T(8,128)(2,1)S(1)}, u32[]{:S(2)}, u32[]{:S(2)}) collective-permute-start(bf16[4,7,128,128]{3,2,1,0:T(8,128)(2,1)S(1)} %get-tuple-element.25), channel_id=1, source_target_pairs={{0,2},{2,4},{4,6},{6,7},{7,5},{5,3},{3,1},{1,0},{8,10},{10,12},{12... | collective-permute-start | bytes 2752520 | tf_op jit(solution)/shard_map/ppermute | solution.py:157
  74.0 37.0 %collective-permute-start.11 = (bf16[4,7,128,128]{3,2,1,0:T(8,128)(2,1)S(1)}, bf16[4,7,128,128]{3,2,1,0:T(8,128)(2,1)S(1)}, u32[]{:S(2)}, u32[]{:S(2)}) collective-permute-start(bf16[4,7,128,128]{3,2,1,0:T(8,128)(2,1)S(1)} %get-tuple-element.32), channel_id=1, source_target_pairs={{0,2},{2,4},{4,6},{6,7},{7,5},{5,3},{3,1},{1,0},{8,10},{10,12},{12... | collective-permute-start | bytes 2752520 | tf_op jit(solution)/shard_map/ppermute | solution.py:157
  91.6 23.3 %collective-permute-start.15 = (bf16[4,7,128,128]{3,2,1,0:T(8,128)(2,1)S(1)}, bf16[4,7,128,128]{3,2,1,0:T(8,128)(2,1)S(1)}, u32[]{:S(2)}, u32[]{:S(2)}) collective-permute-start(bf16[4,7,128,128]{3,2,1,0:T(8,128)(2,1)S(1)} %add_convert_fusion.3), channel_id=1, source_target_pairs={{2,0},{4,2},{6,4},{7,6},{5,7},{3,5},{1,3},{0,1},{10,8},{12,10},{14... | collective-permute-start | bytes 2752520 | tf_op jit(solution)/shard_map/ppermute | solution.py:157
  91.6 42.9 %collective-permute-start.8 = (bf16[4,7,128,128]{3,2,1,0:T(8,128)(2,1)S(1)}, bf16[4,7,128,128]{3,2,1,0:T(8,128)(2,1)S(1)}, u32[]{:S(2)}, u32[]{:S(2)}) collective-permute-start(bf16[4,7,128,128]{3,2,1,0:T(8,128)(2,1)S(1)} %get-tuple-element.28), channel_id=1, source_target_pairs={{2,0},{4,2},{6,4},{7,6},{5,7},{3,5},{1,3},{0,1},{10,8},{12,10},{14... | collective-permute-start | bytes 2752520 | tf_op jit(solution)/shard_map/ppermute | solution.py:157
  93.3 41.7 %collective-permute-start.5 = (bf16[4,7,128,128]{3,2,1,0:T(8,128)(2,1)S(1)}, bf16[4,7,128,128]{3,2,1,0:T(8,128)(2,1)S(1)}, u32[]{:S(2)}, u32[]{:S(2)}) collective-permute-start(bf16[4,7,128,128]{3,2,1,0:T(8,128)(2,1)S(1)} %add_convert_fusion.11), channel_id=1, source_target_pairs={{0,2},{2,4},{4,6},{6,7},{7,5},{5,3},{3,1},{1,0},{8,10},{10,12},{12... | collective-permute-start | bytes 2752520 | tf_op jit(solution)/shard_map/ppermute | solution.py:157
  111.4 38.9 %collective-permute-start.12 = (bf16[4,7,128,128]{3,2,1,0:T(8,128)(2,1)S(1)}, bf16[4,7,128,128]{3,2,1,0:T(8,128)(2,1)S(1)}, u32[]{:S(2)}, u32[]{:S(2)}) collective-permute-start(bf16[4,7,128,128]{3,2,1,0:T(8,128)(2,1)S(1)} %add_convert_fusion.5), channel_id=1, source_target_pairs={{0,2},{2,4},{4,6},{6,7},{7,5},{5,3},{3,1},{1,0},{8,10},{10,12},{12... | collective-permute-start | bytes 2752520 | tf_op jit(solution)/shard_map/ppermute | solution.py:157
  115.3 38.9 %collective-permute-start.16 = (bf16[4,7,128,128]{3,2,1,0:T(8,128)(2,1)S(1)}, bf16[4,7,128,128]{3,2,1,0:T(8,128)(2,1)S(1)}, u32[]{:S(2)}, u32[]{:S(2)}) collective-permute-start(bf16[4,7,128,128]{3,2,1,0:T(8,128)(2,1)S(1)} %add_convert_fusion.2), channel_id=1, source_target_pairs={{2,0},{4,2},{6,4},{7,6},{5,7},{3,5},{1,3},{0,1},{10,8},{12,10},{14... | collective-permute-start | bytes 2752520 | tf_op jit(solution)/shard_map/ppermute | solution.py:157
  134.9 38.9 %collective-permute-start.9 = (bf16[4,7,128,128]{3,2,1,0:T(8,128)(2,1)S(1)}, bf16[4,7,128,128]{3,2,1,0:T(8,128)(2,1)S(1)}, u32[]{:S(2)}, u32[]{:S(2)}) collective-permute-start(bf16[4,7,128,128]{3,2,1,0:T(8,128)(2,1)S(1)} %add_convert_fusion.8), channel_id=1, source_target_pairs={{2,0},{4,2},{6,4},{7,6},{5,7},{3,5},{1,3},{0,1},{10,8},{12,10},{14... | collective-permute-start | bytes 2752520 | tf_op jit(solution)/shard_map/ppermute | solution.py:157
  135.4 38.9 %collective-permute-start.6 = (bf16[4,7,128,128]{3,2,1,0:T(8,128)(2,1)S(1)}, bf16[4,7,128,128]{3,2,1,0:T(8,128)(2,1)S(1)}, u32[]{:S(2)}, u32[]{:S(2)}) collective-permute-start(bf16[4,7,128,128]{3,2,1,0:T(8,128)(2,1)S(1)} %add_convert_fusion.10), channel_id=1, source_target_pairs={{0,2},{2,4},{4,6},{6,7},{7,5},{5,3},{3,1},{1,0},{8,10},{10,12},{12... | collective-permute-start | bytes 2752520 | tf_op jit(solution)/shard_map/ppermute | solution.py:157
  150.7 38.9 %collective-permute-start.13 = (bf16[4,7,128,128]{3,2,1,0:T(8,128)(2,1)S(1)}, bf16[4,7,128,128]{3,2,1,0:T(8,128)(2,1)S(1)}, u32[]{:S(2)}, u32[]{:S(2)}) collective-permute-start(bf16[4,7,128,128]{3,2,1,0:T(8,128)(2,1)S(1)} %add_convert_fusion.4), channel_id=1, source_target_pairs={{0,2},{2,4},{4,6},{6,7},{7,5},{5,3},{3,1},{1,0},{8,10},{10,12},{12... | collective-permute-start | bytes 2752520 | tf_op jit(solution)/shard_map/ppermute | solution.py:157
  154.6 38.9 %collective-permute-start.17 = (bf16[4,7,128,128]{3,2,1,0:T(8,128)(2,1)S(1)}, bf16[4,7,128,128]{3,2,1,0:T(8,128)(2,1)S(1)}, u32[]{:S(2)}, u32[]{:S(2)}) collective-permute-start(bf16[4,7,128,128]{3,2,1,0:T(8,128)(2,1)S(1)} %add_convert_fusion.1), channel_id=1, source_target_pairs={{2,0},{4,2},{6,4},{7,6},{5,7},{3,5},{1,3},{0,1},{10,8},{12,10},{14... | collective-permute-start | bytes 2752520 | tf_op jit(solution)/shard_map/ppermute | solution.py:157
  174.3 37.5 %collective-permute-start.10 = (bf16[4,7,128,128]{3,2,1,0:T(8,128)(2,1)S(1)}, bf16[4,7,128,128]{3,2,1,0:T(8,128)(2,1)S(1)}, u32[]{:S(2)}, u32[]{:S(2)}) collective-permute-start(bf16[4,7,128,128]{3,2,1,0:T(8,128)(2,1)S(1)} %add_convert_fusion.7), channel_id=1, source_target_pairs={{2,0},{4,2},{6,4},{7,6},{5,7},{3,5},{1,3},{0,1},{10,8},{12,10},{14... | collective-permute-start | bytes 2752520 | tf_op jit(solution)/shard_map/ppermute | solution.py:157
  174.7 37.0 %collective-permute-start.7 = (bf16[4,7,128,128]{3,2,1,0:T(8,128)(2,1)S(1)}, bf16[4,7,128,128]{3,2,1,0:T(8,128)(2,1)S(1)}, u32[]{:S(2)}, u32[]{:S(2)}) collective-permute-start(bf16[4,7,128,128]{3,2,1,0:T(8,128)(2,1)S(1)} %add_convert_fusion.9), channel_id=1, source_target_pairs={{0,2},{2,4},{4,6},{6,7},{7,5},{5,3},{3,1},{1,0},{8,10},{10,12},{12... | collective-permute-start | bytes 2752520 | tf_op jit(solution)/shard_map/ppermute | solution.py:157

commit v2 on v1

--- a/solution.py
+++ b/solution.py
@@ -9,7 +9,7 @@
 
 KC = 7
 FACES = 6
-VMEM_BYTES = 40 * 1024 * 1024
+VMEM_BYTES = 56 * 1024 * 1024
 
 
 def ring_order(count):
@@ -25,15 +25,18 @@
 
 
 def chunk_kernel(
-    distance, rel, agg, near, slot, a_ref, own, below, above, left, right,
-    low, high, acc, a_buf, t_buf, picked, sems,
+    distance, places, owner, agg, near, slot, a_ref, own, below, above, left, right,
+    low, high, acc, a_buf, p_buf, t_buf, picked, sems,
 ):
-    elems = rel.shape[0]
-    half = low.shape[0]
-    width = own.shape[1]
+    elems, count_dev = owner.shape[0], places.shape[0]
+    aggs, _, half, width = low.shape
+    depth = a_buf.shape[0]
+    sources = (own, own, below, above, left, right)
+
+    target = lax.rem(places[lax.axis_index("dev")] + distance, count_dev)
 
     def pick(e, count):
-        hit = rel[e] == distance
+        hit = places[owner[e, 0]] == target
 
         @pl.when(hit)
         def _():
@@ -43,64 +46,73 @@
 
     count = lax.fori_loop(0, elems, pick, jnp.int32(0))
 
-    def fetch(i, buf):
-        return pltpu.make_async_copy(a_ref.at[picked[i]], a_buf.at[buf], sems.at[buf])
+    def fetches(i):
+        e, buf = picked[i], lax.rem(i, depth)
+        copies = [pltpu.make_async_copy(a_ref.at[e], a_buf.at[buf], sems.at[buf, 0])]
+        for f in range(KC):
+            source = own.at[e] if f == 0 else sources[f - 1].at[near[e, f - 1]]
+            copies.append(pltpu.make_async_copy(source, p_buf.at[buf, f], sems.at[buf, f + 1]))
+        return copies
 
-    @pl.when(count > 0)
-    def _():
-        fetch(0, 0).start()
+    def start(i):
+        @pl.when(i < count)
+        def _():
+            for copy in fetches(i):
+                copy.start()
 
+    for i in range(depth - 1):
+        start(i)
     acc[...] = jnp.zeros_like(acc)
-    sources = (own, own, below, above, left, right)
 
     def element(i, carry):
-        buf = lax.rem(i, 2)
-
-        @pl.when(i + 1 < count)
-        def _():
-            fetch(i + 1, 1 - buf).start()
-
-        e = picked[i]
-        fetch(i, buf).wait()
-        p_e = own[e]
+        start(i + depth - 1)
+        e, buf = picked[i], lax.rem(i, depth)
+        for copy in fetches(i):
+            copy.wait()
         for f in range(KC):
-            facing = p_e if f == 0 else sources[f - 1][near[e * FACES + f - 1]]
             t_buf[:, f * width : (f + 1) * width] = jnp.dot(
-                a_buf[buf, f], facing, preferred_element_type=jnp.float32
+                a_buf[buf, f], p_buf[buf, f], preferred_element_type=jnp.float32
             ).astype(jnp.bfloat16)
         weighted = lax.dot_general(
-            p_e, t_buf[...], (((0,), (0,)), ((), ())), preferred_element_type=jnp.float32
+            p_buf[buf, 0], t_buf[...], (((0,), (0,)), ((), ())), preferred_element_type=jnp.float32
         )
         a = agg[e]
         for f in range(KC):
-            row = a * KC + slot[e * KC + f]
+            row = a * KC + slot[e, f]
             acc[row] = acc[row] + weighted[:, f * width : (f + 1) * width]
         return carry
 
     lax.fori_loop(0, count, element, 0)
-    for r in range(2 * half):
-        out = low if r < half else high
+
+    def store(r, carry):
         for s in range(KC):
-            out[r % half, s] = acc[r * KC + s].astype(jnp.bfloat16)
+            block = acc[r * KC + s].astype(jnp.bfloat16)
+            low[r, s] = block[:half]
+            high[r, s] = block[half:]
+        return carry
+
+    lax.fori_loop(0, aggs, store, 0)
 
 
 def chunk(distance, aggs, tables, a_blocks, blocks):
     elems, _, width, _ = a_blocks.shape
-    half = aggs // 2
-    out = jax.ShapeDtypeStruct((half, KC, width, width), jnp.bfloat16)
+    out = jax.ShapeDtypeStruct((aggs, KC, width // 2, width), jnp.bfloat16)
     smem = pl.BlockSpec(memory_space=pltpu.SMEM)
     vmem = pl.BlockSpec(memory_space=pltpu.VMEM)
+    hbm = pl.BlockSpec(memory_space=pl.ANY)
+    depth = 4
     return pl.pallas_call(
         functools.partial(chunk_kernel, distance),
         out_shape=(out, out),
-        in_specs=[smem] * 4 + [pl.BlockSpec(memory_space=pl.ANY)] + [vmem] * 5,
+        in_specs=[smem] * 5 + [hbm] * 6,
         out_specs=(vmem, vmem),
         scratch_shapes=[
             pltpu.VMEM((aggs * KC, width, width), jnp.float32),
-            pltpu.VMEM((2, KC, width, width), jnp.bfloat16),
+            pltpu.VMEM((depth, KC, width, width), jnp.bfloat16),
+            pltpu.VMEM((depth, KC, width, width), jnp.bfloat16),
             pltpu.VMEM((width, KC * width), jnp.bfloat16),
             pltpu.SMEM((elems,), jnp.int32),
-            pltpu.SemaphoreType.DMA((2,)),
+            pltpu.SemaphoreType.DMA((depth, KC + 1)),
         ],
         compiler_params=pltpu.CompilerParams(vmem_limit_bytes=VMEM_BYTES),
         cost_estimate=pl.CostEstimate(
@@ -118,6 +130,10 @@
     aggs = elems // 4
     count = lax.axis_size("dev")
 
+    order = ring_order(count)
+    places = jnp.array([order.index(d) for d in range(count)], jnp.int32)
+    tables = (places, owner, agg_local, neighbours, coarse_slot)
+
     halo = []
     for axis in ("dev", "grp"):
         size = lax.axis_size(axis)
@@ -125,15 +141,7 @@
         backward = [(b, a) for a, b in forward]
         halo += [lax.ppermute(p_blocks, axis, forward), lax.ppermute(p_blocks, axis, backward)]
     blocks = (p_blocks, *halo)
-
-    order = ring_order(count)
-    place = [order.index(d) for d in range(count)]
-    index = jnp.arange(count, dtype=jnp.int32)
-    places = jnp.array(place, jnp.int32)
-    mine = jnp.sum(jnp.where(index == lax.axis_index("dev"), places, 0))
-    theirs = jnp.sum(jnp.where(owner == index[None, :], places[None, :], 0), 1)
-    rel = lax.rem(theirs - mine + count, count)
-    tables = (rel, agg_local, neighbours.reshape(-1), coarse_slot.reshape(-1))
+    blocks = lax.optimization_barrier(blocks)
 
     chunks = {}
 
@@ -158,7 +166,7 @@
     last = 2 * far - 2
     low = add(part(0, 0), got[1, last], got[-1, last - 1])
     high = add(part(0, 1), got[1, last - 1], got[-1, last])
-    return jnp.concatenate([low, high], 0)
+    return jnp.concatenate([low, high], 2)
 
 
 def solution(mesh):

time: 214 us -> 208 us (0.972)
  waiting for transfers between devices: 128 us -> 111 us
  Pallas kernels: 38 us -> 50.7 us
  starting transfers between devices: 31.7 us -> 29.4 us
    ppermute x14, waiting for transfers between devices: 88.3 us -> 71.7 us  [on_device(): got[sign, n] = lax.ppermute(terms[0] if n < 2 else add(*terms), 'dev', perm)]
    pallas_call x8, Pallas kernels: 38 us -> 50.7 us  [chunk(): pl.pallas_call(functools.partial(chunk_kernel, distance), out_shape=(out,...]
    convert_element_type x12, other arithmetic: 4.82 us -> 8.93 us  [add(): return sum((t.astype(jnp.float32) for t in terms)).astype(jnp.bfloat16)]
    ppermute x2, starting transfers between devices: 9.58 us -> 7.34 us  [on_device(): lax.ppermute(p_blocks, axis, forward)]
    unnamed x8 -> x29, local copies, waits for them, and re-layouts: 6.5 us -> 5.07 us
  transfers between devices with their start and end apart: 18 -> 18, of which waited for: 12 -> 11; matrix products, arithmetic and copies ran while one was open for 4% -> 6% of each run, Pallas kernels for 16% -> 22%
where the time goes in v2:
time: 208 us; the launch traced here: 207 us
  waiting for transfers between devices  111 us (53%)
  Pallas kernels  50.7 us (24%)
  starting transfers between devices  29.4 us (14%)
  other arithmetic  10.3 us (5%)
  local copies, waits for them, and re-layouts  5.07 us (2%)
    ppermute x14, waiting for transfers between devices, on_device(): got[sign, n] = lax.ppermute(terms[0] if n < 2 else add(*terms), 'dev', perm)  71.7 us
    pallas_call x8, Pallas kernels, chunk(): pl.pallas_call(functools.partial(chunk_kernel, distance), out_shape=(out,...  50.7 us
    ppermute x2, waiting for transfers between devices, on_device(): lax.ppermute(p_blocks, axis, forward)  24.2 us
    ppermute x14, starting transfers between devices, on_device(): got[sign, n] = lax.ppermute(terms[0] if n < 2 else add(*terms), 'dev', perm)  19.5 us
    ppermute x2, waiting for transfers between devices, on_device(): lax.ppermute(p_blocks, axis, backward)  15.5 us
    convert_element_type x12, other arithmetic, add(): return sum((t.astype(jnp.float32) for t in terms)).astype(jnp.bfloat16)  8.93 us
    ppermute x2, starting transfers between devices, on_device(): lax.ppermute(p_blocks, axis, forward)  7.34 us
    unnamed x29, local copies, waits for them, and re-layouts  5.07 us
  transfers between devices with their start and end apart: 18, of which 11 were waited for; matrix products, arithmetic and copies ran while one was open for 6% of the time, Pallas kernels for 22%

profile of v2, /device:TPU:0, one launch (start us, length us, event | category | flops | bytes accessed | tf_op | source)
XLA Modules:
  0.0 207.2 jit_solution(6299947754880674172)
XLA Ops:
  0.0 2.4 %collective-permute-start.2 = (bf16[32,128,128]{2,1,0:T(8,128)(2,1)}, bf16[32,128,128]{2,1,0:T(8,128)(2,1)S(1)}, u32[]{:S(2)}, u32[]{:S(2)}) collective-permute-start(bf16[32,128,128]{2,1,0:T(8,128)(2,1)} %own.7), channel_id=1, source_target_pairs={{0,8},{8,16},{16,24},{1,9},{9,17},{17,25},{2,10},{10,18},{18,26},{... | collective-permute-start | bytes 3145736 | tf_op jit(solution)/shard_map/ppermute | solution.py:142
  3.7 4.9 %collective-permute-start = (bf16[32,128,128]{2,1,0:T(8,128)(2,1)}, bf16[32,128,128]{2,1,0:T(8,128)(2,1)S(1)}, u32[]{:S(2)}, u32[]{:S(2)}) collective-permute-start(bf16[32,128,128]{2,1,0:T(8,128)(2,1)} %own.7), channel_id=1, source_target_pairs={{0,1},{1,2},{2,3},{3,4},{4,5},{5,6},{6,7},{8,9},{9,10},{10,11},{11... | collective-permute-start | bytes 3145736 | tf_op jit(solution)/shard_map/ppermute | solution.py:142
  10.0 1.4 copy.9.near
  11.3 1.4 copy.10.slot
  14.0 15.5 %collective-permute-done.1.above = bf16[32,128,128]{2,1,0:T(8,128)(2,1)S(1)} collective-permute-done((bf16[32,128,128]{2,1,0:T(8,128)(2,1)}, bf16[32,128,128]{2,1,0:T(8,128)(2,1)S(1)}, u32[]{:S(2)}, u32[]{:S(2)}) %collective-permute-start.1) | collective-permute-done | bytes 1048608 | tf_op jit(solution)/shard_map/ppermute | solution.py:142
  29.5 24.2 %collective-permute-done.below = bf16[32,128,128]{2,1,0:T(8,128)(2,1)S(1)} collective-permute-done((bf16[32,128,128]{2,1,0:T(8,128)(2,1)}, bf16[32,128,128]{2,1,0:T(8,128)(2,1)S(1)}, u32[]{:S(2)}, u32[]{:S(2)}) %collective-permute-start) | collective-permute-done | bytes 1048608 | tf_op jit(solution)/shard_map/ppermute | solution.py:142
  54.7 5.5 %shard_map.77 = (bf16[8,7,64,128]{3,2,1,0:T(8,128)(2,1)}, bf16[8,7,64,128]{3,2,1,0:T(8,128)(2,1)}) custom-call(s32[8]{0:T(128)} %constant.2.clone.places, s32[32,1]{1,0:T(8,128)} %copy.8.owner, s32[32]{0:T(128)} %agg.15, s32[32,6]{1,0:T(8,128)} %copy.9.near, s32[32,7]{1,0:T(8,128)} %copy.10.slot, bf16[32,7,128,128]{3,2,1,0:T(8,128)(2,1)} %a_ref.15, ...), custom_call_target="tpu_custom_call" | custom-call | flops 234881024 | bytes 12582912 | tf_op jit(solution)/shard_map/pallas_call | solution.py:104
  60.2 4.5 %collective-permute-start.14 = (bf16[8,7,64,128]{3,2,1,0:T(8,128)(2,1)}, bf16[8,7,64,128]{3,2,1,0:T(8,128)(2,1)S(1)}, u32[]{:S(2)}, u32[]{:S(2)}) collective-permute-start(bf16[8,7,64,128]{3,2,1,0:T(8,128)(2,1)} %get-tuple-element.46), channel_id=1, source_target_pairs={{2,0},{4,2},{6,4},{7,6},{5,7},{3,5},{1,3},{0,1},{10,8},{12,10},{14... | collective-permute-start | bytes 2752520 | tf_op jit(solution)/shard_map/ppermute | solution.py:165
  64.8 5.5 %shard_map.80 = (bf16[8,7,64,128]{3,2,1,0:T(8,128)(2,1)}, bf16[8,7,64,128]{3,2,1,0:T(8,128)(2,1)}) custom-call(s32[8]{0:T(128)} %constant.2.clone.places, s32[32,1]{1,0:T(8,128)} %copy.8.owner, s32[32]{0:T(128)} %agg.15, s32[32,6]{1,0:T(8,128)} %copy.9.near, s32[32,7]{1,0:T(8,128)} %copy.10.slot, bf16[32,7,128,128]{3,2,1,0:T(8,128)(2,1)} %a_ref.15, ...), custom_call_target="tpu_custom_call" | custom-call | flops 234881024 | bytes 12582912 | tf_op jit(solution)/shard_map/pallas_call | solution.py:104
  70.3 7.7 %shard_map.76 = (bf16[8,7,64,128]{3,2,1,0:T(8,128)(2,1)}, bf16[8,7,64,128]{3,2,1,0:T(8,128)(2,1)}) custom-call(s32[8]{0:T(128)} %constant.2.clone.places, s32[32,1]{1,0:T(8,128)} %copy.8.owner, s32[32]{0:T(128)} %agg.15, s32[32,6]{1,0:T(8,128)} %copy.9.near, s32[32,7]{1,0:T(8,128)} %copy.10.slot, bf16[32,7,128,128]{3,2,1,0:T(8,128)(2,1)} %a_ref.15, ...), custom_call_target="tpu_custom_call" | custom-call | flops 234881024 | bytes 12582912 | tf_op jit(solution)/shard_map/pallas_call | solution.py:104
  78.1 6.0 %collective-permute-done.14 = bf16[8,7,64,128]{3,2,1,0:T(8,128)(2,1)S(1)} collective-permute-done((bf16[8,7,64,128]{3,2,1,0:T(8,128)(2,1)}, bf16[8,7,64,128]{3,2,1,0:T(8,128)(2,1)S(1)}, u32[]{:S(2)}, u32[]{:S(2)}) %collective-permute-start.14) | collective-permute-done | bytes 917536 | tf_op jit(solution)/shard_map/ppermute | solution.py:165
  84.5 3.0 %collective-permute-start.15 = (bf16[8,7,64,128]{3,2,1,0:T(8,128)(2,1)S(1)}, bf16[8,7,64,128]{3,2,1,0:T(8,128)(2,1)S(1)}, u32[]{:S(2)}, u32[]{:S(2)}) collective-permute-start(bf16[8,7,64,128]{3,2,1,0:T(8,128)(2,1)S(1)} %add_convert_fusion.3), channel_id=1, source_target_pairs={{2,0},{4,2},{6,4},{7,6},{5,7},{3,5},{1,3},{0,1},{10,8},{12,10},{14... | collective-permute-start | bytes 2752520 | tf_op jit(solution)/shard_map/ppermute | solution.py:165
  87.4 2.4 %collective-permute-start.8 = (bf16[8,7,64,128]{3,2,1,0:T(8,128)(2,1)S(1)}, bf16[8,7,64,128]{3,2,1,0:T(8,128)(2,1)S(1)}, u32[]{:S(2)}, u32[]{:S(2)}) collective-permute-start(bf16[8,7,64,128]{3,2,1,0:T(8,128)(2,1)S(1)} %copy-done.12), channel_id=1, source_target_pairs={{2,0},{4,2},{6,4},{7,6},{5,7},{3,5},{1,3},{0,1},{10,8},{12,10},{14... | collective-permute-start | bytes 2752520 | tf_op jit(solution)/shard_map/ppermute | solution.py:165
  90.2 5.5 %shard_map.79 = (bf16[8,7,64,128]{3,2,1,0:T(8,128)(2,1)}, bf16[8,7,64,128]{3,2,1,0:T(8,128)(2,1)}) custom-call(s32[8]{0:T(128)} %constant.2.clone.places, s32[32,1]{1,0:T(8,128)} %copy.8.owner, s32[32]{0:T(128)} %agg.15, s32[32,6]{1,0:T(8,128)} %copy.9.near, s32[32,7]{1,0:T(8,128)} %copy.10.slot, bf16[32,7,128,128]{3,2,1,0:T(8,128)(2,1)} %a_ref.15, ...), custom_call_target="tpu_custom_call" | custom-call | flops 234881024 | bytes 12582912 | tf_op jit(solution)/shard_map/pallas_call | solution.py:104
  95.7 8.0 %shard_map.75 = (bf16[8,7,64,128]{3,2,1,0:T(8,128)(2,1)}, bf16[8,7,64,128]{3,2,1,0:T(8,128)(2,1)}) custom-call(s32[8]{0:T(128)} %constant.2.clone.places, s32[32,1]{1,0:T(8,128)} %copy.8.owner, s32[32]{0:T(128)} %agg.15, s32[32,6]{1,0:T(8,128)} %copy.9.near, s32[32,7]{1,0:T(8,128)} %copy.10.slot, bf16[32,7,128,128]{3,2,1,0:T(8,128)(2,1)} %a_ref.15, ...), custom_call_target="tpu_custom_call" | custom-call | flops 234881024 | bytes 12582912 | tf_op jit(solution)/shard_map/pallas_call | solution.py:104
  103.8 4.1 %collective-permute-done.11 = bf16[8,7,64,128]{3,2,1,0:T(8,128)(2,1)S(1)} collective-permute-done((bf16[8,7,64,128]{3,2,1,0:T(8,128)(2,1)}, bf16[8,7,64,128]{3,2,1,0:T(8,128)(2,1)S(1)}, u32[]{:S(2)}, u32[]{:S(2)}) %collective-permute-start.11) | collective-permute-done | bytes 917536 | tf_op jit(solution)/shard_map/ppermute | solution.py:165
  107.9 1.5 add_convert_fusion.5
  109.9 2.1 %collective-permute-start.16 = (bf16[8,7,64,128]{3,2,1,0:T(8,128)(2,1)S(1)}, bf16[8,7,64,128]{3,2,1,0:T(8,128)(2,1)S(1)}, u32[]{:S(2)}, u32[]{:S(2)}) collective-permute-start(bf16[8,7,64,128]{3,2,1,0:T(8,128)(2,1)S(1)} %add_convert_fusion.2), channel_id=1, source_target_pairs={{2,0},{4,2},{6,4},{7,6},{5,7},{3,5},{1,3},{0,1},{10,8},{12,10},{14... | collective-permute-start | bytes 2752520 | tf_op jit(solution)/shard_map/ppermute | solution.py:165
  112.0 15.9 %collective-permute-done.8 = bf16[8,7,64,128]{3,2,1,0:T(8,128)(2,1)S(1)} collective-permute-done((bf16[8,7,64,128]{3,2,1,0:T(8,128)(2,1)S(1)}, bf16[8,7,64,128]{3,2,1,0:T(8,128)(2,1)S(1)}, u32[]{:S(2)}, u32[]{:S(2)}) %collective-permute-start.8) | collective-permute-done | bytes 917536 | tf_op jit(solution)/shard_map/ppermute | solution.py:165
  128.2 2.5 %collective-permute-start.9 = (bf16[8,7,64,128]{3,2,1,0:T(8,128)(2,1)S(1)}, bf16[8,7,64,128]{3,2,1,0:T(8,128)(2,1)S(1)}, u32[]{:S(2)}, u32[]{:S(2)}) collective-permute-start(bf16[8,7,64,128]{3,2,1,0:T(8,128)(2,1)S(1)} %add_convert_fusion.8), channel_id=1, source_target_pairs={{2,0},{4,2},{6,4},{7,6},{5,7},{3,5},{1,3},{0,1},{10,8},{12,10},{14... | collective-permute-start | bytes 2752520 | tf_op jit(solution)/shard_map/ppermute | solution.py:165
  131.2 6.7 %shard_map.78 = (bf16[8,7,64,128]{3,2,1,0:T(8,128)(2,1)}, bf16[8,7,64,128]{3,2,1,0:T(8,128)(2,1)}) custom-call(s32[8]{0:T(128)} %constant.2.clone.places, s32[32,1]{1,0:T(8,128)} %copy.8.owner, s32[32]{0:T(128)} %agg.15, s32[32,6]{1,0:T(8,128)} %copy.9.near, s32[32,7]{1,0:T(8,128)} %copy.10.slot, bf16[32,7,128,128]{3,2,1,0:T(8,128)(2,1)} %a_ref.15, ...), custom_call_target="tpu_custom_call" | custom-call | flops 234881024 | bytes 12582912 | tf_op jit(solution)/shard_map/pallas_call | solution.py:104
  137.9 6.3 %shard_map.74 = (bf16[8,7,64,128]{3,2,1,0:T(8,128)(2,1)}, bf16[8,7,64,128]{3,2,1,0:T(8,128)(2,1)}) custom-call(s32[8]{0:T(128)} %constant.2.clone.places, s32[32,1]{1,0:T(8,128)} %copy.8.owner, s32[32]{0:T(128)} %agg.15, s32[32,6]{1,0:T(8,128)} %copy.9.near, s32[32,7]{1,0:T(8,128)} %copy.10.slot, bf16[32,7,128,128]{3,2,1,0:T(8,128)(2,1)} %a_ref.15, ...), custom_call_target="tpu_custom_call" | custom-call | flops 234881024 | bytes 12582912 | tf_op jit(solution)/shard_map/pallas_call | solution.py:104
  144.3 2.9 %collective-permute-done.12 = bf16[8,7,64,128]{3,2,1,0:T(8,128)(2,1)S(1)} collective-permute-done((bf16[8,7,64,128]{3,2,1,0:T(8,128)(2,1)S(1)}, bf16[8,7,64,128]{3,2,1,0:T(8,128)(2,1)S(1)}, u32[]{:S(2)}, u32[]{:S(2)}) %collective-permute-start.12) | collective-permute-done | bytes 917536 | tf_op jit(solution)/shard_map/ppermute | solution.py:165
  147.2 1.5 add_convert_fusion.4
  149.2 2.1 %collective-permute-start.17 = (bf16[8,7,64,128]{3,2,1,0:T(8,128)(2,1)S(1)}, bf16[8,7,64,128]{3,2,1,0:T(8,128)(2,1)S(1)}, u32[]{:S(2)}, u32[]{:S(2)}) collective-permute-start(bf16[8,7,64,128]{3,2,1,0:T(8,128)(2,1)S(1)} %add_convert_fusion.1), channel_id=1, source_target_pairs={{2,0},{4,2},{6,4},{7,6},{5,7},{3,5},{1,3},{0,1},{10,8},{12,10},{14... | collective-permute-start | bytes 2752520 | tf_op jit(solution)/shard_map/ppermute | solution.py:165
  151.3 15.9 %collective-permute-done.9 = bf16[8,7,64,128]{3,2,1,0:T(8,128)(2,1)S(1)} collective-permute-done((bf16[8,7,64,128]{3,2,1,0:T(8,128)(2,1)S(1)}, bf16[8,7,64,128]{3,2,1,0:T(8,128)(2,1)S(1)}, u32[]{:S(2)}, u32[]{:S(2)}) %collective-permute-start.9) | collective-permute-done | bytes 917536 | tf_op jit(solution)/shard_map/ppermute | solution.py:165
  167.6 2.5 %collective-permute-start.10 = (bf16[8,7,64,128]{3,2,1,0:T(8,128)(2,1)S(1)}, bf16[8,7,64,128]{3,2,1,0:T(8,128)(2,1)S(1)}, u32[]{:S(2)}, u32[]{:S(2)}) collective-permute-start(bf16[8,7,64,128]{3,2,1,0:T(8,128)(2,1)S(1)} %add_convert_fusion.7), channel_id=1, source_target_pairs={{2,0},{4,2},{6,4},{7,6},{5,7},{3,5},{1,3},{0,1},{10,8},{12,10},{14... | collective-permute-start | bytes 2752520 | tf_op jit(solution)/shard_map/ppermute | solution.py:165
  171.4 5.5 %shard_map.73 = (bf16[8,7,64,128]{3,2,1,0:T(8,128)(2,1)}, bf16[8,7,64,128]{3,2,1,0:T(8,128)(2,1)}) custom-call(s32[8]{0:T(128)} %constant.2.clone.places, s32[32,1]{1,0:T(8,128)} %copy.8.owner, s32[32]{0:T(128)} %agg.15, s32[32,6]{1,0:T(8,128)} %copy.9.near, s32[32,7]{1,0:T(8,128)} %copy.10.slot, bf16[32,7,128,128]{3,2,1,0:T(8,128)(2,1)} %a_ref.15, ...), custom_call_target="tpu_custom_call" | custom-call | flops 234881024 | bytes 12582912 | tf_op jit(solution)/shard_map/pallas_call | solution.py:104
  176.9 9.6 %collective-permute-done.13 = bf16[8,7,64,128]{3,2,1,0:T(8,128)(2,1)S(1)} collective-permute-done((bf16[8,7,64,128]{3,2,1,0:T(8,128)(2,1)S(1)}, bf16[8,7,64,128]{3,2,1,0:T(8,128)(2,1)S(1)}, u32[]{:S(2)}, u32[]{:S(2)}) %collective-permute-start.13) | collective-permute-done | bytes 917536 | tf_op jit(solution)/shard_map/ppermute | solution.py:165
  186.9 1.7 add_convert_fusion
  188.6 16.2 %collective-permute-done.10 = bf16[8,7,64,128]{3,2,1,0:T(8,128)(2,1)S(1)} collective-permute-done((bf16[8,7,64,128]{3,2,1,0:T(8,128)(2,1)S(1)}, bf16[8,7,64,128]{3,2,1,0:T(8,128)(2,1)S(1)}, u32[]{:S(2)}, u32[]{:S(2)}) %collective-permute-start.10) | collective-permute-done | bytes 917536 | tf_op jit(solution)/shard_map/ppermute | solution.py:165
  205.9 1.4 pad_maximum_fusion
  (54 shorter events, 10.4 us)
Async XLA Ops:
  0.0 14.0 %collective-permute-start.2 = (bf16[32,128,128]{2,1,0:T(8,128)(2,1)}, bf16[32,128,128]{2,1,0:T(8,128)(2,1)S(1)}, u32[]{:S(2)}, u32[]{:S(2)}) collective-permute-start(bf16[32,128,128]{2,1,0:T(8,128)(2,1)} %own.7), channel_id=1, source_target_pairs={{0,8},{8,16},{16,24},{1,9},{9,17},{17,25},{2,10},{10,18},{18,26},{... | collective-permute-start | bytes 3145736 | tf_op jit(solution)/shard_map/ppermute | solution.py:142
  2.4 27.1 %collective-permute-start.1 = (bf16[32,128,128]{2,1,0:T(8,128)(2,1)}, bf16[32,128,128]{2,1,0:T(8,128)(2,1)S(1)}, u32[]{:S(2)}, u32[]{:S(2)}) collective-permute-start(bf16[32,128,128]{2,1,0:T(8,128)(2,1)} %own.7), channel_id=1, source_target_pairs={{1,0},{2,1},{3,2},{4,3},{5,4},{6,5},{7,6},{9,8},{10,9},{11,10},{12... | collective-permute-start | bytes 3145736 | tf_op jit(solution)/shard_map/ppermute | solution.py:142
  3.7 50.1 %collective-permute-start = (bf16[32,128,128]{2,1,0:T(8,128)(2,1)}, bf16[32,128,128]{2,1,0:T(8,128)(2,1)S(1)}, u32[]{:S(2)}, u32[]{:S(2)}) collective-permute-start(bf16[32,128,128]{2,1,0:T(8,128)(2,1)} %own.7), channel_id=1, source_target_pairs={{0,1},{1,2},{2,3},{3,4},{4,5},{5,6},{6,7},{8,9},{9,10},{10,11},{11... | collective-permute-start | bytes 3145736 | tf_op jit(solution)/shard_map/ppermute | solution.py:142
  8.7 45.1 %collective-permute-start.3 = (bf16[32,128,128]{2,1,0:T(8,128)(2,1)}, bf16[32,128,128]{2,1,0:T(8,128)(2,1)}, u32[]{:S(2)}, u32[]{:S(2)}) collective-permute-start(bf16[32,128,128]{2,1,0:T(8,128)(2,1)} %own.7), channel_id=1, source_target_pairs={{8,0},{16,8},{24,16},{9,1},{17,9},{25,17},{10,2},{18,10},{26,18},{... | collective-permute-start | bytes 3145736 | tf_op jit(solution)/shard_map/ppermute | solution.py:142
  14.0 39.8 %copy-start = (bf16[32,128,128]{2,1,0:T(8,128)(2,1)}, bf16[32,128,128]{2,1,0:T(8,128)(2,1)S(1)}, u32[]{:S(2)}) copy-start(bf16[32,128,128]{2,1,0:T(8,128)(2,1)S(1)} %collective-permute-done.2.left) | copy-start | bytes 3145732
  29.5 24.3 %copy-start.1 = (bf16[32,128,128]{2,1,0:T(8,128)(2,1)}, bf16[32,128,128]{2,1,0:T(8,128)(2,1)S(1)}, u32[]{:S(2)}) copy-start(bf16[32,128,128]{2,1,0:T(8,128)(2,1)S(1)} %collective-permute-done.1.above) | copy-start | bytes 3145732
  53.8 1.0 copy-start.2
  60.2 23.9 %collective-permute-start.14 = (bf16[8,7,64,128]{3,2,1,0:T(8,128)(2,1)}, bf16[8,7,64,128]{3,2,1,0:T(8,128)(2,1)S(1)}, u32[]{:S(2)}, u32[]{:S(2)}) collective-permute-start(bf16[8,7,64,128]{3,2,1,0:T(8,128)(2,1)} %get-tuple-element.46), channel_id=1, source_target_pairs={{2,0},{4,2},{6,4},{7,6},{5,7},{3,5},{1,3},{0,1},{10,8},{12,10},{14... | collective-permute-start | bytes 2752520 | tf_op jit(solution)/shard_map/ppermute | solution.py:165
  64.8 25.1 %collective-permute-start.4 = (bf16[8,7,64,128]{3,2,1,0:T(8,128)(2,1)}, bf16[8,7,64,128]{3,2,1,0:T(8,128)(2,1)S(1)}, u32[]{:S(2)}, u32[]{:S(2)}) collective-permute-start(bf16[8,7,64,128]{3,2,1,0:T(8,128)(2,1)} %get-tuple-element.35), channel_id=1, source_target_pairs={{0,2},{2,4},{4,6},{6,7},{7,5},{5,3},{3,1},{1,0},{8,10},{10,12},{12... | collective-permute-start | bytes 2752520 | tf_op jit(solution)/shard_map/ppermute | solution.py:165
  70.3 13.8 %copy-start.11 = (bf16[8,7,64,128]{3,2,1,0:T(8,128)(2,1)S(1)}, bf16[8,7,64,128]{3,2,1,0:T(8,128)(2,1)}, u32[]{:S(2)}) copy-start(bf16[8,7,64,128]{3,2,1,0:T(8,128)(2,1)} %get-tuple-element.45) | copy-start | bytes 2752516
  78.0 9.4 %copy-start.12 = (bf16[8,7,64,128]{3,2,1,0:T(8,128)(2,1)S(1)}, bf16[8,7,64,128]{3,2,1,0:T(8,128)(2,1)}, u32[]{:S(2)}) copy-start(bf16[8,7,64,128]{3,2,1,0:T(8,128)(2,1)} %get-tuple-element.38) | copy-start | bytes 2752516
  78.0 11.8 %copy-start.8 = (bf16[8,7,64,128]{3,2,1,0:T(8,128)(2,1)S(1)}, bf16[8,7,64,128]{3,2,1,0:T(8,128)(2,1)}, u32[]{:S(2)}) copy-start(bf16[8,7,64,128]{3,2,1,0:T(8,128)(2,1)} %get-tuple-element.34) | copy-start | bytes 2752516
  78.0 29.8 %collective-permute-start.11 = (bf16[8,7,64,128]{3,2,1,0:T(8,128)(2,1)}, bf16[8,7,64,128]{3,2,1,0:T(8,128)(2,1)S(1)}, u32[]{:S(2)}, u32[]{:S(2)}) collective-permute-start(bf16[8,7,64,128]{3,2,1,0:T(8,128)(2,1)} %get-tuple-element.42), channel_id=1, source_target_pairs={{0,2},{2,4},{4,6},{6,7},{7,5},{5,3},{3,1},{1,0},{8,10},{10,12},{12... | collective-permute-start | bytes 2752520 | tf_op jit(solution)/shard_map/ppermute | solution.py:165
  84.5 25.0 %collective-permute-start.15 = (bf16[8,7,64,128]{3,2,1,0:T(8,128)(2,1)S(1)}, bf16[8,7,64,128]{3,2,1,0:T(8,128)(2,1)S(1)}, u32[]{:S(2)}, u32[]{:S(2)}) collective-permute-start(bf16[8,7,64,128]{3,2,1,0:T(8,128)(2,1)S(1)} %add_convert_fusion.3), channel_id=1, source_target_pairs={{2,0},{4,2},{6,4},{7,6},{5,7},{3,5},{1,3},{0,1},{10,8},{12,10},{14... | collective-permute-start | bytes 2752520 | tf_op jit(solution)/shard_map/ppermute | solution.py:165
  87.4 40.5 %collective-permute-start.8 = (bf16[8,7,64,128]{3,2,1,0:T(8,128)(2,1)S(1)}, bf16[8,7,64,128]{3,2,1,0:T(8,128)(2,1)S(1)}, u32[]{:S(2)}, u32[]{:S(2)}) collective-permute-start(bf16[8,7,64,128]{3,2,1,0:T(8,128)(2,1)S(1)} %copy-done.12), channel_id=1, source_target_pairs={{2,0},{4,2},{6,4},{7,6},{5,7},{3,5},{1,3},{0,1},{10,8},{12,10},{14... | collective-permute-start | bytes 2752520 | tf_op jit(solution)/shard_map/ppermute | solution.py:165
  90.2 40.6 %collective-permute-start.5 = (bf16[8,7,64,128]{3,2,1,0:T(8,128)(2,1)S(1)}, bf16[8,7,64,128]{3,2,1,0:T(8,128)(2,1)S(1)}, u32[]{:S(2)}, u32[]{:S(2)}) collective-permute-start(bf16[8,7,64,128]{3,2,1,0:T(8,128)(2,1)S(1)} %add_convert_fusion.11), channel_id=1, source_target_pairs={{0,2},{2,4},{4,6},{6,7},{7,5},{5,3},{3,1},{1,0},{8,10},{10,12},{12... | collective-permute-start | bytes 2752520 | tf_op jit(solution)/shard_map/ppermute | solution.py:165
  103.7 5.8 %copy-start.9 = (bf16[8,7,64,128]{3,2,1,0:T(8,128)(2,1)S(1)}, bf16[8,7,64,128]{3,2,1,0:T(8,128)(2,1)}, u32[]{:S(2)}) copy-start(bf16[8,7,64,128]{3,2,1,0:T(8,128)(2,1)} %get-tuple-element.44) | copy-start | bytes 2752516
  109.4 18.5 %copy-start.6 = (bf16[8,7,64,128]{3,2,1,0:T(8,128)(2,1)S(1)}, bf16[8,7,64,128]{3,2,1,0:T(8,128)(2,1)}, u32[]{:S(2)}) copy-start(bf16[8,7,64,128]{3,2,1,0:T(8,128)(2,1)} %get-tuple-element.37) | copy-start | bytes 2752516
  109.4 37.8 %collective-permute-start.12 = (bf16[8,7,64,128]{3,2,1,0:T(8,128)(2,1)S(1)}, bf16[8,7,64,128]{3,2,1,0:T(8,128)(2,1)S(1)}, u32[]{:S(2)}, u32[]{:S(2)}) collective-permute-start(bf16[8,7,64,128]{3,2,1,0:T(8,128)(2,1)S(1)} %add_convert_fusion.5), channel_id=1, source_target_pairs={{0,2},{2,4},{4,6},{6,7},{7,5},{5,3},{3,1},{1,0},{8,10},{10,12},{12... | collective-permute-start | bytes 2752520 | tf_op jit(solution)/shard_map/ppermute | solution.py:165
  109.9 20.9 %copy-start.4 = (bf16[8,7,64,128]{3,2,1,0:T(8,128)(2,1)S(1)}, bf16[8,7,64,128]{3,2,1,0:T(8,128)(2,1)}, u32[]{:S(2)}) copy-start(bf16[8,7,64,128]{3,2,1,0:T(8,128)(2,1)} %get-tuple-element.33) | copy-start | bytes 2752516
  109.9 39.0 %collective-permute-start.16 = (bf16[8,7,64,128]{3,2,1,0:T(8,128)(2,1)S(1)}, bf16[8,7,64,128]{3,2,1,0:T(8,128)(2,1)S(1)}, u32[]{:S(2)}, u32[]{:S(2)}) collective-permute-start(bf16[8,7,64,128]{3,2,1,0:T(8,128)(2,1)S(1)} %add_convert_fusion.2), channel_id=1, source_target_pairs={{2,0},{4,2},{6,4},{7,6},{5,7},{3,5},{1,3},{0,1},{10,8},{12,10},{14... | collective-permute-start | bytes 2752520 | tf_op jit(solution)/shard_map/ppermute | solution.py:165
  128.2 39.0 %collective-permute-start.9 = (bf16[8,7,64,128]{3,2,1,0:T(8,128)(2,1)S(1)}, bf16[8,7,64,128]{3,2,1,0:T(8,128)(2,1)S(1)}, u32[]{:S(2)}, u32[]{:S(2)}) collective-permute-start(bf16[8,7,64,128]{3,2,1,0:T(8,128)(2,1)S(1)} %add_convert_fusion.8), channel_id=1, source_target_pairs={{2,0},{4,2},{6,4},{7,6},{5,7},{3,5},{1,3},{0,1},{10,8},{12,10},{14... | collective-permute-start | bytes 2752520 | tf_op jit(solution)/shard_map/ppermute | solution.py:165
  131.1 39.0 %collective-permute-start.6 = (bf16[8,7,64,128]{3,2,1,0:T(8,128)(2,1)S(1)}, bf16[8,7,64,128]{3,2,1,0:T(8,128)(2,1)S(1)}, u32[]{:S(2)}, u32[]{:S(2)}) collective-permute-start(bf16[8,7,64,128]{3,2,1,0:T(8,128)(2,1)S(1)} %add_convert_fusion.10), channel_id=1, source_target_pairs={{0,2},{2,4},{4,6},{6,7},{7,5},{5,3},{3,1},{1,0},{8,10},{10,12},{12... | collective-permute-start | bytes 2752520 | tf_op jit(solution)/shard_map/ppermute | solution.py:165
  144.3 4.6 %copy-start.10 = (bf16[8,7,64,128]{3,2,1,0:T(8,128)(2,1)S(1)}, bf16[8,7,64,128]{3,2,1,0:T(8,128)(2,1)}, u32[]{:S(2)}) copy-start(bf16[8,7,64,128]{3,2,1,0:T(8,128)(2,1)} %get-tuple-element.43) | copy-start | bytes 2752516
  148.7 18.5 %copy-start.7 = (bf16[8,7,64,128]{3,2,1,0:T(8,128)(2,1)S(1)}, bf16[8,7,64,128]{3,2,1,0:T(8,128)(2,1)}, u32[]{:S(2)}) copy-start(bf16[8,7,64,128]{3,2,1,0:T(8,128)(2,1)} %get-tuple-element.36) | copy-start | bytes 2752516
  148.7 37.8 %collective-permute-start.13 = (bf16[8,7,64,128]{3,2,1,0:T(8,128)(2,1)S(1)}, bf16[8,7,64,128]{3,2,1,0:T(8,128)(2,1)S(1)}, u32[]{:S(2)}, u32[]{:S(2)}) collective-permute-start(bf16[8,7,64,128]{3,2,1,0:T(8,128)(2,1)S(1)} %add_convert_fusion.4), channel_id=1, source_target_pairs={{0,2},{2,4},{4,6},{6,7},{7,5},{5,3},{3,1},{1,0},{8,10},{10,12},{12... | collective-permute-start | bytes 2752520 | tf_op jit(solution)/shard_map/ppermute | solution.py:165
  149.2 20.9 %copy-start.5 = (bf16[8,7,64,128]{3,2,1,0:T(8,128)(2,1)S(1)}, bf16[8,7,64,128]{3,2,1,0:T(8,128)(2,1)}, u32[]{:S(2)}) copy-start(bf16[8,7,64,128]{3,2,1,0:T(8,128)(2,1)} %get-tuple-element.32) | copy-start | bytes 2752516
  149.2 37.7 %collective-permute-start.17 = (bf16[8,7,64,128]{3,2,1,0:T(8,128)(2,1)S(1)}, bf16[8,7,64,128]{3,2,1,0:T(8,128)(2,1)S(1)}, u32[]{:S(2)}, u32[]{:S(2)}) collective-permute-start(bf16[8,7,64,128]{3,2,1,0:T(8,128)(2,1)S(1)} %add_convert_fusion.1), channel_id=1, source_target_pairs={{2,0},{4,2},{6,4},{7,6},{5,7},{3,5},{1,3},{0,1},{10,8},{12,10},{14... | collective-permute-start | bytes 2752520 | tf_op jit(solution)/shard_map/ppermute | solution.py:165
  167.6 37.2 %collective-permute-start.10 = (bf16[8,7,64,128]{3,2,1,0:T(8,128)(2,1)S(1)}, bf16[8,7,64,128]{3,2,1,0:T(8,128)(2,1)S(1)}, u32[]{:S(2)}, u32[]{:S(2)}) collective-permute-start(bf16[8,7,64,128]{3,2,1,0:T(8,128)(2,1)S(1)} %add_convert_fusion.7), channel_id=1, source_target_pairs={{2,0},{4,2},{6,4},{7,6},{5,7},{3,5},{1,3},{0,1},{10,8},{12,10},{14... | collective-permute-start | bytes 2752520 | tf_op jit(solution)/shard_map/ppermute | solution.py:165
  171.4 34.0 %collective-permute-start.7 = (bf16[8,7,64,128]{3,2,1,0:T(8,128)(2,1)}, bf16[8,7,64,128]{3,2,1,0:T(8,128)(2,1)S(1)}, u32[]{:S(2)}, u32[]{:S(2)}) collective-permute-start(bf16[8,7,64,128]{3,2,1,0:T(8,128)(2,1)} %add_convert_fusion.9), channel_id=1, source_target_pairs={{0,2},{2,4},{4,6},{6,7},{7,5},{5,3},{3,1},{1,0},{8,10},{10,12},{12... | collective-permute-start | bytes 2752520 | tf_op jit(solution)/shard_map/ppermute | solution.py:165
  186.9 18.5 %copy-start.3 = (bf16[8,7,64,128]{3,2,1,0:T(8,128)(2,1)S(1)}, bf16[8,7,64,128]{3,2,1,0:T(8,128)(2,1)}, u32[]{:S(2)}) copy-start(bf16[8,7,64,128]{3,2,1,0:T(8,128)(2,1)} %get-tuple-element.31) | copy-start | bytes 2752516

commit v3 on v2

--- a/solution.py
+++ b/solution.py
@@ -12,8 +12,12 @@
 VMEM_BYTES = 56 * 1024 * 1024
 
 
+def columns(count):
+    return 1 << ((count.bit_length() - 1) // 2)
+
+
 def ring_order(count):
-    nx = 1 << ((count.bit_length() - 1) // 2)
+    nx = columns(count)
     nz = count // nx
     if nx < 2 or nz < 2 or nz % 2 or nx * nz != count:
         return list(range(count))
@@ -24,16 +28,44 @@
     return [z * nx + x for z, x in walk]
 
 
-def chunk_kernel(
-    distance, places, owner, agg, near, slot, a_ref, own, below, above, left, right,
-    low, high, acc, a_buf, p_buf, t_buf, picked, sems,
-):
+def halo_dev(p_blocks, count):
+    if columns(count) != 2:
+        forward = [(i, i + 1) for i in range(count - 1)]
+        backward = [(b, a) for a, b in forward]
+        return (
+            (0, p_blocks.shape[0]),
+            [lax.ppermute(p_blocks, "dev", backward)],
+            [lax.ppermute(p_blocks, "dev", forward)],
+        )
+    elems = p_blocks.shape[0]
+    cuts = (0, 3 * elems // 8, 3 * elems // 4, elems)
+    swap = [(i, i ^ 1) for i in range(count)]
+    relay = [(i, i + 2) for i in range(0, count - 2, 2)] + [(i, i - 2) for i in range(3, count, 2)]
+    straight = [(i, i - 1) for i in range(2, count, 2)] + [(i, i + 1) for i in range(1, count - 1, 2)]
+    first, second = [], []
+    for low, high in zip(cuts, cuts[1:]):
+        piece = p_blocks[low:high]
+        if first:
+            piece, _ = lax.optimization_barrier((piece, first[-1]))
+        first.append(lax.ppermute(piece, "dev", swap))
+        if high < elems:
+            second.append(lax.ppermute(first[-1], "dev", relay))
+        else:
+            second.append(lax.ppermute(piece, "dev", straight))
+    return cuts, first, second
+
+
+def chunk_kernel(distance, cuts, places, owner, agg, near, slot, a_ref, own, *refs):
+    pieces = len(cuts) - 1
+    first, second, (left, right) = refs[:pieces], refs[pieces : 2 * pieces], refs[2 * pieces : 2 * pieces + 2]
+    low, high, acc, a_buf, p_buf, t_buf, picked, sems = refs[2 * pieces + 2 :]
     elems, count_dev = owner.shape[0], places.shape[0]
     aggs, _, half, width = low.shape
     depth = a_buf.shape[0]
-    sources = (own, own, below, above, left, right)
-
-    target = lax.rem(places[lax.axis_index("dev")] + distance, count_dev)
+    me = lax.axis_index("dev")
+    odd = lax.rem(me, 2) if pieces > 1 else 0
+
+    target = lax.rem(places[me] + distance, count_dev)
 
     def pick(e, count):
         hit = places[owner[e, 0]] == target
@@ -46,19 +78,24 @@
 
     count = lax.fori_loop(0, elems, pick, jnp.int32(0))
 
-    def fetches(i):
-        e, buf = picked[i], lax.rem(i, depth)
-        copies = [pltpu.make_async_copy(a_ref.at[e], a_buf.at[buf], sems.at[buf, 0])]
-        for f in range(KC):
-            source = own.at[e] if f == 0 else sources[f - 1].at[near[e, f - 1]]
-            copies.append(pltpu.make_async_copy(source, p_buf.at[buf, f], sems.at[buf, f + 1]))
-        return copies
+    def fetch(source, buf, f):
+        return pltpu.make_async_copy(source, p_buf.at[buf, f], sems.at[buf, f])
 
     def start(i):
         @pl.when(i < count)
         def _():
-            for copy in fetches(i):
-                copy.start()
+            e, buf = picked[i], lax.rem(i, depth)
+            pltpu.make_async_copy(a_ref.at[e], a_buf.at[buf], sems.at[buf, KC]).start()
+            fetch(own.at[e], buf, 0).start()
+            for f, source in ((1, own), (2, own), (5, left), (6, right)):
+                fetch(source.at[near[e, f - 1]], buf, f).start()
+            for f, parts in ((4 - odd, first), (3 + odd, second)):
+                n = near[e, f - 1]
+                for part, at, end in zip(parts, cuts, cuts[1:]):
+
+                    @pl.when((n >= at) & (n < end))
+                    def _():
+                        fetch(part.at[n - at], buf, f).start()
 
     for i in range(depth - 1):
         start(i)
@@ -67,8 +104,9 @@
     def element(i, carry):
         start(i + depth - 1)
         e, buf = picked[i], lax.rem(i, depth)
-        for copy in fetches(i):
-            copy.wait()
+        pltpu.make_async_copy(a_ref.at[e], a_buf.at[buf], sems.at[buf, KC]).wait()
+        for f in range(KC):
+            fetch(own.at[e], buf, f).wait()
         for f in range(KC):
             t_buf[:, f * width : (f + 1) * width] = jnp.dot(
                 a_buf[buf, f], p_buf[buf, f], preferred_element_type=jnp.float32
@@ -94,7 +132,7 @@
     lax.fori_loop(0, aggs, store, 0)
 
 
-def chunk(distance, aggs, tables, a_blocks, blocks):
+def chunk(distance, aggs, cuts, tables, a_blocks, blocks):
     elems, _, width, _ = a_blocks.shape
     out = jax.ShapeDtypeStruct((aggs, KC, width // 2, width), jnp.bfloat16)
     smem = pl.BlockSpec(memory_space=pltpu.SMEM)
@@ -102,9 +140,9 @@
     hbm = pl.BlockSpec(memory_space=pl.ANY)
     depth = 4
     return pl.pallas_call(
-        functools.partial(chunk_kernel, distance),
+        functools.partial(chunk_kernel, distance, cuts),
         out_shape=(out, out),
-        in_specs=[smem] * 5 + [hbm] * 6,
+        in_specs=[smem] * 5 + [hbm] * (1 + len(blocks)),
         out_specs=(vmem, vmem),
         scratch_shapes=[
             pltpu.VMEM((aggs * KC, width, width), jnp.float32),
@@ -134,21 +172,19 @@
     places = jnp.array([order.index(d) for d in range(count)], jnp.int32)
     tables = (places, owner, agg_local, neighbours, coarse_slot)
 
-    halo = []
-    for axis in ("dev", "grp"):
-        size = lax.axis_size(axis)
-        forward = [(i, i + 1) for i in range(size - 1)]
-        backward = [(b, a) for a, b in forward]
-        halo += [lax.ppermute(p_blocks, axis, forward), lax.ppermute(p_blocks, axis, backward)]
-    blocks = (p_blocks, *halo)
-    blocks = lax.optimization_barrier(blocks)
+    cuts, first, second = halo_dev(p_blocks, count)
+    size = lax.axis_size("grp")
+    forward = [(i, i + 1) for i in range(size - 1)]
+    backward = [(b, a) for a, b in forward]
+    left, right = lax.ppermute(p_blocks, "grp", forward), lax.ppermute(p_blocks, "grp", backward)
+    blocks = lax.optimization_barrier((p_blocks, *first, *second, left, right))
 
     chunks = {}
 
     def part(distance, side):
         distance %= count
         if distance not in chunks:
-            chunks[distance] = chunk(distance, aggs, tables, a_blocks, blocks)
+            chunks[distance] = chunk(distance, aggs, cuts, tables, a_blocks, blocks)
         return chunks[distance][side]
 
     right = [(order[i], order[(i + 1) % count]) for i in range(count)]

time: 208 us -> 196 us (0.942)
  waiting for transfers between devices: 111 us -> 89.6 us
  starting transfers between devices: 29.4 us -> 38.7 us
    ppermute x4 -> x8, waiting for transfers between devices: 39.8 us -> 16.9 us  [the longest x3 16.9 us: halo_dev(): first.append(lax.ppermute(piece, 'dev', swap))]
    ppermute x4 -> x8, starting transfers between devices: 9.92 us -> 19.5 us  [the longest x3 8.3 us: halo_dev(): first.append(lax.ppermute(piece, 'dev', swap))]
    slice x0 -> x2, local copies, waits for them, and re-layouts: none -> 2.89 us  [halo_dev(): piece = p_blocks[low:high]]
    unnamed x29 -> x41, local copies, waits for them, and re-layouts: 5.07 us -> 3.41 us
  transfers between devices with their start and end apart: 18 -> 22, of which waited for: 11 -> 11; matrix products, arithmetic and copies ran while one was open for 6% -> 6% of each run, Pallas kernels for 22% -> 22%
where the time goes in v3:
time: 196 us; the launch traced here: 195 us
  waiting for transfers between devices  89.6 us (46%)
  Pallas kernels  50.5 us (26%)
  starting transfers between devices  38.7 us (20%)
  other arithmetic  9.38 us (5%)
  local copies, waits for them, and re-layouts  6.3 us (3%)
    ppermute x14, waiting for transfers between devices, on_device(): got[sign, n] = lax.ppermute(terms[0] if n < 2 else add(*terms), 'dev', perm)  72.7 us
    pallas_call x8, Pallas kernels, chunk(): pl.pallas_call(functools.partial(chunk_kernel, distance, cuts), out_shape...  50.5 us
    ppermute x14, starting transfers between devices, on_device(): got[sign, n] = lax.ppermute(terms[0] if n < 2 else add(*terms), 'dev', perm)  19.3 us
    ppermute x3, waiting for transfers between devices, halo_dev(): first.append(lax.ppermute(piece, 'dev', swap))  16.9 us
    ppermute x3, starting transfers between devices, halo_dev(): first.append(lax.ppermute(piece, 'dev', swap))  8.3 us
    convert_element_type x12, other arithmetic, add(): return sum((t.astype(jnp.float32) for t in terms)).astype(jnp.bfloat16)  7.99 us
    ppermute x2, starting transfers between devices, halo_dev(): second.append(lax.ppermute(first[-1], 'dev', relay))  7.69 us
  transfers between devices with their start and end apart: 22, of which 11 were waited for; matrix products, arithmetic and copies ran while one was open for 6% of the time, Pallas kernels for 22%

profile of v3, /device:TPU:0, one launch (start us, length us, event | category | flops | bytes accessed | tf_op | source)
XLA Modules:
  0.0 194.9 jit_solution(3015796782416929372)
XLA Ops:
  1.2 3.0 %collective-permute-start = (bf16[12,128,128]{2,1,0:T(8,128)(2,1)S(1)}, bf16[12,128,128]{2,1,0:T(8,128)(2,1)S(1)}, u32[]{:S(2)}, u32[]{:S(2)}) collective-permute-start(bf16[12,128,128]{2,1,0:T(8,128)(2,1)S(1)} %get-tuple-element.60), channel_id=1, source_target_pairs={{0,1},{1,0},{2,3},{3,2},{4,5},{5,4},{6,7},{7,6},{8,9},{9,8},{10,11... | collective-permute-start | bytes 1179656 | tf_op jit(solution)/shard_map/ppermute | solution.py:50
  4.2 1.5 collective-permute-start.6
  7.1 6.3 %collective-permute-done.refs_0_ = bf16[12,128,128]{2,1,0:T(8,128)(2,1)S(1)} collective-permute-done((bf16[12,128,128]{2,1,0:T(8,128)(2,1)S(1)}, bf16[12,128,128]{2,1,0:T(8,128)(2,1)S(1)}, u32[]{:S(2)}, u32[]{:S(2)}) %collective-permute-start) | collective-permute-done | bytes 393248 | tf_op jit(solution)/shard_map/ppermute | solution.py:50
  13.4 1.7 collective-permute-start.1
  15.1 3.5 %collective-permute-start.3 = (bf16[12,128,128]{2,1,0:T(8,128)(2,1)S(1)}, bf16[12,128,128]{2,1,0:T(8,128)(2,1)S(1)}, u32[]{:S(2)}, u32[]{:S(2)}) collective-permute-start(bf16[12,128,128]{2,1,0:T(8,128)(2,1)S(1)} %collective-permute-done.refs_0_), channel_id=1, source_target_pairs={{0,2},{2,4},{4,6},{3,1},{5,3},{7,5},{8,10},{10,12},{12,14},{11,9},... | collective-permute-start | bytes 1179656 | tf_op jit(solution)/shard_map/ppermute | solution.py:52
  18.6 5.1 %collective-permute-done.1.refs_1_ = bf16[12,128,128]{2,1,0:T(8,128)(2,1)S(1)} collective-permute-done((bf16[12,128,128]{2,1,0:T(8,128)(2,1)S(1)}, bf16[12,128,128]{2,1,0:T(8,128)(2,1)S(1)}, u32[]{:S(2)}, u32[]{:S(2)}) %collective-permute-start.1) | collective-permute-done | bytes 393248 | tf_op jit(solution)/shard_map/ppermute | solution.py:50
  23.7 4.2 %collective-permute-start.4 = (bf16[12,128,128]{2,1,0:T(8,128)(2,1)S(1)}, bf16[12,128,128]{2,1,0:T(8,128)(2,1)}, u32[]{:S(2)}, u32[]{:S(2)}) collective-permute-start(bf16[12,128,128]{2,1,0:T(8,128)(2,1)S(1)} %collective-permute-done.1.refs_1_), channel_id=1, source_target_pairs={{0,2},{2,4},{4,6},{3,1},{5,3},{7,5},{8,10},{10,12},{12,14},{11,9},... | collective-permute-start | bytes 1179656 | tf_op jit(solution)/shard_map/ppermute | solution.py:52
  27.9 1.7 slice.11
  30.2 3.6 %collective-permute-start.2 = (bf16[8,128,128]{2,1,0:T(8,128)(2,1)}, bf16[8,128,128]{2,1,0:T(8,128)(2,1)}, u32[]{:S(2)}, u32[]{:S(2)}) collective-permute-start(bf16[8,128,128]{2,1,0:T(8,128)(2,1)} %slice.11), channel_id=1, source_target_pairs={{0,1},{1,0},{2,3},{3,2},{4,5},{5,4},{6,7},{7,6},{8,9},{9,8},{10,11... | collective-permute-start | bytes 786440 | tf_op jit(solution)/shard_map/ppermute | solution.py:50
  35.8 5.5 %collective-permute-done.2.refs_2_ = bf16[8,128,128]{2,1,0:T(8,128)(2,1)} collective-permute-done((bf16[8,128,128]{2,1,0:T(8,128)(2,1)}, bf16[8,128,128]{2,1,0:T(8,128)(2,1)}, u32[]{:S(2)}, u32[]{:S(2)}) %collective-permute-start.2) | collective-permute-done | bytes 262176 | tf_op jit(solution)/shard_map/ppermute | solution.py:50
  42.7 6.7 %shard_map.77 = (bf16[8,7,64,128]{3,2,1,0:T(8,128)(2,1)}, bf16[8,7,64,128]{3,2,1,0:T(8,128)(2,1)}) custom-call(s32[8]{0:T(128)} %constant.2.clone.places, s32[32,1]{1,0:T(8,128)} %copy.8.owner, s32[32]{0:T(128)} %agg.15, s32[32,6]{1,0:T(8,128)} %copy.9.near, s32[32,7]{1,0:T(8,128)} %copy.10.slot, bf16[32,7,128,128]{3,2,1,0:T(8,128)(2,1)} %a_ref.15, ...), custom_call_target="tpu_custom_call" | custom-call | flops 234881024 | bytes 12582912 | tf_op jit(solution)/shard_map/pallas_call | solution.py:142
  50.7 2.9 %collective-permute-start.8 = (bf16[8,7,64,128]{3,2,1,0:T(8,128)(2,1)}, bf16[8,7,64,128]{3,2,1,0:T(8,128)(2,1)S(1)}, u32[]{:S(2)}, u32[]{:S(2)}) collective-permute-start(bf16[8,7,64,128]{3,2,1,0:T(8,128)(2,1)} %get-tuple-element.47), channel_id=1, source_target_pairs={{0,2},{2,4},{4,6},{6,7},{7,5},{5,3},{3,1},{1,0},{8,10},{10,12},{12... | collective-permute-start | bytes 2752520 | tf_op jit(solution)/shard_map/ppermute | solution.py:201
  53.6 6.3 %shard_map.80 = (bf16[8,7,64,128]{3,2,1,0:T(8,128)(2,1)}, bf16[8,7,64,128]{3,2,1,0:T(8,128)(2,1)}) custom-call(s32[8]{0:T(128)} %constant.2.clone.places, s32[32,1]{1,0:T(8,128)} %copy.8.owner, s32[32]{0:T(128)} %agg.15, s32[32,6]{1,0:T(8,128)} %copy.9.near, s32[32,7]{1,0:T(8,128)} %copy.10.slot, bf16[32,7,128,128]{3,2,1,0:T(8,128)(2,1)} %a_ref.15, ...), custom_call_target="tpu_custom_call" | custom-call | flops 234881024 | bytes 12582912 | tf_op jit(solution)/shard_map/pallas_call | solution.py:142
  59.9 5.6 %shard_map.76 = (bf16[8,7,64,128]{3,2,1,0:T(8,128)(2,1)}, bf16[8,7,64,128]{3,2,1,0:T(8,128)(2,1)}) custom-call(s32[8]{0:T(128)} %constant.2.clone.places, s32[32,1]{1,0:T(8,128)} %copy.8.owner, s32[32]{0:T(128)} %agg.15, s32[32,6]{1,0:T(8,128)} %copy.9.near, s32[32,7]{1,0:T(8,128)} %copy.10.slot, bf16[32,7,128,128]{3,2,1,0:T(8,128)(2,1)} %a_ref.15, ...), custom_call_target="tpu_custom_call" | custom-call | flops 234881024 | bytes 12582912 | tf_op jit(solution)/shard_map/pallas_call | solution.py:142
  65.6 2.9 %collective-permute-start.15 = (bf16[8,7,64,128]{3,2,1,0:T(8,128)(2,1)}, bf16[8,7,64,128]{3,2,1,0:T(8,128)(2,1)S(1)}, u32[]{:S(2)}, u32[]{:S(2)}) collective-permute-start(bf16[8,7,64,128]{3,2,1,0:T(8,128)(2,1)} %get-tuple-element.54), channel_id=1, source_target_pairs={{0,2},{2,4},{4,6},{6,7},{7,5},{5,3},{3,1},{1,0},{8,10},{10,12},{12... | collective-permute-start | bytes 2752520 | tf_op jit(solution)/shard_map/ppermute | solution.py:201
  68.4 5.0 %collective-permute-done.18 = bf16[8,7,64,128]{3,2,1,0:T(8,128)(2,1)S(1)} collective-permute-done((bf16[8,7,64,128]{3,2,1,0:T(8,128)(2,1)}, bf16[8,7,64,128]{3,2,1,0:T(8,128)(2,1)S(1)}, u32[]{:S(2)}, u32[]{:S(2)}) %collective-permute-start.18) | collective-permute-done | bytes 917536 | tf_op jit(solution)/shard_map/ppermute | solution.py:201
  75.0 2.4 %collective-permute-start.12 = (bf16[8,7,64,128]{3,2,1,0:T(8,128)(2,1)S(1)}, bf16[8,7,64,128]{3,2,1,0:T(8,128)(2,1)S(1)}, u32[]{:S(2)}, u32[]{:S(2)}) collective-permute-start(bf16[8,7,64,128]{3,2,1,0:T(8,128)(2,1)S(1)} %copy-done.18), channel_id=1, source_target_pairs={{2,0},{4,2},{6,4},{7,6},{5,7},{3,5},{1,3},{0,1},{10,8},{12,10},{14... | collective-permute-start | bytes 2752520 | tf_op jit(solution)/shard_map/ppermute | solution.py:201
  77.8 5.9 %shard_map.79 = (bf16[8,7,64,128]{3,2,1,0:T(8,128)(2,1)}, bf16[8,7,64,128]{3,2,1,0:T(8,128)(2,1)}) custom-call(s32[8]{0:T(128)} %constant.2.clone.places, s32[32,1]{1,0:T(8,128)} %copy.8.owner, s32[32]{0:T(128)} %agg.15, s32[32,6]{1,0:T(8,128)} %copy.9.near, s32[32,7]{1,0:T(8,128)} %copy.10.slot, bf16[32,7,128,128]{3,2,1,0:T(8,128)(2,1)} %a_ref.15, ...), custom_call_target="tpu_custom_call" | custom-call | flops 234881024 | bytes 12582912 | tf_op jit(solution)/shard_map/pallas_call | solution.py:142
  83.6 8.0 %shard_map.75 = (bf16[8,7,64,128]{3,2,1,0:T(8,128)(2,1)}, bf16[8,7,64,128]{3,2,1,0:T(8,128)(2,1)}) custom-call(s32[8]{0:T(128)} %constant.2.clone.places, s32[32,1]{1,0:T(8,128)} %copy.8.owner, s32[32]{0:T(128)} %agg.15, s32[32,6]{1,0:T(8,128)} %copy.9.near, s32[32,7]{1,0:T(8,128)} %copy.10.slot, bf16[32,7,128,128]{3,2,1,0:T(8,128)(2,1)} %a_ref.15, ...), custom_call_target="tpu_custom_call" | custom-call | flops 234881024 | bytes 12582912 | tf_op jit(solution)/shard_map/pallas_call | solution.py:142
  91.7 4.3 %collective-permute-done.15 = bf16[8,7,64,128]{3,2,1,0:T(8,128)(2,1)S(1)} collective-permute-done((bf16[8,7,64,128]{3,2,1,0:T(8,128)(2,1)}, bf16[8,7,64,128]{3,2,1,0:T(8,128)(2,1)S(1)}, u32[]{:S(2)}, u32[]{:S(2)}) %collective-permute-start.15) | collective-permute-done | bytes 917536 | tf_op jit(solution)/shard_map/ppermute | solution.py:201
  96.0 1.5 add_convert_fusion.5
  100.0 16.8 %collective-permute-done.12 = bf16[8,7,64,128]{3,2,1,0:T(8,128)(2,1)S(1)} collective-permute-done((bf16[8,7,64,128]{3,2,1,0:T(8,128)(2,1)S(1)}, bf16[8,7,64,128]{3,2,1,0:T(8,128)(2,1)S(1)}, u32[]{:S(2)}, u32[]{:S(2)}) %collective-permute-start.12) | collective-permute-done | bytes 917536 | tf_op jit(solution)/shard_map/ppermute | solution.py:201
  119.6 5.4 %shard_map.78 = (bf16[8,7,64,128]{3,2,1,0:T(8,128)(2,1)}, bf16[8,7,64,128]{3,2,1,0:T(8,128)(2,1)}) custom-call(s32[8]{0:T(128)} %constant.2.clone.places, s32[32,1]{1,0:T(8,128)} %copy.8.owner, s32[32]{0:T(128)} %agg.15, s32[32,6]{1,0:T(8,128)} %copy.9.near, s32[32,7]{1,0:T(8,128)} %copy.10.slot, bf16[32,7,128,128]{3,2,1,0:T(8,128)(2,1)} %a_ref.15, ...), custom_call_target="tpu_custom_call" | custom-call | flops 234881024 | bytes 12582912 | tf_op jit(solution)/shard_map/pallas_call | solution.py:142
  125.1 5.5 %shard_map.74 = (bf16[8,7,64,128]{3,2,1,0:T(8,128)(2,1)}, bf16[8,7,64,128]{3,2,1,0:T(8,128)(2,1)}) custom-call(s32[8]{0:T(128)} %constant.2.clone.places, s32[32,1]{1,0:T(8,128)} %copy.8.owner, s32[32]{0:T(128)} %agg.15, s32[32,6]{1,0:T(8,128)} %copy.9.near, s32[32,7]{1,0:T(8,128)} %copy.10.slot, bf16[32,7,128,128]{3,2,1,0:T(8,128)(2,1)} %a_ref.15, ...), custom_call_target="tpu_custom_call" | custom-call | flops 234881024 | bytes 12582912 | tf_op jit(solution)/shard_map/pallas_call | solution.py:142
  130.5 4.7 %collective-permute-done.16 = bf16[8,7,64,128]{3,2,1,0:T(8,128)(2,1)S(1)} collective-permute-done((bf16[8,7,64,128]{3,2,1,0:T(8,128)(2,1)S(1)}, bf16[8,7,64,128]{3,2,1,0:T(8,128)(2,1)S(1)}, u32[]{:S(2)}, u32[]{:S(2)}) %collective-permute-start.16) | collective-permute-done | bytes 917536 | tf_op jit(solution)/shard_map/ppermute | solution.py:201
  135.3 1.5 add_convert_fusion.4
  139.4 16.8 %collective-permute-done.13 = bf16[8,7,64,128]{3,2,1,0:T(8,128)(2,1)S(1)} collective-permute-done((bf16[8,7,64,128]{3,2,1,0:T(8,128)(2,1)S(1)}, bf16[8,7,64,128]{3,2,1,0:T(8,128)(2,1)S(1)}, u32[]{:S(2)}, u32[]{:S(2)}) %collective-permute-start.13) | collective-permute-done | bytes 917536 | tf_op jit(solution)/shard_map/ppermute | solution.py:201
  159.0 7.2 %shard_map.73 = (bf16[8,7,64,128]{3,2,1,0:T(8,128)(2,1)}, bf16[8,7,64,128]{3,2,1,0:T(8,128)(2,1)}) custom-call(s32[8]{0:T(128)} %constant.2.clone.places, s32[32,1]{1,0:T(8,128)} %copy.8.owner, s32[32]{0:T(128)} %agg.15, s32[32,6]{1,0:T(8,128)} %copy.9.near, s32[32,7]{1,0:T(8,128)} %copy.10.slot, bf16[32,7,128,128]{3,2,1,0:T(8,128)(2,1)} %a_ref.15, ...), custom_call_target="tpu_custom_call" | custom-call | flops 234881024 | bytes 12582912 | tf_op jit(solution)/shard_map/pallas_call | solution.py:142
  166.2 8.5 %collective-permute-done.17 = bf16[8,7,64,128]{3,2,1,0:T(8,128)(2,1)S(1)} collective-permute-done((bf16[8,7,64,128]{3,2,1,0:T(8,128)(2,1)S(1)}, bf16[8,7,64,128]{3,2,1,0:T(8,128)(2,1)S(1)}, u32[]{:S(2)}, u32[]{:S(2)}) %collective-permute-start.17) | collective-permute-done | bytes 917536 | tf_op jit(solution)/shard_map/ppermute | solution.py:201
  175.8 1.7 add_convert_fusion
  177.6 15.4 %collective-permute-done.14 = bf16[8,7,64,128]{3,2,1,0:T(8,128)(2,1)S(1)} collective-permute-done((bf16[8,7,64,128]{3,2,1,0:T(8,128)(2,1)S(1)}, bf16[8,7,64,128]{3,2,1,0:T(8,128)(2,1)S(1)}, u32[]{:S(2)}, u32[]{:S(2)}) %collective-permute-start.14) | collective-permute-done | bytes 917536 | tf_op jit(solution)/shard_map/ppermute | solution.py:201
  193.5 1.4 pad_maximum_fusion
  (76 shorter events, 22.1 us)
Async XLA Ops:
  0.0 33.8 %copy-start.15 = (s32[32,6]{0,1:T(8,128)S(1)}, s32[32,6]{0,1:T(8,128)}, u32[]{:S(2)}) copy-start(s32[32,6]{0,1:T(8,128)} %param.9) | copy-start | bytes 2308
  0.0 34.5 %copy-start.16 = (s32[32,7]{0,1:T(8,128)S(1)}, s32[32,7]{0,1:T(8,128)}, u32[]{:S(2)}) copy-start(s32[32,7]{0,1:T(8,128)} %param.10) | copy-start | bytes 2692
  0.0 35.2 %copy-start.17 = (s32[32,1]{0,1:T(1,128)S(1)}, s32[32,1]{0,1:T(1,128)}, u32[]{:S(2)}) copy-start(s32[32,1]{0,1:T(1,128)} %param.11) | copy-start | bytes 388
  1.2 12.1 %collective-permute-start = (bf16[12,128,128]{2,1,0:T(8,128)(2,1)S(1)}, bf16[12,128,128]{2,1,0:T(8,128)(2,1)S(1)}, u32[]{:S(2)}, u32[]{:S(2)}) collective-permute-start(bf16[12,128,128]{2,1,0:T(8,128)(2,1)S(1)} %get-tuple-element.60), channel_id=1, source_target_pairs={{0,1},{1,0},{2,3},{3,2},{4,5},{5,4},{6,7},{7,6},{8,9},{9,8},{10,11... | collective-permute-start | bytes 1179656 | tf_op jit(solution)/shard_map/ppermute | solution.py:50
  4.2 37.1 %collective-permute-start.6 = (bf16[32,128,128]{2,1,0:T(8,128)(2,1)}, bf16[32,128,128]{2,1,0:T(8,128)(2,1)S(1)}, u32[]{:S(2)}, u32[]{:S(2)}) collective-permute-start(bf16[32,128,128]{2,1,0:T(8,128)(2,1)} %own.7), channel_id=1, source_target_pairs={{0,8},{8,16},{16,24},{1,9},{9,17},{17,25},{2,10},{10,18},{18,26},{... | collective-permute-start | bytes 3145736 | tf_op jit(solution)/shard_map/ppermute | solution.py:179
  5.8 35.6 %collective-permute-start.7 = (bf16[32,128,128]{2,1,0:T(8,128)(2,1)}, bf16[32,128,128]{2,1,0:T(8,128)(2,1)S(1)}, u32[]{:S(2)}, u32[]{:S(2)}) collective-permute-start(bf16[32,128,128]{2,1,0:T(8,128)(2,1)} %own.7), channel_id=1, source_target_pairs={{8,0},{16,8},{24,16},{9,1},{17,9},{25,17},{10,2},{18,10},{26,18},{... | collective-permute-start | bytes 3145736 | tf_op jit(solution)/shard_map/ppermute | solution.py:179
  13.4 28.0 %copy-start.2 = (bf16[12,128,128]{2,1,0:T(8,128)(2,1)}, bf16[12,128,128]{2,1,0:T(8,128)(2,1)S(1)}, u32[]{:S(2)}) copy-start(bf16[12,128,128]{2,1,0:T(8,128)(2,1)S(1)} %collective-permute-done.refs_0_) | copy-start | bytes 1179652
  13.4 10.3 %collective-permute-start.1 = (bf16[12,128,128]{2,1,0:T(8,128)(2,1)S(1)}, bf16[12,128,128]{2,1,0:T(8,128)(2,1)S(1)}, u32[]{:S(2)}, u32[]{:S(2)}) collective-permute-start(bf16[12,128,128]{2,1,0:T(8,128)(2,1)S(1)} %get-tuple-element.32), channel_id=1, source_target_pairs={{0,1},{1,0},{2,3},{3,2},{4,5},{5,4},{6,7},{7,6},{8,9},{9,8},{10,11... | collective-permute-start | bytes 1179656 | tf_op jit(solution)/shard_map/ppermute | solution.py:50
  15.1 15.1 %collective-permute-start.3 = (bf16[12,128,128]{2,1,0:T(8,128)(2,1)S(1)}, bf16[12,128,128]{2,1,0:T(8,128)(2,1)S(1)}, u32[]{:S(2)}, u32[]{:S(2)}) collective-permute-start(bf16[12,128,128]{2,1,0:T(8,128)(2,1)S(1)} %collective-permute-done.refs_0_), channel_id=1, source_target_pairs={{0,2},{2,4},{4,6},{3,1},{5,3},{7,5},{8,10},{10,12},{12,14},{11,9},... | collective-permute-start | bytes 1179656 | tf_op jit(solution)/shard_map/ppermute | solution.py:52
  23.7 17.7 %copy-start.3 = (bf16[12,128,128]{2,1,0:T(8,128)(2,1)}, bf16[12,128,128]{2,1,0:T(8,128)(2,1)S(1)}, u32[]{:S(2)}) copy-start(bf16[12,128,128]{2,1,0:T(8,128)(2,1)S(1)} %collective-permute-done.1.refs_1_) | copy-start | bytes 1179652
  23.7 17.7 %collective-permute-start.4 = (bf16[12,128,128]{2,1,0:T(8,128)(2,1)S(1)}, bf16[12,128,128]{2,1,0:T(8,128)(2,1)}, u32[]{:S(2)}, u32[]{:S(2)}) collective-permute-start(bf16[12,128,128]{2,1,0:T(8,128)(2,1)S(1)} %collective-permute-done.1.refs_1_), channel_id=1, source_target_pairs={{0,2},{2,4},{4,6},{3,1},{5,3},{7,5},{8,10},{10,12},{12,14},{11,9},... | collective-permute-start | bytes 1179656 | tf_op jit(solution)/shard_map/ppermute | solution.py:52
  29.5 6.3 %collective-permute-start.5 = (bf16[8,128,128]{2,1,0:T(8,128)(2,1)}, bf16[8,128,128]{2,1,0:T(8,128)(2,1)S(1)}, u32[]{:S(2)}, u32[]{:S(2)}) collective-permute-start(bf16[8,128,128]{2,1,0:T(8,128)(2,1)} %slice.11), channel_id=1, source_target_pairs={{2,1},{4,3},{6,5},{1,2},{3,4},{5,6},{10,9},{12,11},{14,13},{9,10},... | collective-permute-start | bytes 786440 | tf_op jit(solution)/shard_map/ppermute | solution.py:54
  30.2 11.1 %collective-permute-start.2 = (bf16[8,128,128]{2,1,0:T(8,128)(2,1)}, bf16[8,128,128]{2,1,0:T(8,128)(2,1)}, u32[]{:S(2)}, u32[]{:S(2)}) collective-permute-start(bf16[8,128,128]{2,1,0:T(8,128)(2,1)} %slice.11), channel_id=1, source_target_pairs={{0,1},{1,0},{2,3},{3,2},{4,5},{5,4},{6,7},{7,6},{8,9},{9,8},{10,11... | collective-permute-start | bytes 786440 | tf_op jit(solution)/shard_map/ppermute | solution.py:50
  49.4 24.1 %collective-permute-start.18 = (bf16[8,7,64,128]{3,2,1,0:T(8,128)(2,1)}, bf16[8,7,64,128]{3,2,1,0:T(8,128)(2,1)S(1)}, u32[]{:S(2)}, u32[]{:S(2)}) collective-permute-start(bf16[8,7,64,128]{3,2,1,0:T(8,128)(2,1)} %get-tuple-element.58), channel_id=1, source_target_pairs={{2,0},{4,2},{6,4},{7,6},{5,7},{3,5},{1,3},{0,1},{10,8},{12,10},{14... | collective-permute-start | bytes 2752520 | tf_op jit(solution)/shard_map/ppermute | solution.py:201
  50.7 26.7 %collective-permute-start.8 = (bf16[8,7,64,128]{3,2,1,0:T(8,128)(2,1)}, bf16[8,7,64,128]{3,2,1,0:T(8,128)(2,1)S(1)}, u32[]{:S(2)}, u32[]{:S(2)}) collective-permute-start(bf16[8,7,64,128]{3,2,1,0:T(8,128)(2,1)} %get-tuple-element.47), channel_id=1, source_target_pairs={{0,2},{2,4},{4,6},{6,7},{7,5},{5,3},{3,1},{1,0},{8,10},{10,12},{12... | collective-permute-start | bytes 2752520 | tf_op jit(solution)/shard_map/ppermute | solution.py:201
  65.6 30.4 %collective-permute-start.15 = (bf16[8,7,64,128]{3,2,1,0:T(8,128)(2,1)}, bf16[8,7,64,128]{3,2,1,0:T(8,128)(2,1)S(1)}, u32[]{:S(2)}, u32[]{:S(2)}) collective-permute-start(bf16[8,7,64,128]{3,2,1,0:T(8,128)(2,1)} %get-tuple-element.54), channel_id=1, source_target_pairs={{0,2},{2,4},{4,6},{6,7},{7,5},{5,3},{3,1},{1,0},{8,10},{10,12},{12... | collective-permute-start | bytes 2752520 | tf_op jit(solution)/shard_map/ppermute | solution.py:201
  73.8 24.6 %collective-permute-start.19 = (bf16[8,7,64,128]{3,2,1,0:T(8,128)(2,1)S(1)}, bf16[8,7,64,128]{3,2,1,0:T(8,128)(2,1)S(1)}, u32[]{:S(2)}, u32[]{:S(2)}) collective-permute-start(bf16[8,7,64,128]{3,2,1,0:T(8,128)(2,1)S(1)} %add_convert_fusion.3), channel_id=1, source_target_pairs={{2,0},{4,2},{6,4},{7,6},{5,7},{3,5},{1,3},{0,1},{10,8},{12,10},{14... | collective-permute-start | bytes 2752520 | tf_op jit(solution)/shard_map/ppermute | solution.py:201
  75.0 41.8 %collective-permute-start.12 = (bf16[8,7,64,128]{3,2,1,0:T(8,128)(2,1)S(1)}, bf16[8,7,64,128]{3,2,1,0:T(8,128)(2,1)S(1)}, u32[]{:S(2)}, u32[]{:S(2)}) collective-permute-start(bf16[8,7,64,128]{3,2,1,0:T(8,128)(2,1)S(1)} %copy-done.18), channel_id=1, source_target_pairs={{2,0},{4,2},{6,4},{7,6},{5,7},{3,5},{1,3},{0,1},{10,8},{12,10},{14... | collective-permute-start | bytes 2752520 | tf_op jit(solution)/shard_map/ppermute | solution.py:201
  77.7 40.6 %collective-permute-start.9 = (bf16[8,7,64,128]{3,2,1,0:T(8,128)(2,1)S(1)}, bf16[8,7,64,128]{3,2,1,0:T(8,128)(2,1)S(1)}, u32[]{:S(2)}, u32[]{:S(2)}) collective-permute-start(bf16[8,7,64,128]{3,2,1,0:T(8,128)(2,1)S(1)} %add_convert_fusion.11), channel_id=1, source_target_pairs={{0,2},{2,4},{4,6},{6,7},{7,5},{5,3},{3,1},{1,0},{8,10},{10,12},{12... | collective-permute-start | bytes 2752520 | tf_op jit(solution)/shard_map/ppermute | solution.py:201
  97.5 19.3 %copy-start.9 = (bf16[8,7,64,128]{3,2,1,0:T(8,128)(2,1)S(1)}, bf16[8,7,64,128]{3,2,1,0:T(8,128)(2,1)}, u32[]{:S(2)}) copy-start(bf16[8,7,64,128]{3,2,1,0:T(8,128)(2,1)} %get-tuple-element.49) | copy-start | bytes 2752516
  97.5 37.8 %collective-permute-start.16 = (bf16[8,7,64,128]{3,2,1,0:T(8,128)(2,1)S(1)}, bf16[8,7,64,128]{3,2,1,0:T(8,128)(2,1)S(1)}, u32[]{:S(2)}, u32[]{:S(2)}) collective-permute-start(bf16[8,7,64,128]{3,2,1,0:T(8,128)(2,1)S(1)} %add_convert_fusion.5), channel_id=1, source_target_pairs={{0,2},{2,4},{4,6},{6,7},{7,5},{5,3},{3,1},{1,0},{8,10},{10,12},{12... | collective-permute-start | bytes 2752520 | tf_op jit(solution)/shard_map/ppermute | solution.py:201
  98.7 19.6 %copy-start.7 = (bf16[8,7,64,128]{3,2,1,0:T(8,128)(2,1)S(1)}, bf16[8,7,64,128]{3,2,1,0:T(8,128)(2,1)}, u32[]{:S(2)}) copy-start(bf16[8,7,64,128]{3,2,1,0:T(8,128)(2,1)} %get-tuple-element.45) | copy-start | bytes 2752516
  98.7 39.0 %collective-permute-start.20 = (bf16[8,7,64,128]{3,2,1,0:T(8,128)(2,1)S(1)}, bf16[8,7,64,128]{3,2,1,0:T(8,128)(2,1)S(1)}, u32[]{:S(2)}, u32[]{:S(2)}) collective-permute-start(bf16[8,7,64,128]{3,2,1,0:T(8,128)(2,1)S(1)} %add_convert_fusion.2), channel_id=1, source_target_pairs={{2,0},{4,2},{6,4},{7,6},{5,7},{3,5},{1,3},{0,1},{10,8},{12,10},{14... | collective-permute-start | bytes 2752520 | tf_op jit(solution)/shard_map/ppermute | solution.py:201
  117.2 39.0 %collective-permute-start.13 = (bf16[8,7,64,128]{3,2,1,0:T(8,128)(2,1)S(1)}, bf16[8,7,64,128]{3,2,1,0:T(8,128)(2,1)S(1)}, u32[]{:S(2)}, u32[]{:S(2)}) collective-permute-start(bf16[8,7,64,128]{3,2,1,0:T(8,128)(2,1)S(1)} %add_convert_fusion.8), channel_id=1, source_target_pairs={{2,0},{4,2},{6,4},{7,6},{5,7},{3,5},{1,3},{0,1},{10,8},{12,10},{14... | collective-permute-start | bytes 2752520 | tf_op jit(solution)/shard_map/ppermute | solution.py:201
  118.7 39.0 %collective-permute-start.10 = (bf16[8,7,64,128]{3,2,1,0:T(8,128)(2,1)S(1)}, bf16[8,7,64,128]{3,2,1,0:T(8,128)(2,1)S(1)}, u32[]{:S(2)}, u32[]{:S(2)}) collective-permute-start(bf16[8,7,64,128]{3,2,1,0:T(8,128)(2,1)S(1)} %add_convert_fusion.10), channel_id=1, source_target_pairs={{0,2},{2,4},{4,6},{6,7},{7,5},{5,3},{3,1},{1,0},{8,10},{10,12},{12... | collective-permute-start | bytes 2752520 | tf_op jit(solution)/shard_map/ppermute | solution.py:201
  136.8 19.3 %copy-start.10 = (bf16[8,7,64,128]{3,2,1,0:T(8,128)(2,1)S(1)}, bf16[8,7,64,128]{3,2,1,0:T(8,128)(2,1)}, u32[]{:S(2)}) copy-start(bf16[8,7,64,128]{3,2,1,0:T(8,128)(2,1)} %get-tuple-element.48) | copy-start | bytes 2752516
  136.8 37.8 %collective-permute-start.17 = (bf16[8,7,64,128]{3,2,1,0:T(8,128)(2,1)S(1)}, bf16[8,7,64,128]{3,2,1,0:T(8,128)(2,1)S(1)}, u32[]{:S(2)}, u32[]{:S(2)}) collective-permute-start(bf16[8,7,64,128]{3,2,1,0:T(8,128)(2,1)S(1)} %add_convert_fusion.4), channel_id=1, source_target_pairs={{0,2},{2,4},{4,6},{6,7},{7,5},{5,3},{3,1},{1,0},{8,10},{10,12},{12... | collective-permute-start | bytes 2752520 | tf_op jit(solution)/shard_map/ppermute | solution.py:201
  138.0 19.6 %copy-start.8 = (bf16[8,7,64,128]{3,2,1,0:T(8,128)(2,1)S(1)}, bf16[8,7,64,128]{3,2,1,0:T(8,128)(2,1)}, u32[]{:S(2)}) copy-start(bf16[8,7,64,128]{3,2,1,0:T(8,128)(2,1)} %get-tuple-element.44) | copy-start | bytes 2752516
  138.1 37.8 %collective-permute-start.21 = (bf16[8,7,64,128]{3,2,1,0:T(8,128)(2,1)S(1)}, bf16[8,7,64,128]{3,2,1,0:T(8,128)(2,1)S(1)}, u32[]{:S(2)}, u32[]{:S(2)}) collective-permute-start(bf16[8,7,64,128]{3,2,1,0:T(8,128)(2,1)S(1)} %add_convert_fusion.1), channel_id=1, source_target_pairs={{2,0},{4,2},{6,4},{7,6},{5,7},{3,5},{1,3},{0,1},{10,8},{12,10},{14... | collective-permute-start | bytes 2752520 | tf_op jit(solution)/shard_map/ppermute | solution.py:201
  156.5 36.5 %collective-permute-start.14 = (bf16[8,7,64,128]{3,2,1,0:T(8,128)(2,1)S(1)}, bf16[8,7,64,128]{3,2,1,0:T(8,128)(2,1)S(1)}, u32[]{:S(2)}, u32[]{:S(2)}) collective-permute-start(bf16[8,7,64,128]{3,2,1,0:T(8,128)(2,1)S(1)} %add_convert_fusion.7), channel_id=1, source_target_pairs={{2,0},{4,2},{6,4},{7,6},{5,7},{3,5},{1,3},{0,1},{10,8},{12,10},{14... | collective-permute-start | bytes 2752520 | tf_op jit(solution)/shard_map/ppermute | solution.py:201
  158.0 35.0 %collective-permute-start.11 = (bf16[8,7,64,128]{3,2,1,0:T(8,128)(2,1)S(1)}, bf16[8,7,64,128]{3,2,1,0:T(8,128)(2,1)S(1)}, u32[]{:S(2)}, u32[]{:S(2)}) collective-permute-start(bf16[8,7,64,128]{3,2,1,0:T(8,128)(2,1)S(1)} %add_convert_fusion.9), channel_id=1, source_target_pairs={{0,2},{2,4},{4,6},{6,7},{7,5},{5,3},{3,1},{1,0},{8,10},{10,12},{12... | collective-permute-start | bytes 2752520 | tf_op jit(solution)/shard_map/ppermute | solution.py:201
  175.8 17.2 %copy-start.6 = (bf16[8,7,64,128]{3,2,1,0:T(8,128)(2,1)S(1)}, bf16[8,7,64,128]{3,2,1,0:T(8,128)(2,1)}, u32[]{:S(2)}) copy-start(bf16[8,7,64,128]{3,2,1,0:T(8,128)(2,1)} %get-tuple-element.43) | copy-start | bytes 2752516
  (9 other events, 67.7 us)

commit v4 on v3

--- a/solution.py
+++ b/solution.py
@@ -8,7 +8,7 @@
 from jax.sharding import PartitionSpec as P
 
 KC = 7
-FACES = 6
+GROUP = 2
 VMEM_BYTES = 56 * 1024 * 1024
 
 
@@ -38,7 +38,7 @@
             [lax.ppermute(p_blocks, "dev", forward)],
         )
     elems = p_blocks.shape[0]
-    cuts = (0, 3 * elems // 8, 3 * elems // 4, elems)
+    cuts = (0, 17 * elems // 32, 25 * elems // 32, elems)
     swap = [(i, i ^ 1) for i in range(count)]
     relay = [(i, i + 2) for i in range(0, count - 2, 2)] + [(i, i - 2) for i in range(3, count, 2)]
     straight = [(i, i - 1) for i in range(2, count, 2)] + [(i, i + 1) for i in range(1, count - 1, 2)]
@@ -58,99 +58,131 @@
 def chunk_kernel(distance, cuts, places, owner, agg, near, slot, a_ref, own, *refs):
     pieces = len(cuts) - 1
     first, second, (left, right) = refs[:pieces], refs[pieces : 2 * pieces], refs[2 * pieces : 2 * pieces + 2]
-    low, high, acc, a_buf, p_buf, t_buf, picked, sems = refs[2 * pieces + 2 :]
-    elems, count_dev = owner.shape[0], places.shape[0]
+    low, high, acc, a_buf, p_buf, t_buf, halves, picked, sems, out_sems = refs[2 * pieces + 2 :]
+    elems, count_dev = owner.shape[1], places.shape[0]
     aggs, _, half, width = low.shape
     depth = a_buf.shape[0]
     me = lax.axis_index("dev")
     odd = lax.rem(me, 2) if pieces > 1 else 0
-
     target = lax.rem(places[me] + distance, count_dev)
 
     def pick(e, count):
-        hit = places[owner[e, 0]] == target
-
-        @pl.when(hit)
-        def _():
-            picked[count] = e
-
-        return count + hit.astype(jnp.int32)
-
-    count = lax.fori_loop(0, elems, pick, jnp.int32(0))
+        picked[count] = e
+        return count + (places[owner[0, e]] == target).astype(jnp.int32)
+
+    count = lax.fori_loop(0, elems, pick, jnp.int32(0), unroll=4)
 
     def fetch(source, buf, f):
         return pltpu.make_async_copy(source, p_buf.at[buf, f], sems.at[buf, f])
+
+    def fetch_a(e, buf):
+        return pltpu.make_async_copy(a_ref.at[e], a_buf.at[buf], sems.at[buf, KC])
 
     def start(i):
         @pl.when(i < count)
         def _():
             e, buf = picked[i], lax.rem(i, depth)
-            pltpu.make_async_copy(a_ref.at[e], a_buf.at[buf], sems.at[buf, KC]).start()
+            fetch_a(e, buf).start()
             fetch(own.at[e], buf, 0).start()
             for f, source in ((1, own), (2, own), (5, left), (6, right)):
-                fetch(source.at[near[e, f - 1]], buf, f).start()
+                fetch(source.at[near[f - 1, e]], buf, f).start()
             for f, parts in ((4 - odd, first), (3 + odd, second)):
-                n = near[e, f - 1]
+                n = near[f - 1, e]
                 for part, at, end in zip(parts, cuts, cuts[1:]):
 
                     @pl.when((n >= at) & (n < end))
                     def _():
                         fetch(part.at[n - at], buf, f).start()
 
-    for i in range(depth - 1):
+    for i in range(depth - GROUP):
         start(i)
     acc[...] = jnp.zeros_like(acc)
 
-    def element(i, carry):
-        start(i + depth - 1)
-        e, buf = picked[i], lax.rem(i, depth)
-        pltpu.make_async_copy(a_ref.at[e], a_buf.at[buf], sems.at[buf, KC]).wait()
-        for f in range(KC):
-            fetch(own.at[e], buf, f).wait()
-        for f in range(KC):
-            t_buf[:, f * width : (f + 1) * width] = jnp.dot(
-                a_buf[buf, f], p_buf[buf, f], preferred_element_type=jnp.float32
-            ).astype(jnp.bfloat16)
-        weighted = lax.dot_general(
-            p_buf[buf, 0], t_buf[...], (((0,), (0,)), ((), ())), preferred_element_type=jnp.float32
-        )
-        a = agg[e]
-        for f in range(KC):
-            row = a * KC + slot[e, f]
-            acc[row] = acc[row] + weighted[:, f * width : (f + 1) * width]
+    def group(g, carry):
+        for u in range(GROUP):
+            start(g * GROUP + u + depth - GROUP)
+        for u in range(GROUP):
+            buf = lax.rem(g * GROUP + u, depth)
+
+            @pl.when(g * GROUP + u < count)
+            def _():
+                fetch_a(0, buf).wait()
+                for f in range(KC):
+                    fetch(own.at[0], buf, f).wait()
+
+        for u in range(GROUP):
+            buf = lax.rem(g * GROUP + u, depth)
+            for f in range(KC):
+                t_buf[u, :, f * width : (f + 1) * width] = jnp.dot(
+                    a_buf[buf, f], p_buf[buf, f], preferred_element_type=jnp.float32
+                ).astype(jnp.bfloat16)
+        weighted = [
+            lax.dot_general(
+                p_buf[lax.rem(g * GROUP + u, depth), 0], t_buf[u], (((0,), (0,)), ((), ())),
+                preferred_element_type=jnp.float32,
+            )
+            for u in range(GROUP)
+        ]
+        for u in range(GROUP):
+            i = g * GROUP + u
+
+            @pl.when(i < count)
+            def _():
+                e = picked[i]
+                a = agg[e]
+                for f in range(KC):
+                    row = a * KC + slot[f, e]
+                    acc[row] = acc[row] + weighted[u][:, f * width : (f + 1) * width]
+
         return carry
 
-    lax.fori_loop(0, count, element, 0)
+    lax.fori_loop(0, (count + GROUP - 1) // GROUP, group, 0)
+
+    def moves(r):
+        return [
+            pltpu.make_async_copy(halves.at[h, r], out.at[r], out_sems.at[h, r])
+            for h, out in ((0, low), (1, high))
+        ]
 
     def store(r, carry):
         for s in range(KC):
             block = acc[r * KC + s].astype(jnp.bfloat16)
-            low[r, s] = block[:half]
-            high[r, s] = block[half:]
+            halves[0, r, s] = block[:half]
+            halves[1, r, s] = block[half:]
+        for move in moves(r):
+            move.start()
         return carry
 
     lax.fori_loop(0, aggs, store, 0)
+
+    def finish(r, carry):
+        for move in moves(r):
+            move.wait()
+        return carry
+
+    lax.fori_loop(0, aggs, finish, 0)
 
 
 def chunk(distance, aggs, cuts, tables, a_blocks, blocks):
     elems, _, width, _ = a_blocks.shape
     out = jax.ShapeDtypeStruct((aggs, KC, width // 2, width), jnp.bfloat16)
     smem = pl.BlockSpec(memory_space=pltpu.SMEM)
-    vmem = pl.BlockSpec(memory_space=pltpu.VMEM)
     hbm = pl.BlockSpec(memory_space=pl.ANY)
-    depth = 4
+    depth = 3 * GROUP
     return pl.pallas_call(
         functools.partial(chunk_kernel, distance, cuts),
         out_shape=(out, out),
-        in_specs=[smem] * 5 + [hbm] * (1 + len(blocks)),
-        out_specs=(vmem, vmem),
+        in_specs=[smem] * len(tables) + [hbm] * (1 + len(blocks)),
+        out_specs=(hbm, hbm),
         scratch_shapes=[
             pltpu.VMEM((aggs * KC, width, width), jnp.float32),
             pltpu.VMEM((depth, KC, width, width), jnp.bfloat16),
             pltpu.VMEM((depth, KC, width, width), jnp.bfloat16),
-            pltpu.VMEM((width, KC * width), jnp.bfloat16),
-            pltpu.SMEM((elems,), jnp.int32),
+            pltpu.VMEM((GROUP, width, KC * width), jnp.bfloat16),
+            pltpu.VMEM((2, aggs, KC, width // 2, width), jnp.bfloat16),
+            pltpu.SMEM((elems + 1,), jnp.int32),
             pltpu.SemaphoreType.DMA((depth, KC + 1)),
+            pltpu.SemaphoreType.DMA((2, aggs)),
         ],
         compiler_params=pltpu.CompilerParams(vmem_limit_bytes=VMEM_BYTES),
         cost_estimate=pl.CostEstimate(
@@ -170,7 +202,7 @@
 
     order = ring_order(count)
     places = jnp.array([order.index(d) for d in range(count)], jnp.int32)
-    tables = (places, owner, agg_local, neighbours, coarse_slot)
+    tables = (places, owner.T, agg_local, neighbours.T, coarse_slot.T)
 
     cuts, first, second = halo_dev(p_blocks, count)
     size = lax.axis_size("grp")

time: 196 us -> 188 us (0.959)
  Pallas kernels: 50.5 us -> 42.6 us
    pallas_call x8, Pallas kernels: 50.5 us -> 42.6 us  [chunk(): pl.pallas_call(functools.partial(chunk_kernel, distance, cuts), out_shape...]
    ppermute x14, waiting for transfers between devices: 72.7 us -> 76.9 us  [on_device(): got[sign, n] = lax.ppermute(terms[0] if n < 2 else add(*terms), 'dev', perm)]
    ppermute x3, waiting for transfers between devices: 16.9 us -> 14.1 us  [halo_dev(): first.append(lax.ppermute(piece, 'dev', swap))]
    ppermute x14, starting transfers between devices: 19.3 us -> 17.3 us  [on_device(): got[sign, n] = lax.ppermute(terms[0] if n < 2 else add(*terms), 'dev', perm)]
  transfers between devices with their start and end apart: 22 -> 22, of which waited for: 11 -> 12; matrix products, arithmetic and copies ran while one was open for 6% -> 5% of each run, Pallas kernels for 22% -> 20%
where the time goes in v4:
time: 188 us; the launch traced here: 187 us
  waiting for transfers between devices  91 us (48%)
  Pallas kernels  42.6 us (23%)
  starting transfers between devices  38.6 us (21%)
  other arithmetic  9.38 us (5%)
  local copies, waits for them, and re-layouts  4.69 us (2%)
    ppermute x14, waiting for transfers between devices, on_device(): got[sign, n] = lax.ppermute(terms[0] if n < 2 else add(*terms), 'dev', perm)  76.9 us
    pallas_call x8, Pallas kernels, chunk(): pl.pallas_call(functools.partial(chunk_kernel, distance, cuts), out_shape...  42.6 us
    ppermute x14, starting transfers between devices, on_device(): got[sign, n] = lax.ppermute(terms[0] if n < 2 else add(*terms), 'dev', perm)  17.3 us
    ppermute x3, waiting for transfers between devices, halo_dev(): first.append(lax.ppermute(piece, 'dev', swap))  14.1 us
    ppermute x2, starting transfers between devices, halo_dev(): second.append(lax.ppermute(first[-1], 'dev', relay))  9.54 us
    ppermute x3, starting transfers between devices, halo_dev(): first.append(lax.ppermute(piece, 'dev', swap))  8.29 us
    convert_element_type x12, other arithmetic, add(): return sum((t.astype(jnp.float32) for t in terms)).astype(jnp.bfloat16)  7.99 us
  transfers between devices with their start and end apart: 22, of which 12 were waited for; matrix products, arithmetic and copies ran while one was open for 5% of the time, Pallas kernels for 20%

profile of v4, /device:TPU:0, one launch (start us, length us, event | category | flops | bytes accessed | tf_op | source)
XLA Modules:
  0.0 186.7 jit_solution(4909259491747310036)
XLA Ops:
  1.1 3.0 %collective-permute-start = (bf16[17,128,128]{2,1,0:T(8,128)(2,1)S(1)}, bf16[17,128,128]{2,1,0:T(8,128)(2,1)S(1)}, u32[]{:S(2)}, u32[]{:S(2)}) collective-permute-start(bf16[17,128,128]{2,1,0:T(8,128)(2,1)S(1)} %slice.9), channel_id=1, source_target_pairs={{0,1},{1,0},{2,3},{3,2},{4,5},{5,4},{6,7},{7,6},{8,9},{9,8},{10,11... | collective-permute-start | bytes 1671176 | tf_op jit(solution)/shard_map/ppermute | solution.py:50
  4.1 1.5 collective-permute-start.6
  7.9 8.8 %collective-permute-done.refs_0_ = bf16[17,128,128]{2,1,0:T(8,128)(2,1)S(1)} collective-permute-done((bf16[17,128,128]{2,1,0:T(8,128)(2,1)S(1)}, bf16[17,128,128]{2,1,0:T(8,128)(2,1)S(1)}, u32[]{:S(2)}, u32[]{:S(2)}) %collective-permute-start) | collective-permute-done | bytes 557088 | tf_op jit(solution)/shard_map/ppermute | solution.py:50
  16.7 1.7 collective-permute-start.1
  18.5 3.5 %collective-permute-start.3 = (bf16[17,128,128]{2,1,0:T(8,128)(2,1)S(1)}, bf16[17,128,128]{2,1,0:T(8,128)(2,1)S(1)}, u32[]{:S(2)}, u32[]{:S(2)}) collective-permute-start(bf16[17,128,128]{2,1,0:T(8,128)(2,1)S(1)} %collective-permute-done.refs_0_), channel_id=1, source_target_pairs={{0,2},{2,4},{4,6},{3,1},{5,3},{7,5},{8,10},{10,12},{12,14},{11,9},... | collective-permute-start | bytes 1671176 | tf_op jit(solution)/shard_map/ppermute | solution.py:52
  24.9 6.0 %collective-permute-start.4 = (bf16[8,128,128]{2,1,0:T(8,128)(2,1)S(1)}, bf16[8,128,128]{2,1,0:T(8,128)(2,1)S(1)}, u32[]{:S(2)}, u32[]{:S(2)}) collective-permute-start(bf16[8,128,128]{2,1,0:T(8,128)(2,1)S(1)} %collective-permute-done.1.refs_1_), channel_id=1, source_target_pairs={{0,2},{2,4},{4,6},{3,1},{5,3},{7,5},{8,10},{10,12},{12,14},{11,9},... | collective-permute-start | bytes 786440 | tf_op jit(solution)/shard_map/ppermute | solution.py:52
  31.0 3.5 %collective-permute-start.2 = (bf16[7,128,128]{2,1,0:T(8,128)(2,1)S(1)}, bf16[7,128,128]{2,1,0:T(8,128)(2,1)S(1)}, u32[]{:S(2)}, u32[]{:S(2)}) collective-permute-start(bf16[7,128,128]{2,1,0:T(8,128)(2,1)S(1)} %slice.11), channel_id=1, source_target_pairs={{0,1},{1,0},{2,3},{3,2},{4,5},{5,4},{6,7},{7,6},{8,9},{9,8},{10,11... | collective-permute-start | bytes 688136 | tf_op jit(solution)/shard_map/ppermute | solution.py:50
  34.5 4.0 %collective-permute-done.2.refs_2_ = bf16[7,128,128]{2,1,0:T(8,128)(2,1)S(1)} collective-permute-done((bf16[7,128,128]{2,1,0:T(8,128)(2,1)S(1)}, bf16[7,128,128]{2,1,0:T(8,128)(2,1)S(1)}, u32[]{:S(2)}, u32[]{:S(2)}) %collective-permute-start.2) | collective-permute-done | bytes 229408 | tf_op jit(solution)/shard_map/ppermute | solution.py:50
  40.2 5.1 %shard_map.77 = (bf16[8,7,64,128]{3,2,1,0:T(8,128)(2,1)}, bf16[8,7,64,128]{3,2,1,0:T(8,128)(2,1)}) custom-call(s32[8]{0:T(128)} %constant.2.clone.places, s32[1,32]{1,0:T(1,128)} %bitcast.19, s32[32]{0:T(128)} %agg.15, s32[6,32]{1,0:T(8,128)} %bitcast.3, s32[7,32]{1,0:T(8,128)} %bitcast.11, bf16[32,7,128,128]{3,2,1,0:T(8,128)(2,1)} %a_ref.15, ...), custom_call_target="tpu_custom_call" | custom-call | flops 234881024 | bytes 12582912 | tf_op jit(solution)/shard_map/pallas_call | solution.py:172
  46.8 2.3 %collective-permute-start.8 = (bf16[8,7,64,128]{3,2,1,0:T(8,128)(2,1)}, bf16[8,7,64,128]{3,2,1,0:T(8,128)(2,1)S(1)}, u32[]{:S(2)}, u32[]{:S(2)}) collective-permute-start(bf16[8,7,64,128]{3,2,1,0:T(8,128)(2,1)} %get-tuple-element.47), channel_id=1, source_target_pairs={{0,2},{2,4},{4,6},{6,7},{7,5},{5,3},{3,1},{1,0},{8,10},{10,12},{12... | collective-permute-start | bytes 2752520 | tf_op jit(solution)/shard_map/ppermute | solution.py:233
  49.2 6.6 %shard_map.80 = (bf16[8,7,64,128]{3,2,1,0:T(8,128)(2,1)}, bf16[8,7,64,128]{3,2,1,0:T(8,128)(2,1)}) custom-call(s32[8]{0:T(128)} %constant.2.clone.places, s32[1,32]{1,0:T(1,128)} %bitcast.20, s32[32]{0:T(128)} %agg.15, s32[6,32]{1,0:T(8,128)} %bitcast.4, s32[7,32]{1,0:T(8,128)} %bitcast.12, bf16[32,7,128,128]{3,2,1,0:T(8,128)(2,1)} %a_ref.15, ...), custom_call_target="tpu_custom_call" | custom-call | flops 234881024 | bytes 12582912 | tf_op jit(solution)/shard_map/pallas_call | solution.py:172
  55.8 5.3 %shard_map.76 = (bf16[8,7,64,128]{3,2,1,0:T(8,128)(2,1)}, bf16[8,7,64,128]{3,2,1,0:T(8,128)(2,1)}) custom-call(s32[8]{0:T(128)} %constant.2.clone.places, s32[1,32]{1,0:T(1,128)} %bitcast.21, s32[32]{0:T(128)} %agg.15, s32[6,32]{1,0:T(8,128)} %bitcast.5, s32[7,32]{1,0:T(8,128)} %bitcast.13, bf16[32,7,128,128]{3,2,1,0:T(8,128)(2,1)} %a_ref.15, ...), custom_call_target="tpu_custom_call" | custom-call | flops 234881024 | bytes 12582912 | tf_op jit(solution)/shard_map/pallas_call | solution.py:172
  61.8 5.6 %collective-permute-done.18 = bf16[8,7,64,128]{3,2,1,0:T(8,128)(2,1)S(1)} collective-permute-done((bf16[8,7,64,128]{3,2,1,0:T(8,128)(2,1)}, bf16[8,7,64,128]{3,2,1,0:T(8,128)(2,1)S(1)}, u32[]{:S(2)}, u32[]{:S(2)}) %collective-permute-start.18) | collective-permute-done | bytes 917536 | tf_op jit(solution)/shard_map/ppermute | solution.py:233
  70.7 2.4 %collective-permute-start.9 = (bf16[8,7,64,128]{3,2,1,0:T(8,128)(2,1)S(1)}, bf16[8,7,64,128]{3,2,1,0:T(8,128)(2,1)S(1)}, u32[]{:S(2)}, u32[]{:S(2)}) collective-permute-start(bf16[8,7,64,128]{3,2,1,0:T(8,128)(2,1)S(1)} %add_convert_fusion.11), channel_id=1, source_target_pairs={{0,2},{2,4},{4,6},{6,7},{7,5},{5,3},{3,1},{1,0},{8,10},{10,12},{12... | collective-permute-start | bytes 2752520 | tf_op jit(solution)/shard_map/ppermute | solution.py:233
  73.1 5.3 %shard_map.79 = (bf16[8,7,64,128]{3,2,1,0:T(8,128)(2,1)}, bf16[8,7,64,128]{3,2,1,0:T(8,128)(2,1)}) custom-call(s32[8]{0:T(128)} %constant.2.clone.places, s32[1,32]{1,0:T(1,128)} %bitcast.22, s32[32]{0:T(128)} %agg.15, s32[6,32]{1,0:T(8,128)} %bitcast.6, s32[7,32]{1,0:T(8,128)} %bitcast.14, bf16[32,7,128,128]{3,2,1,0:T(8,128)(2,1)} %a_ref.15, ...), custom_call_target="tpu_custom_call" | custom-call | flops 234881024 | bytes 12582912 | tf_op jit(solution)/shard_map/pallas_call | solution.py:172
  78.4 4.6 %shard_map.75 = (bf16[8,7,64,128]{3,2,1,0:T(8,128)(2,1)}, bf16[8,7,64,128]{3,2,1,0:T(8,128)(2,1)}) custom-call(s32[8]{0:T(128)} %constant.2.clone.places, s32[1,32]{1,0:T(1,128)} %bitcast.23, s32[32]{0:T(128)} %agg.15, s32[6,32]{1,0:T(8,128)} %bitcast.7, s32[7,32]{1,0:T(8,128)} %bitcast.15, bf16[32,7,128,128]{3,2,1,0:T(8,128)(2,1)} %a_ref.15, ...), custom_call_target="tpu_custom_call" | custom-call | flops 234881024 | bytes 12582912 | tf_op jit(solution)/shard_map/pallas_call | solution.py:172
  82.9 7.1 %collective-permute-done.15 = bf16[8,7,64,128]{3,2,1,0:T(8,128)(2,1)S(1)} collective-permute-done((bf16[8,7,64,128]{3,2,1,0:T(8,128)(2,1)}, bf16[8,7,64,128]{3,2,1,0:T(8,128)(2,1)S(1)}, u32[]{:S(2)}, u32[]{:S(2)}) %collective-permute-start.15) | collective-permute-done | bytes 917536 | tf_op jit(solution)/shard_map/ppermute | solution.py:233
  90.0 1.5 add_convert_fusion.5
  91.5 2.4 %collective-permute-start.16 = (bf16[8,7,64,128]{3,2,1,0:T(8,128)(2,1)S(1)}, bf16[8,7,64,128]{3,2,1,0:T(8,128)(2,1)S(1)}, u32[]{:S(2)}, u32[]{:S(2)}) collective-permute-start(bf16[8,7,64,128]{3,2,1,0:T(8,128)(2,1)S(1)} %add_convert_fusion.5), channel_id=1, source_target_pairs={{0,2},{2,4},{4,6},{6,7},{7,5},{5,3},{3,1},{1,0},{8,10},{10,12},{12... | collective-permute-start | bytes 2752520 | tf_op jit(solution)/shard_map/ppermute | solution.py:233
  94.3 16.4 %collective-permute-done.12 = bf16[8,7,64,128]{3,2,1,0:T(8,128)(2,1)S(1)} collective-permute-done((bf16[8,7,64,128]{3,2,1,0:T(8,128)(2,1)S(1)}, bf16[8,7,64,128]{3,2,1,0:T(8,128)(2,1)S(1)}, u32[]{:S(2)}, u32[]{:S(2)}) %collective-permute-start.12) | collective-permute-done | bytes 917536 | tf_op jit(solution)/shard_map/ppermute | solution.py:233
  111.5 2.1 %collective-permute-start.10 = (bf16[8,7,64,128]{3,2,1,0:T(8,128)(2,1)S(1)}, bf16[8,7,64,128]{3,2,1,0:T(8,128)(2,1)S(1)}, u32[]{:S(2)}, u32[]{:S(2)}) collective-permute-start(bf16[8,7,64,128]{3,2,1,0:T(8,128)(2,1)S(1)} %add_convert_fusion.10), channel_id=1, source_target_pairs={{0,2},{2,4},{4,6},{6,7},{7,5},{5,3},{3,1},{1,0},{8,10},{10,12},{12... | collective-permute-start | bytes 2752520 | tf_op jit(solution)/shard_map/ppermute | solution.py:233
  113.6 5.9 %shard_map.78 = (bf16[8,7,64,128]{3,2,1,0:T(8,128)(2,1)}, bf16[8,7,64,128]{3,2,1,0:T(8,128)(2,1)}) custom-call(s32[8]{0:T(128)} %constant.2.clone.places, s32[1,32]{1,0:T(1,128)} %bitcast.24, s32[32]{0:T(128)} %agg.15, s32[6,32]{1,0:T(8,128)} %bitcast.8, s32[7,32]{1,0:T(8,128)} %bitcast.16, bf16[32,7,128,128]{3,2,1,0:T(8,128)(2,1)} %a_ref.15, ...), custom_call_target="tpu_custom_call" | custom-call | flops 234881024 | bytes 12582912 | tf_op jit(solution)/shard_map/pallas_call | solution.py:172
  119.5 4.6 %shard_map.74 = (bf16[8,7,64,128]{3,2,1,0:T(8,128)(2,1)}, bf16[8,7,64,128]{3,2,1,0:T(8,128)(2,1)}) custom-call(s32[8]{0:T(128)} %constant.2.clone.places, s32[1,32]{1,0:T(1,128)} %bitcast.25, s32[32]{0:T(128)} %agg.15, s32[6,32]{1,0:T(8,128)} %bitcast.9, s32[7,32]{1,0:T(8,128)} %bitcast.17, bf16[32,7,128,128]{3,2,1,0:T(8,128)(2,1)} %a_ref.15, ...), custom_call_target="tpu_custom_call" | custom-call | flops 234881024 | bytes 12582912 | tf_op jit(solution)/shard_map/pallas_call | solution.py:172
  124.1 5.3 %collective-permute-done.16 = bf16[8,7,64,128]{3,2,1,0:T(8,128)(2,1)S(1)} collective-permute-done((bf16[8,7,64,128]{3,2,1,0:T(8,128)(2,1)S(1)}, bf16[8,7,64,128]{3,2,1,0:T(8,128)(2,1)S(1)}, u32[]{:S(2)}, u32[]{:S(2)}) %collective-permute-start.16) | collective-permute-done | bytes 917536 | tf_op jit(solution)/shard_map/ppermute | solution.py:233
  129.3 1.5 add_convert_fusion.4
  130.9 2.4 %collective-permute-start.17 = (bf16[8,7,64,128]{3,2,1,0:T(8,128)(2,1)S(1)}, bf16[8,7,64,128]{3,2,1,0:T(8,128)(2,1)S(1)}, u32[]{:S(2)}, u32[]{:S(2)}) collective-permute-start(bf16[8,7,64,128]{3,2,1,0:T(8,128)(2,1)S(1)} %add_convert_fusion.4), channel_id=1, source_target_pairs={{0,2},{2,4},{4,6},{6,7},{7,5},{5,3},{3,1},{1,0},{8,10},{10,12},{12... | collective-permute-start | bytes 2752520 | tf_op jit(solution)/shard_map/ppermute | solution.py:233
  133.7 16.4 %collective-permute-done.13 = bf16[8,7,64,128]{3,2,1,0:T(8,128)(2,1)S(1)} collective-permute-done((bf16[8,7,64,128]{3,2,1,0:T(8,128)(2,1)S(1)}, bf16[8,7,64,128]{3,2,1,0:T(8,128)(2,1)S(1)}, u32[]{:S(2)}, u32[]{:S(2)}) %collective-permute-start.13) | collective-permute-done | bytes 917536 | tf_op jit(solution)/shard_map/ppermute | solution.py:233
  150.8 2.1 %collective-permute-start.11 = (bf16[8,7,64,128]{3,2,1,0:T(8,128)(2,1)S(1)}, bf16[8,7,64,128]{3,2,1,0:T(8,128)(2,1)S(1)}, u32[]{:S(2)}, u32[]{:S(2)}) collective-permute-start(bf16[8,7,64,128]{3,2,1,0:T(8,128)(2,1)S(1)} %add_convert_fusion.9), channel_id=1, source_target_pairs={{0,2},{2,4},{4,6},{6,7},{7,5},{5,3},{3,1},{1,0},{8,10},{10,12},{12... | collective-permute-start | bytes 2752520 | tf_op jit(solution)/shard_map/ppermute | solution.py:233
  152.9 5.2 %shard_map.73 = (bf16[8,7,64,128]{3,2,1,0:T(8,128)(2,1)}, bf16[8,7,64,128]{3,2,1,0:T(8,128)(2,1)}) custom-call(s32[8]{0:T(128)} %constant.2.clone.places, s32[1,32]{1,0:T(1,128)} %bitcast.26, s32[32]{0:T(128)} %agg.15, s32[6,32]{1,0:T(8,128)} %bitcast.10, s32[7,32]{1,0:T(8,128)} %bitcast.18, bf16[32,7,128,128]{3,2,1,0:T(8,128)(2,1)} %a_ref.15, ...), custom_call_target="tpu_custom_call" | custom-call | flops 234881024 | bytes 12582912 | tf_op jit(solution)/shard_map/pallas_call | solution.py:172
  158.1 10.5 %collective-permute-done.17 = bf16[8,7,64,128]{3,2,1,0:T(8,128)(2,1)S(1)} collective-permute-done((bf16[8,7,64,128]{3,2,1,0:T(8,128)(2,1)S(1)}, bf16[8,7,64,128]{3,2,1,0:T(8,128)(2,1)S(1)}, u32[]{:S(2)}, u32[]{:S(2)}) %collective-permute-start.17) | collective-permute-done | bytes 917536 | tf_op jit(solution)/shard_map/ppermute | solution.py:233
  169.7 1.7 add_convert_fusion
  171.5 13.3 %collective-permute-done.14 = bf16[8,7,64,128]{3,2,1,0:T(8,128)(2,1)S(1)} collective-permute-done((bf16[8,7,64,128]{3,2,1,0:T(8,128)(2,1)S(1)}, bf16[8,7,64,128]{3,2,1,0:T(8,128)(2,1)S(1)}, u32[]{:S(2)}, u32[]{:S(2)}) %collective-permute-start.14) | collective-permute-done | bytes 917536 | tf_op jit(solution)/shard_map/ppermute | solution.py:233
  (72 shorter events, 18.6 us)
Async XLA Ops:
  1.1 15.6 %collective-permute-start = (bf16[17,128,128]{2,1,0:T(8,128)(2,1)S(1)}, bf16[17,128,128]{2,1,0:T(8,128)(2,1)S(1)}, u32[]{:S(2)}, u32[]{:S(2)}) collective-permute-start(bf16[17,128,128]{2,1,0:T(8,128)(2,1)S(1)} %slice.9), channel_id=1, source_target_pairs={{0,1},{1,0},{2,3},{3,2},{4,5},{5,4},{6,7},{7,6},{8,9},{9,8},{10,11... | collective-permute-start | bytes 1671176 | tf_op jit(solution)/shard_map/ppermute | solution.py:50
  4.1 34.4 %collective-permute-start.6 = (bf16[32,128,128]{2,1,0:T(8,128)(2,1)}, bf16[32,128,128]{2,1,0:T(8,128)(2,1)S(1)}, u32[]{:S(2)}, u32[]{:S(2)}) collective-permute-start(bf16[32,128,128]{2,1,0:T(8,128)(2,1)} %own.7), channel_id=1, source_target_pairs={{0,8},{8,16},{16,24},{1,9},{9,17},{17,25},{2,10},{10,18},{18,26},{... | collective-permute-start | bytes 3145736 | tf_op jit(solution)/shard_map/ppermute | solution.py:211
  5.6 32.9 %collective-permute-start.7 = (bf16[32,128,128]{2,1,0:T(8,128)(2,1)}, bf16[32,128,128]{2,1,0:T(8,128)(2,1)S(1)}, u32[]{:S(2)}, u32[]{:S(2)}) collective-permute-start(bf16[32,128,128]{2,1,0:T(8,128)(2,1)} %own.7), channel_id=1, source_target_pairs={{8,0},{16,8},{24,16},{9,1},{17,9},{25,17},{10,2},{18,10},{26,18},{... | collective-permute-start | bytes 3145736 | tf_op jit(solution)/shard_map/ppermute | solution.py:211
  16.7 21.8 %copy-start.2 = (bf16[17,128,128]{2,1,0:T(8,128)(2,1)}, bf16[17,128,128]{2,1,0:T(8,128)(2,1)S(1)}, u32[]{:S(2)}) copy-start(bf16[17,128,128]{2,1,0:T(8,128)(2,1)S(1)} %collective-permute-done.refs_0_) | copy-start | bytes 1671172
  16.7 7.5 %collective-permute-start.1 = (bf16[8,128,128]{2,1,0:T(8,128)(2,1)S(1)}, bf16[8,128,128]{2,1,0:T(8,128)(2,1)S(1)}, u32[]{:S(2)}, u32[]{:S(2)}) collective-permute-start(bf16[8,128,128]{2,1,0:T(8,128)(2,1)S(1)} %slice.10), channel_id=1, source_target_pairs={{0,1},{1,0},{2,3},{3,2},{4,5},{5,4},{6,7},{7,6},{8,9},{9,8},{10,11... | collective-permute-start | bytes 786440 | tf_op jit(solution)/shard_map/ppermute | solution.py:50
  18.5 20.1 %collective-permute-start.3 = (bf16[17,128,128]{2,1,0:T(8,128)(2,1)S(1)}, bf16[17,128,128]{2,1,0:T(8,128)(2,1)S(1)}, u32[]{:S(2)}, u32[]{:S(2)}) collective-permute-start(bf16[17,128,128]{2,1,0:T(8,128)(2,1)S(1)} %collective-permute-done.refs_0_), channel_id=1, source_target_pairs={{0,2},{2,4},{4,6},{3,1},{5,3},{7,5},{8,10},{10,12},{12,14},{11,9},... | collective-permute-start | bytes 1671176 | tf_op jit(solution)/shard_map/ppermute | solution.py:52
  24.2 14.4 %copy-start.4 = (bf16[8,128,128]{2,1,0:T(8,128)(2,1)}, bf16[8,128,128]{2,1,0:T(8,128)(2,1)S(1)}, u32[]{:S(2)}) copy-start(bf16[8,128,128]{2,1,0:T(8,128)(2,1)S(1)} %collective-permute-done.1.refs_1_) | copy-start | bytes 786436
  24.2 6.7 %collective-permute-start.5 = (bf16[7,128,128]{2,1,0:T(8,128)(2,1)S(1)}, bf16[7,128,128]{2,1,0:T(8,128)(2,1)S(1)}, u32[]{:S(2)}, u32[]{:S(2)}) collective-permute-start(bf16[7,128,128]{2,1,0:T(8,128)(2,1)S(1)} %slice.11), channel_id=1, source_target_pairs={{2,1},{4,3},{6,5},{1,2},{3,4},{5,6},{10,9},{12,11},{14,13},{9,10},... | collective-permute-start | bytes 688136 | tf_op jit(solution)/shard_map/ppermute | solution.py:54
  24.9 13.6 %collective-permute-start.4 = (bf16[8,128,128]{2,1,0:T(8,128)(2,1)S(1)}, bf16[8,128,128]{2,1,0:T(8,128)(2,1)S(1)}, u32[]{:S(2)}, u32[]{:S(2)}) collective-permute-start(bf16[8,128,128]{2,1,0:T(8,128)(2,1)S(1)} %collective-permute-done.1.refs_1_), channel_id=1, source_target_pairs={{0,2},{2,4},{4,6},{3,1},{5,3},{7,5},{8,10},{10,12},{12,14},{11,9},... | collective-permute-start | bytes 786440 | tf_op jit(solution)/shard_map/ppermute | solution.py:52
  31.0 7.5 %collective-permute-start.2 = (bf16[7,128,128]{2,1,0:T(8,128)(2,1)S(1)}, bf16[7,128,128]{2,1,0:T(8,128)(2,1)S(1)}, u32[]{:S(2)}, u32[]{:S(2)}) collective-permute-start(bf16[7,128,128]{2,1,0:T(8,128)(2,1)S(1)} %slice.11), channel_id=1, source_target_pairs={{0,1},{1,0},{2,3},{3,2},{4,5},{5,4},{6,7},{7,6},{8,9},{9,8},{10,11... | collective-permute-start | bytes 688136 | tf_op jit(solution)/shard_map/ppermute | solution.py:50
  45.4 22.0 %collective-permute-start.18 = (bf16[8,7,64,128]{3,2,1,0:T(8,128)(2,1)}, bf16[8,7,64,128]{3,2,1,0:T(8,128)(2,1)S(1)}, u32[]{:S(2)}, u32[]{:S(2)}) collective-permute-start(bf16[8,7,64,128]{3,2,1,0:T(8,128)(2,1)} %get-tuple-element.58), channel_id=1, source_target_pairs={{2,0},{4,2},{6,4},{7,6},{5,7},{3,5},{1,3},{0,1},{10,8},{12,10},{14... | collective-permute-start | bytes 2752520 | tf_op jit(solution)/shard_map/ppermute | solution.py:233
  46.8 23.5 %collective-permute-start.8 = (bf16[8,7,64,128]{3,2,1,0:T(8,128)(2,1)}, bf16[8,7,64,128]{3,2,1,0:T(8,128)(2,1)S(1)}, u32[]{:S(2)}, u32[]{:S(2)}) collective-permute-start(bf16[8,7,64,128]{3,2,1,0:T(8,128)(2,1)} %get-tuple-element.47), channel_id=1, source_target_pairs={{0,2},{2,4},{4,6},{6,7},{7,5},{5,3},{3,1},{1,0},{8,10},{10,12},{12... | collective-permute-start | bytes 2752520 | tf_op jit(solution)/shard_map/ppermute | solution.py:233
  55.8 11.6 %copy-start.16 = (bf16[8,7,64,128]{3,2,1,0:T(8,128)(2,1)S(1)}, bf16[8,7,64,128]{3,2,1,0:T(8,128)(2,1)}, u32[]{:S(2)}) copy-start(bf16[8,7,64,128]{3,2,1,0:T(8,128)(2,1)} %get-tuple-element.57) | copy-start | bytes 2752516
  61.1 9.2 %copy-start.13 = (bf16[8,7,64,128]{3,2,1,0:T(8,128)(2,1)S(1)}, bf16[8,7,64,128]{3,2,1,0:T(8,128)(2,1)}, u32[]{:S(2)}) copy-start(bf16[8,7,64,128]{3,2,1,0:T(8,128)(2,1)} %get-tuple-element.46) | copy-start | bytes 2752516
  61.1 28.9 %collective-permute-start.15 = (bf16[8,7,64,128]{3,2,1,0:T(8,128)(2,1)}, bf16[8,7,64,128]{3,2,1,0:T(8,128)(2,1)S(1)}, u32[]{:S(2)}, u32[]{:S(2)}) collective-permute-start(bf16[8,7,64,128]{3,2,1,0:T(8,128)(2,1)} %get-tuple-element.54), channel_id=1, source_target_pairs={{0,2},{2,4},{4,6},{6,7},{7,5},{5,3},{3,1},{1,0},{8,10},{10,12},{12... | collective-permute-start | bytes 2752520 | tf_op jit(solution)/shard_map/ppermute | solution.py:233
  67.7 26.2 %collective-permute-start.19 = (bf16[8,7,64,128]{3,2,1,0:T(8,128)(2,1)S(1)}, bf16[8,7,64,128]{3,2,1,0:T(8,128)(2,1)S(1)}, u32[]{:S(2)}, u32[]{:S(2)}) collective-permute-start(bf16[8,7,64,128]{3,2,1,0:T(8,128)(2,1)S(1)} %add_convert_fusion.3), channel_id=1, source_target_pairs={{2,0},{4,2},{6,4},{7,6},{5,7},{3,5},{1,3},{0,1},{10,8},{12,10},{14... | collective-permute-start | bytes 2752520 | tf_op jit(solution)/shard_map/ppermute | solution.py:233
  67.8 42.9 %collective-permute-start.12 = (bf16[8,7,64,128]{3,2,1,0:T(8,128)(2,1)S(1)}, bf16[8,7,64,128]{3,2,1,0:T(8,128)(2,1)S(1)}, u32[]{:S(2)}, u32[]{:S(2)}) collective-permute-start(bf16[8,7,64,128]{3,2,1,0:T(8,128)(2,1)S(1)} %copy-done.17), channel_id=1, source_target_pairs={{2,0},{4,2},{6,4},{7,6},{5,7},{3,5},{1,3},{0,1},{10,8},{12,10},{14... | collective-permute-start | bytes 2752520 | tf_op jit(solution)/shard_map/ppermute | solution.py:233
  70.7 40.5 %collective-permute-start.9 = (bf16[8,7,64,128]{3,2,1,0:T(8,128)(2,1)S(1)}, bf16[8,7,64,128]{3,2,1,0:T(8,128)(2,1)S(1)}, u32[]{:S(2)}, u32[]{:S(2)}) collective-permute-start(bf16[8,7,64,128]{3,2,1,0:T(8,128)(2,1)S(1)} %add_convert_fusion.11), channel_id=1, source_target_pairs={{0,2},{2,4},{4,6},{6,7},{7,5},{5,3},{3,1},{1,0},{8,10},{10,12},{12... | collective-permute-start | bytes 2752520 | tf_op jit(solution)/shard_map/ppermute | solution.py:233
  82.9 11.0 %copy-start.14 = (bf16[8,7,64,128]{3,2,1,0:T(8,128)(2,1)S(1)}, bf16[8,7,64,128]{3,2,1,0:T(8,128)(2,1)}, u32[]{:S(2)}) copy-start(bf16[8,7,64,128]{3,2,1,0:T(8,128)(2,1)} %get-tuple-element.56) | copy-start | bytes 2752516
  91.5 19.2 %copy-start.11 = (bf16[8,7,64,128]{3,2,1,0:T(8,128)(2,1)S(1)}, bf16[8,7,64,128]{3,2,1,0:T(8,128)(2,1)}, u32[]{:S(2)}) copy-start(bf16[8,7,64,128]{3,2,1,0:T(8,128)(2,1)} %get-tuple-element.49) | copy-start | bytes 2752516
  91.5 37.8 %collective-permute-start.16 = (bf16[8,7,64,128]{3,2,1,0:T(8,128)(2,1)S(1)}, bf16[8,7,64,128]{3,2,1,0:T(8,128)(2,1)S(1)}, u32[]{:S(2)}, u32[]{:S(2)}) collective-permute-start(bf16[8,7,64,128]{3,2,1,0:T(8,128)(2,1)S(1)} %add_convert_fusion.5), channel_id=1, source_target_pairs={{0,2},{2,4},{4,6},{6,7},{7,5},{5,3},{3,1},{1,0},{8,10},{10,12},{12... | collective-permute-start | bytes 2752520 | tf_op jit(solution)/shard_map/ppermute | solution.py:233
  94.3 16.9 %copy-start.9 = (bf16[8,7,64,128]{3,2,1,0:T(8,128)(2,1)S(1)}, bf16[8,7,64,128]{3,2,1,0:T(8,128)(2,1)}, u32[]{:S(2)}) copy-start(bf16[8,7,64,128]{3,2,1,0:T(8,128)(2,1)} %get-tuple-element.45) | copy-start | bytes 2752516
  94.3 39.0 %collective-permute-start.20 = (bf16[8,7,64,128]{3,2,1,0:T(8,128)(2,1)S(1)}, bf16[8,7,64,128]{3,2,1,0:T(8,128)(2,1)S(1)}, u32[]{:S(2)}, u32[]{:S(2)}) collective-permute-start(bf16[8,7,64,128]{3,2,1,0:T(8,128)(2,1)S(1)} %add_convert_fusion.2), channel_id=1, source_target_pairs={{2,0},{4,2},{6,4},{7,6},{5,7},{3,5},{1,3},{0,1},{10,8},{12,10},{14... | collective-permute-start | bytes 2752520 | tf_op jit(solution)/shard_map/ppermute | solution.py:233
  111.1 39.0 %collective-permute-start.13 = (bf16[8,7,64,128]{3,2,1,0:T(8,128)(2,1)S(1)}, bf16[8,7,64,128]{3,2,1,0:T(8,128)(2,1)S(1)}, u32[]{:S(2)}, u32[]{:S(2)}) collective-permute-start(bf16[8,7,64,128]{3,2,1,0:T(8,128)(2,1)S(1)} %add_convert_fusion.8), channel_id=1, source_target_pairs={{2,0},{4,2},{6,4},{7,6},{5,7},{3,5},{1,3},{0,1},{10,8},{12,10},{14... | collective-permute-start | bytes 2752520 | tf_op jit(solution)/shard_map/ppermute | solution.py:233
  111.5 39.0 %collective-permute-start.10 = (bf16[8,7,64,128]{3,2,1,0:T(8,128)(2,1)S(1)}, bf16[8,7,64,128]{3,2,1,0:T(8,128)(2,1)S(1)}, u32[]{:S(2)}, u32[]{:S(2)}) collective-permute-start(bf16[8,7,64,128]{3,2,1,0:T(8,128)(2,1)S(1)} %add_convert_fusion.10), channel_id=1, source_target_pairs={{0,2},{2,4},{4,6},{6,7},{7,5},{5,3},{3,1},{1,0},{8,10},{10,12},{12... | collective-permute-start | bytes 2752520 | tf_op jit(solution)/shard_map/ppermute | solution.py:233
  130.9 19.2 %copy-start.12 = (bf16[8,7,64,128]{3,2,1,0:T(8,128)(2,1)S(1)}, bf16[8,7,64,128]{3,2,1,0:T(8,128)(2,1)}, u32[]{:S(2)}) copy-start(bf16[8,7,64,128]{3,2,1,0:T(8,128)(2,1)} %get-tuple-element.48) | copy-start | bytes 2752516
  130.9 37.8 %collective-permute-start.17 = (bf16[8,7,64,128]{3,2,1,0:T(8,128)(2,1)S(1)}, bf16[8,7,64,128]{3,2,1,0:T(8,128)(2,1)S(1)}, u32[]{:S(2)}, u32[]{:S(2)}) collective-permute-start(bf16[8,7,64,128]{3,2,1,0:T(8,128)(2,1)S(1)} %add_convert_fusion.4), channel_id=1, source_target_pairs={{0,2},{2,4},{4,6},{6,7},{7,5},{5,3},{3,1},{1,0},{8,10},{10,12},{12... | collective-permute-start | bytes 2752520 | tf_op jit(solution)/shard_map/ppermute | solution.py:233
  133.6 16.9 %copy-start.10 = (bf16[8,7,64,128]{3,2,1,0:T(8,128)(2,1)S(1)}, bf16[8,7,64,128]{3,2,1,0:T(8,128)(2,1)}, u32[]{:S(2)}) copy-start(bf16[8,7,64,128]{3,2,1,0:T(8,128)(2,1)} %get-tuple-element.44) | copy-start | bytes 2752516
  133.6 36.1 %collective-permute-start.21 = (bf16[8,7,64,128]{3,2,1,0:T(8,128)(2,1)S(1)}, bf16[8,7,64,128]{3,2,1,0:T(8,128)(2,1)S(1)}, u32[]{:S(2)}, u32[]{:S(2)}) collective-permute-start(bf16[8,7,64,128]{3,2,1,0:T(8,128)(2,1)S(1)} %add_convert_fusion.1), channel_id=1, source_target_pairs={{2,0},{4,2},{6,4},{7,6},{5,7},{3,5},{1,3},{0,1},{10,8},{12,10},{14... | collective-permute-start | bytes 2752520 | tf_op jit(solution)/shard_map/ppermute | solution.py:233
  150.4 34.4 %collective-permute-start.14 = (bf16[8,7,64,128]{3,2,1,0:T(8,128)(2,1)S(1)}, bf16[8,7,64,128]{3,2,1,0:T(8,128)(2,1)S(1)}, u32[]{:S(2)}, u32[]{:S(2)}) collective-permute-start(bf16[8,7,64,128]{3,2,1,0:T(8,128)(2,1)S(1)} %add_convert_fusion.7), channel_id=1, source_target_pairs={{2,0},{4,2},{6,4},{7,6},{5,7},{3,5},{1,3},{0,1},{10,8},{12,10},{14... | collective-permute-start | bytes 2752520 | tf_op jit(solution)/shard_map/ppermute | solution.py:233
  150.8 33.9 %collective-permute-start.11 = (bf16[8,7,64,128]{3,2,1,0:T(8,128)(2,1)S(1)}, bf16[8,7,64,128]{3,2,1,0:T(8,128)(2,1)S(1)}, u32[]{:S(2)}, u32[]{:S(2)}) collective-permute-start(bf16[8,7,64,128]{3,2,1,0:T(8,128)(2,1)S(1)} %add_convert_fusion.9), channel_id=1, source_target_pairs={{0,2},{2,4},{4,6},{6,7},{7,5},{5,3},{3,1},{1,0},{8,10},{10,12},{12... | collective-permute-start | bytes 2752520 | tf_op jit(solution)/shard_map/ppermute | solution.py:233
  169.7 15.1 %copy-start.8 = (bf16[8,7,64,128]{3,2,1,0:T(8,128)(2,1)S(1)}, bf16[8,7,64,128]{3,2,1,0:T(8,128)(2,1)}, u32[]{:S(2)}) copy-start(bf16[8,7,64,128]{3,2,1,0:T(8,128)(2,1)} %get-tuple-element.43) | copy-start | bytes 2752516
  (8 other events, 29.8 us)

commit v5 on v4

--- a/solution.py
+++ b/solution.py
@@ -38,7 +38,7 @@
             [lax.ppermute(p_blocks, "dev", forward)],
         )
     elems = p_blocks.shape[0]
-    cuts = (0, 17 * elems // 32, 25 * elems // 32, elems)
+    cuts = (0, 16 * elems // 32, 25 * elems // 32, elems)
     swap = [(i, i ^ 1) for i in range(count)]
     relay = [(i, i + 2) for i in range(0, count - 2, 2)] + [(i, i - 2) for i in range(3, count, 2)]
     straight = [(i, i - 1) for i in range(2, count, 2)] + [(i, i + 1) for i in range(1, count - 1, 2)]

time: 188 us -> 187 us (level)
  no operation moved by 1% of the time
where the time goes in v5:
time: 187 us
  waiting for transfers between devices  90.4 us (48%)
  Pallas kernels  42.6 us (23%)
  starting transfers between devices  39.1 us (21%)
  other arithmetic  9.38 us (5%)
  local copies, waits for them, and re-layouts  4.64 us (2%)
    ppermute x14, waiting for transfers between devices, on_device(): got[sign, n] = lax.ppermute(terms[0] if n < 2 else add(*terms), 'dev', perm)  76.3 us
    pallas_call x8, Pallas kernels, chunk(): pl.pallas_call(functools.partial(chunk_kernel, distance, cuts), out_shape...  42.6 us
    ppermute x14, starting transfers between devices, on_device(): got[sign, n] = lax.ppermute(terms[0] if n < 2 else add(*terms), 'dev', perm)  17.8 us
    ppermute x3, waiting for transfers between devices, halo_dev(): first.append(lax.ppermute(piece, 'dev', swap))  14.1 us
    ppermute x2, starting transfers between devices, halo_dev(): second.append(lax.ppermute(first[-1], 'dev', relay))  9.54 us
    ppermute x3, starting transfers between devices, halo_dev(): first.append(lax.ppermute(piece, 'dev', swap))  8.29 us
    convert_element_type x12, other arithmetic, add(): return sum((t.astype(jnp.float32) for t in terms)).astype(jnp.bfloat16)  7.99 us
  transfers between devices with their start and end apart: 22, of which 12 were waited for; matrix products, arithmetic and copies ran while one was open for 5% of the time, Pallas kernels for 20%

profile of v5, /device:TPU:0, one launch (start us, length us, event | category | flops | bytes accessed | tf_op | source)
XLA Modules:
  0.0 186.5 jit_solution(1376487653720660208)
XLA Ops:
  1.1 3.0 %collective-permute-start = (bf16[16,128,128]{2,1,0:T(8,128)(2,1)S(1)}, bf16[16,128,128]{2,1,0:T(8,128)(2,1)S(1)}, u32[]{:S(2)}, u32[]{:S(2)}) collective-permute-start(bf16[16,128,128]{2,1,0:T(8,128)(2,1)S(1)} %slice.9), channel_id=1, source_target_pairs={{0,1},{1,0},{2,3},{3,2},{4,5},{5,4},{6,7},{7,6},{8,9},{9,8},{10,11... | collective-permute-start | bytes 1572872 | tf_op jit(solution)/shard_map/ppermute | solution.py:50
  7.9 8.1 %collective-permute-done.refs_0_ = bf16[16,128,128]{2,1,0:T(8,128)(2,1)S(1)} collective-permute-done((bf16[16,128,128]{2,1,0:T(8,128)(2,1)S(1)}, bf16[16,128,128]{2,1,0:T(8,128)(2,1)S(1)}, u32[]{:S(2)}, u32[]{:S(2)}) %collective-permute-start) | collective-permute-done | bytes 524320 | tf_op jit(solution)/shard_map/ppermute | solution.py:50
  16.0 1.7 collective-permute-start.1
  17.8 3.5 %collective-permute-start.3 = (bf16[16,128,128]{2,1,0:T(8,128)(2,1)S(1)}, bf16[16,128,128]{2,1,0:T(8,128)(2,1)S(1)}, u32[]{:S(2)}, u32[]{:S(2)}) collective-permute-start(bf16[16,128,128]{2,1,0:T(8,128)(2,1)S(1)} %collective-permute-done.refs_0_), channel_id=1, source_target_pairs={{0,2},{2,4},{4,6},{3,1},{5,3},{7,5},{8,10},{10,12},{12,14},{11,9},... | collective-permute-start | bytes 1572872 | tf_op jit(solution)/shard_map/ppermute | solution.py:52
  22.2 2.0 %collective-permute-done.1.refs_1_ = bf16[9,128,128]{2,1,0:T(8,128)(2,1)S(1)} collective-permute-done((bf16[9,128,128]{2,1,0:T(8,128)(2,1)S(1)}, bf16[9,128,128]{2,1,0:T(8,128)(2,1)S(1)}, u32[]{:S(2)}, u32[]{:S(2)}) %collective-permute-start.1) | collective-permute-done | bytes 294944 | tf_op jit(solution)/shard_map/ppermute | solution.py:50
  24.9 6.0 %collective-permute-start.4 = (bf16[9,128,128]{2,1,0:T(8,128)(2,1)S(1)}, bf16[9,128,128]{2,1,0:T(8,128)(2,1)S(1)}, u32[]{:S(2)}, u32[]{:S(2)}) collective-permute-start(bf16[9,128,128]{2,1,0:T(8,128)(2,1)S(1)} %collective-permute-done.1.refs_1_), channel_id=1, source_target_pairs={{0,2},{2,4},{4,6},{3,1},{5,3},{7,5},{8,10},{10,12},{12,14},{11,9},... | collective-permute-start | bytes 884744 | tf_op jit(solution)/shard_map/ppermute | solution.py:52
  30.9 3.5 %collective-permute-start.2 = (bf16[7,128,128]{2,1,0:T(8,128)(2,1)S(1)}, bf16[7,128,128]{2,1,0:T(8,128)(2,1)S(1)}, u32[]{:S(2)}, u32[]{:S(2)}) collective-permute-start(bf16[7,128,128]{2,1,0:T(8,128)(2,1)S(1)} %slice.11), channel_id=1, source_target_pairs={{0,1},{1,0},{2,3},{3,2},{4,5},{5,4},{6,7},{7,6},{8,9},{9,8},{10,11... | collective-permute-start | bytes 688136 | tf_op jit(solution)/shard_map/ppermute | solution.py:50
  34.5 4.0 %collective-permute-done.2.refs_2_ = bf16[7,128,128]{2,1,0:T(8,128)(2,1)S(1)} collective-permute-done((bf16[7,128,128]{2,1,0:T(8,128)(2,1)S(1)}, bf16[7,128,128]{2,1,0:T(8,128)(2,1)S(1)}, u32[]{:S(2)}, u32[]{:S(2)}) %collective-permute-start.2) | collective-permute-done | bytes 229408 | tf_op jit(solution)/shard_map/ppermute | solution.py:50
  40.1 4.6 %shard_map.77 = (bf16[8,7,64,128]{3,2,1,0:T(8,128)(2,1)}, bf16[8,7,64,128]{3,2,1,0:T(8,128)(2,1)}) custom-call(s32[8]{0:T(128)} %constant.2.clone.places, s32[1,32]{1,0:T(1,128)} %bitcast.19, s32[32]{0:T(128)} %agg.15, s32[6,32]{1,0:T(8,128)} %bitcast.3, s32[7,32]{1,0:T(8,128)} %bitcast.11, bf16[32,7,128,128]{3,2,1,0:T(8,128)(2,1)} %a_ref.15, ...), custom_call_target="tpu_custom_call" | custom-call | flops 234881024 | bytes 12582912 | tf_op jit(solution)/shard_map/pallas_call | solution.py:172
  44.7 3.4 %collective-permute-start.18 = (bf16[8,7,64,128]{3,2,1,0:T(8,128)(2,1)}, bf16[8,7,64,128]{3,2,1,0:T(8,128)(2,1)S(1)}, u32[]{:S(2)}, u32[]{:S(2)}) collective-permute-start(bf16[8,7,64,128]{3,2,1,0:T(8,128)(2,1)} %get-tuple-element.58), channel_id=1, source_target_pairs={{2,0},{4,2},{6,4},{7,6},{5,7},{3,5},{1,3},{0,1},{10,8},{12,10},{14... | collective-permute-start | bytes 2752520 | tf_op jit(solution)/shard_map/ppermute | solution.py:233
  48.1 4.6 %shard_map.80 = (bf16[8,7,64,128]{3,2,1,0:T(8,128)(2,1)}, bf16[8,7,64,128]{3,2,1,0:T(8,128)(2,1)}) custom-call(s32[8]{0:T(128)} %constant.2.clone.places, s32[1,32]{1,0:T(1,128)} %bitcast.20, s32[32]{0:T(128)} %agg.15, s32[6,32]{1,0:T(8,128)} %bitcast.4, s32[7,32]{1,0:T(8,128)} %bitcast.12, bf16[32,7,128,128]{3,2,1,0:T(8,128)(2,1)} %a_ref.15, ...), custom_call_target="tpu_custom_call" | custom-call | flops 234881024 | bytes 12582912 | tf_op jit(solution)/shard_map/pallas_call | solution.py:172
  52.7 6.0 %shard_map.76 = (bf16[8,7,64,128]{3,2,1,0:T(8,128)(2,1)}, bf16[8,7,64,128]{3,2,1,0:T(8,128)(2,1)}) custom-call(s32[8]{0:T(128)} %constant.2.clone.places, s32[1,32]{1,0:T(1,128)} %bitcast.21, s32[32]{0:T(128)} %agg.15, s32[6,32]{1,0:T(8,128)} %bitcast.5, s32[7,32]{1,0:T(8,128)} %bitcast.13, bf16[32,7,128,128]{3,2,1,0:T(8,128)(2,1)} %a_ref.15, ...), custom_call_target="tpu_custom_call" | custom-call | flops 234881024 | bytes 12582912 | tf_op jit(solution)/shard_map/pallas_call | solution.py:172
  60.0 6.1 %collective-permute-done.18 = bf16[8,7,64,128]{3,2,1,0:T(8,128)(2,1)S(1)} collective-permute-done((bf16[8,7,64,128]{3,2,1,0:T(8,128)(2,1)}, bf16[8,7,64,128]{3,2,1,0:T(8,128)(2,1)S(1)}, u32[]{:S(2)}, u32[]{:S(2)}) %collective-permute-start.18) | collective-permute-done | bytes 917536 | tf_op jit(solution)/shard_map/ppermute | solution.py:233
  66.4 2.4 %collective-permute-start.19 = (bf16[8,7,64,128]{3,2,1,0:T(8,128)(2,1)S(1)}, bf16[8,7,64,128]{3,2,1,0:T(8,128)(2,1)S(1)}, u32[]{:S(2)}, u32[]{:S(2)}) collective-permute-start(bf16[8,7,64,128]{3,2,1,0:T(8,128)(2,1)S(1)} %add_convert_fusion.3), channel_id=1, source_target_pairs={{2,0},{4,2},{6,4},{7,6},{5,7},{3,5},{1,3},{0,1},{10,8},{12,10},{14... | collective-permute-start | bytes 2752520 | tf_op jit(solution)/shard_map/ppermute | solution.py:233
  72.0 5.2 %shard_map.79 = (bf16[8,7,64,128]{3,2,1,0:T(8,128)(2,1)}, bf16[8,7,64,128]{3,2,1,0:T(8,128)(2,1)}) custom-call(s32[8]{0:T(128)} %constant.2.clone.places, s32[1,32]{1,0:T(1,128)} %bitcast.22, s32[32]{0:T(128)} %agg.15, s32[6,32]{1,0:T(8,128)} %bitcast.6, s32[7,32]{1,0:T(8,128)} %bitcast.14, bf16[32,7,128,128]{3,2,1,0:T(8,128)(2,1)} %a_ref.15, ...), custom_call_target="tpu_custom_call" | custom-call | flops 234881024 | bytes 12582912 | tf_op jit(solution)/shard_map/pallas_call | solution.py:172
  77.2 5.9 %shard_map.75 = (bf16[8,7,64,128]{3,2,1,0:T(8,128)(2,1)}, bf16[8,7,64,128]{3,2,1,0:T(8,128)(2,1)}) custom-call(s32[8]{0:T(128)} %constant.2.clone.places, s32[1,32]{1,0:T(1,128)} %bitcast.23, s32[32]{0:T(128)} %agg.15, s32[6,32]{1,0:T(8,128)} %bitcast.7, s32[7,32]{1,0:T(8,128)} %bitcast.15, bf16[32,7,128,128]{3,2,1,0:T(8,128)(2,1)} %a_ref.15, ...), custom_call_target="tpu_custom_call" | custom-call | flops 234881024 | bytes 12582912 | tf_op jit(solution)/shard_map/pallas_call | solution.py:172
  83.1 8.1 %collective-permute-done.15 = bf16[8,7,64,128]{3,2,1,0:T(8,128)(2,1)S(1)} collective-permute-done((bf16[8,7,64,128]{3,2,1,0:T(8,128)(2,1)}, bf16[8,7,64,128]{3,2,1,0:T(8,128)(2,1)S(1)}, u32[]{:S(2)}, u32[]{:S(2)}) %collective-permute-start.15) | collective-permute-done | bytes 917536 | tf_op jit(solution)/shard_map/ppermute | solution.py:233
  91.3 1.5 add_convert_fusion.5
  93.2 2.0 %collective-permute-start.20 = (bf16[8,7,64,128]{3,2,1,0:T(8,128)(2,1)S(1)}, bf16[8,7,64,128]{3,2,1,0:T(8,128)(2,1)S(1)}, u32[]{:S(2)}, u32[]{:S(2)}) collective-permute-start(bf16[8,7,64,128]{3,2,1,0:T(8,128)(2,1)S(1)} %add_convert_fusion.2), channel_id=1, source_target_pairs={{2,0},{4,2},{6,4},{7,6},{5,7},{3,5},{1,3},{0,1},{10,8},{12,10},{14... | collective-permute-start | bytes 2752520 | tf_op jit(solution)/shard_map/ppermute | solution.py:233
  95.3 14.1 %collective-permute-done.12 = bf16[8,7,64,128]{3,2,1,0:T(8,128)(2,1)S(1)} collective-permute-done((bf16[8,7,64,128]{3,2,1,0:T(8,128)(2,1)S(1)}, bf16[8,7,64,128]{3,2,1,0:T(8,128)(2,1)S(1)}, u32[]{:S(2)}, u32[]{:S(2)}) %collective-permute-start.12) | collective-permute-done | bytes 917536 | tf_op jit(solution)/shard_map/ppermute | solution.py:233
  109.7 2.4 %collective-permute-start.13 = (bf16[8,7,64,128]{3,2,1,0:T(8,128)(2,1)S(1)}, bf16[8,7,64,128]{3,2,1,0:T(8,128)(2,1)S(1)}, u32[]{:S(2)}, u32[]{:S(2)}) collective-permute-start(bf16[8,7,64,128]{3,2,1,0:T(8,128)(2,1)S(1)} %add_convert_fusion.8), channel_id=1, source_target_pairs={{2,0},{4,2},{6,4},{7,6},{5,7},{3,5},{1,3},{0,1},{10,8},{12,10},{14... | collective-permute-start | bytes 2752520 | tf_op jit(solution)/shard_map/ppermute | solution.py:233
  112.6 4.6 %shard_map.78 = (bf16[8,7,64,128]{3,2,1,0:T(8,128)(2,1)}, bf16[8,7,64,128]{3,2,1,0:T(8,128)(2,1)}) custom-call(s32[8]{0:T(128)} %constant.2.clone.places, s32[1,32]{1,0:T(1,128)} %bitcast.24, s32[32]{0:T(128)} %agg.15, s32[6,32]{1,0:T(8,128)} %bitcast.8, s32[7,32]{1,0:T(8,128)} %bitcast.16, bf16[32,7,128,128]{3,2,1,0:T(8,128)(2,1)} %a_ref.15, ...), custom_call_target="tpu_custom_call" | custom-call | flops 234881024 | bytes 12582912 | tf_op jit(solution)/shard_map/pallas_call | solution.py:172
  117.2 6.7 %shard_map.74 = (bf16[8,7,64,128]{3,2,1,0:T(8,128)(2,1)}, bf16[8,7,64,128]{3,2,1,0:T(8,128)(2,1)}) custom-call(s32[8]{0:T(128)} %constant.2.clone.places, s32[1,32]{1,0:T(1,128)} %bitcast.25, s32[32]{0:T(128)} %agg.15, s32[6,32]{1,0:T(8,128)} %bitcast.9, s32[7,32]{1,0:T(8,128)} %bitcast.17, bf16[32,7,128,128]{3,2,1,0:T(8,128)(2,1)} %a_ref.15, ...), custom_call_target="tpu_custom_call" | custom-call | flops 234881024 | bytes 12582912 | tf_op jit(solution)/shard_map/pallas_call | solution.py:172
  123.9 6.7 %collective-permute-done.16 = bf16[8,7,64,128]{3,2,1,0:T(8,128)(2,1)S(1)} collective-permute-done((bf16[8,7,64,128]{3,2,1,0:T(8,128)(2,1)S(1)}, bf16[8,7,64,128]{3,2,1,0:T(8,128)(2,1)S(1)}, u32[]{:S(2)}, u32[]{:S(2)}) %collective-permute-start.16) | collective-permute-done | bytes 917536 | tf_op jit(solution)/shard_map/ppermute | solution.py:233
  132.6 2.0 %collective-permute-start.21 = (bf16[8,7,64,128]{3,2,1,0:T(8,128)(2,1)S(1)}, bf16[8,7,64,128]{3,2,1,0:T(8,128)(2,1)S(1)}, u32[]{:S(2)}, u32[]{:S(2)}) collective-permute-start(bf16[8,7,64,128]{3,2,1,0:T(8,128)(2,1)S(1)} %add_convert_fusion.1), channel_id=1, source_target_pairs={{2,0},{4,2},{6,4},{7,6},{5,7},{3,5},{1,3},{0,1},{10,8},{12,10},{14... | collective-permute-start | bytes 2752520 | tf_op jit(solution)/shard_map/ppermute | solution.py:233
  134.6 14.1 %collective-permute-done.13 = bf16[8,7,64,128]{3,2,1,0:T(8,128)(2,1)S(1)} collective-permute-done((bf16[8,7,64,128]{3,2,1,0:T(8,128)(2,1)S(1)}, bf16[8,7,64,128]{3,2,1,0:T(8,128)(2,1)S(1)}, u32[]{:S(2)}, u32[]{:S(2)}) %collective-permute-start.13) | collective-permute-done | bytes 917536 | tf_op jit(solution)/shard_map/ppermute | solution.py:233
  149.1 2.4 %collective-permute-start.14 = (bf16[8,7,64,128]{3,2,1,0:T(8,128)(2,1)S(1)}, bf16[8,7,64,128]{3,2,1,0:T(8,128)(2,1)S(1)}, u32[]{:S(2)}, u32[]{:S(2)}) collective-permute-start(bf16[8,7,64,128]{3,2,1,0:T(8,128)(2,1)S(1)} %add_convert_fusion.7), channel_id=1, source_target_pairs={{2,0},{4,2},{6,4},{7,6},{5,7},{3,5},{1,3},{0,1},{10,8},{12,10},{14... | collective-permute-start | bytes 2752520 | tf_op jit(solution)/shard_map/ppermute | solution.py:233
  151.9 5.2 %shard_map.73 = (bf16[8,7,64,128]{3,2,1,0:T(8,128)(2,1)}, bf16[8,7,64,128]{3,2,1,0:T(8,128)(2,1)}) custom-call(s32[8]{0:T(128)} %constant.2.clone.places, s32[1,32]{1,0:T(1,128)} %bitcast.26, s32[32]{0:T(128)} %agg.15, s32[6,32]{1,0:T(8,128)} %bitcast.10, s32[7,32]{1,0:T(8,128)} %bitcast.18, bf16[32,7,128,128]{3,2,1,0:T(8,128)(2,1)} %a_ref.15, ...), custom_call_target="tpu_custom_call" | custom-call | flops 234881024 | bytes 12582912 | tf_op jit(solution)/shard_map/pallas_call | solution.py:172
  157.1 12.8 %collective-permute-done.17 = bf16[8,7,64,128]{3,2,1,0:T(8,128)(2,1)S(1)} collective-permute-done((bf16[8,7,64,128]{3,2,1,0:T(8,128)(2,1)S(1)}, bf16[8,7,64,128]{3,2,1,0:T(8,128)(2,1)S(1)}, u32[]{:S(2)}, u32[]{:S(2)}) %collective-permute-start.17) | collective-permute-done | bytes 917536 | tf_op jit(solution)/shard_map/ppermute | solution.py:233
  169.9 1.7 add_convert_fusion
  171.7 10.8 %collective-permute-done.14 = bf16[8,7,64,128]{3,2,1,0:T(8,128)(2,1)S(1)} collective-permute-done((bf16[8,7,64,128]{3,2,1,0:T(8,128)(2,1)S(1)}, bf16[8,7,64,128]{3,2,1,0:T(8,128)(2,1)S(1)}, u32[]{:S(2)}, u32[]{:S(2)}) %collective-permute-start.14) | collective-permute-done | bytes 917536 | tf_op jit(solution)/shard_map/ppermute | solution.py:233
  182.4 2.2 %collective-permute-done.11 = bf16[8,7,64,128]{3,2,1,0:T(8,128)(2,1)S(1)} collective-permute-done((bf16[8,7,64,128]{3,2,1,0:T(8,128)(2,1)S(1)}, bf16[8,7,64,128]{3,2,1,0:T(8,128)(2,1)S(1)}, u32[]{:S(2)}, u32[]{:S(2)}) %collective-permute-start.11) | collective-permute-done | bytes 917536 | tf_op jit(solution)/shard_map/ppermute | solution.py:233
  (72 shorter events, 18.6 us)
Async XLA Ops:
  1.1 14.9 %collective-permute-start = (bf16[16,128,128]{2,1,0:T(8,128)(2,1)S(1)}, bf16[16,128,128]{2,1,0:T(8,128)(2,1)S(1)}, u32[]{:S(2)}, u32[]{:S(2)}) collective-permute-start(bf16[16,128,128]{2,1,0:T(8,128)(2,1)S(1)} %slice.9), channel_id=1, source_target_pairs={{0,1},{1,0},{2,3},{3,2},{4,5},{5,4},{6,7},{7,6},{8,9},{9,8},{10,11... | collective-permute-start | bytes 1572872 | tf_op jit(solution)/shard_map/ppermute | solution.py:50
  4.1 34.4 %collective-permute-start.6 = (bf16[32,128,128]{2,1,0:T(8,128)(2,1)}, bf16[32,128,128]{2,1,0:T(8,128)(2,1)S(1)}, u32[]{:S(2)}, u32[]{:S(2)}) collective-permute-start(bf16[32,128,128]{2,1,0:T(8,128)(2,1)} %own.7), channel_id=1, source_target_pairs={{0,8},{8,16},{16,24},{1,9},{9,17},{17,25},{2,10},{10,18},{18,26},{... | collective-permute-start | bytes 3145736 | tf_op jit(solution)/shard_map/ppermute | solution.py:211
  5.6 32.9 %collective-permute-start.7 = (bf16[32,128,128]{2,1,0:T(8,128)(2,1)}, bf16[32,128,128]{2,1,0:T(8,128)(2,1)S(1)}, u32[]{:S(2)}, u32[]{:S(2)}) collective-permute-start(bf16[32,128,128]{2,1,0:T(8,128)(2,1)} %own.7), channel_id=1, source_target_pairs={{8,0},{16,8},{24,16},{9,1},{17,9},{25,17},{10,2},{18,10},{26,18},{... | collective-permute-start | bytes 3145736 | tf_op jit(solution)/shard_map/ppermute | solution.py:211
  16.0 22.5 %copy-start.2 = (bf16[16,128,128]{2,1,0:T(8,128)(2,1)}, bf16[16,128,128]{2,1,0:T(8,128)(2,1)S(1)}, u32[]{:S(2)}) copy-start(bf16[16,128,128]{2,1,0:T(8,128)(2,1)S(1)} %collective-permute-done.refs_0_) | copy-start | bytes 1572868
  16.0 8.2 %collective-permute-start.1 = (bf16[9,128,128]{2,1,0:T(8,128)(2,1)S(1)}, bf16[9,128,128]{2,1,0:T(8,128)(2,1)S(1)}, u32[]{:S(2)}, u32[]{:S(2)}) collective-permute-start(bf16[9,128,128]{2,1,0:T(8,128)(2,1)S(1)} %slice.10), channel_id=1, source_target_pairs={{0,1},{1,0},{2,3},{3,2},{4,5},{5,4},{6,7},{7,6},{8,9},{9,8},{10,11... | collective-permute-start | bytes 884744 | tf_op jit(solution)/shard_map/ppermute | solution.py:50
  17.8 20.7 %collective-permute-start.3 = (bf16[16,128,128]{2,1,0:T(8,128)(2,1)S(1)}, bf16[16,128,128]{2,1,0:T(8,128)(2,1)S(1)}, u32[]{:S(2)}, u32[]{:S(2)}) collective-permute-start(bf16[16,128,128]{2,1,0:T(8,128)(2,1)S(1)} %collective-permute-done.refs_0_), channel_id=1, source_target_pairs={{0,2},{2,4},{4,6},{3,1},{5,3},{7,5},{8,10},{10,12},{12,14},{11,9},... | collective-permute-start | bytes 1572872 | tf_op jit(solution)/shard_map/ppermute | solution.py:52
  24.2 14.4 %copy-start.4 = (bf16[9,128,128]{2,1,0:T(8,128)(2,1)}, bf16[9,128,128]{2,1,0:T(8,128)(2,1)S(1)}, u32[]{:S(2)}) copy-start(bf16[9,128,128]{2,1,0:T(8,128)(2,1)S(1)} %collective-permute-done.1.refs_1_) | copy-start | bytes 884740
  24.2 6.7 %collective-permute-start.5 = (bf16[7,128,128]{2,1,0:T(8,128)(2,1)S(1)}, bf16[7,128,128]{2,1,0:T(8,128)(2,1)S(1)}, u32[]{:S(2)}, u32[]{:S(2)}) collective-permute-start(bf16[7,128,128]{2,1,0:T(8,128)(2,1)S(1)} %slice.11), channel_id=1, source_target_pairs={{2,1},{4,3},{6,5},{1,2},{3,4},{5,6},{10,9},{12,11},{14,13},{9,10},... | collective-permute-start | bytes 688136 | tf_op jit(solution)/shard_map/ppermute | solution.py:54
  24.9 13.7 %collective-permute-start.4 = (bf16[9,128,128]{2,1,0:T(8,128)(2,1)S(1)}, bf16[9,128,128]{2,1,0:T(8,128)(2,1)S(1)}, u32[]{:S(2)}, u32[]{:S(2)}) collective-permute-start(bf16[9,128,128]{2,1,0:T(8,128)(2,1)S(1)} %collective-permute-done.1.refs_1_), channel_id=1, source_target_pairs={{0,2},{2,4},{4,6},{3,1},{5,3},{7,5},{8,10},{10,12},{12,14},{11,9},... | collective-permute-start | bytes 884744 | tf_op jit(solution)/shard_map/ppermute | solution.py:52
  30.9 7.5 %collective-permute-start.2 = (bf16[7,128,128]{2,1,0:T(8,128)(2,1)S(1)}, bf16[7,128,128]{2,1,0:T(8,128)(2,1)S(1)}, u32[]{:S(2)}, u32[]{:S(2)}) collective-permute-start(bf16[7,128,128]{2,1,0:T(8,128)(2,1)S(1)} %slice.11), channel_id=1, source_target_pairs={{0,1},{1,0},{2,3},{3,2},{4,5},{5,4},{6,7},{7,6},{8,9},{9,8},{10,11... | collective-permute-start | bytes 688136 | tf_op jit(solution)/shard_map/ppermute | solution.py:50
  44.7 21.3 %collective-permute-start.18 = (bf16[8,7,64,128]{3,2,1,0:T(8,128)(2,1)}, bf16[8,7,64,128]{3,2,1,0:T(8,128)(2,1)S(1)}, u32[]{:S(2)}, u32[]{:S(2)}) collective-permute-start(bf16[8,7,64,128]{3,2,1,0:T(8,128)(2,1)} %get-tuple-element.58), channel_id=1, source_target_pairs={{2,0},{4,2},{6,4},{7,6},{5,7},{3,5},{1,3},{0,1},{10,8},{12,10},{14... | collective-permute-start | bytes 2752520 | tf_op jit(solution)/shard_map/ppermute | solution.py:233
  48.1 23.5 %collective-permute-start.8 = (bf16[8,7,64,128]{3,2,1,0:T(8,128)(2,1)}, bf16[8,7,64,128]{3,2,1,0:T(8,128)(2,1)S(1)}, u32[]{:S(2)}, u32[]{:S(2)}) collective-permute-start(bf16[8,7,64,128]{3,2,1,0:T(8,128)(2,1)} %get-tuple-element.47), channel_id=1, source_target_pairs={{0,2},{2,4},{4,6},{6,7},{7,5},{5,3},{3,1},{1,0},{8,10},{10,12},{12... | collective-permute-start | bytes 2752520 | tf_op jit(solution)/shard_map/ppermute | solution.py:233
  52.7 13.3 %copy-start.16 = (bf16[8,7,64,128]{3,2,1,0:T(8,128)(2,1)S(1)}, bf16[8,7,64,128]{3,2,1,0:T(8,128)(2,1)}, u32[]{:S(2)}) copy-start(bf16[8,7,64,128]{3,2,1,0:T(8,128)(2,1)} %get-tuple-element.57) | copy-start | bytes 2752516
  58.7 10.1 %copy-start.17 = (bf16[8,7,64,128]{3,2,1,0:T(8,128)(2,1)S(1)}, bf16[8,7,64,128]{3,2,1,0:T(8,128)(2,1)}, u32[]{:S(2)}) copy-start(bf16[8,7,64,128]{3,2,1,0:T(8,128)(2,1)} %get-tuple-element.50) | copy-start | bytes 2752516
  58.7 12.9 %copy-start.13 = (bf16[8,7,64,128]{3,2,1,0:T(8,128)(2,1)S(1)}, bf16[8,7,64,128]{3,2,1,0:T(8,128)(2,1)}, u32[]{:S(2)}) copy-start(bf16[8,7,64,128]{3,2,1,0:T(8,128)(2,1)} %get-tuple-element.46) | copy-start | bytes 2752516
  58.7 32.5 %collective-permute-start.15 = (bf16[8,7,64,128]{3,2,1,0:T(8,128)(2,1)}, bf16[8,7,64,128]{3,2,1,0:T(8,128)(2,1)S(1)}, u32[]{:S(2)}, u32[]{:S(2)}) collective-permute-start(bf16[8,7,64,128]{3,2,1,0:T(8,128)(2,1)} %get-tuple-element.54), channel_id=1, source_target_pairs={{0,2},{2,4},{4,6},{6,7},{7,5},{5,3},{3,1},{1,0},{8,10},{10,12},{12... | collective-permute-start | bytes 2752520 | tf_op jit(solution)/shard_map/ppermute | solution.py:233
  66.4 26.5 %collective-permute-start.19 = (bf16[8,7,64,128]{3,2,1,0:T(8,128)(2,1)S(1)}, bf16[8,7,64,128]{3,2,1,0:T(8,128)(2,1)S(1)}, u32[]{:S(2)}, u32[]{:S(2)}) collective-permute-start(bf16[8,7,64,128]{3,2,1,0:T(8,128)(2,1)S(1)} %add_convert_fusion.3), channel_id=1, source_target_pairs={{2,0},{4,2},{6,4},{7,6},{5,7},{3,5},{1,3},{0,1},{10,8},{12,10},{14... | collective-permute-start | bytes 2752520 | tf_op jit(solution)/shard_map/ppermute | solution.py:233
  68.8 40.6 %collective-permute-start.12 = (bf16[8,7,64,128]{3,2,1,0:T(8,128)(2,1)S(1)}, bf16[8,7,64,128]{3,2,1,0:T(8,128)(2,1)S(1)}, u32[]{:S(2)}, u32[]{:S(2)}) collective-permute-start(bf16[8,7,64,128]{3,2,1,0:T(8,128)(2,1)S(1)} %copy-done.17), channel_id=1, source_target_pairs={{2,0},{4,2},{6,4},{7,6},{5,7},{3,5},{1,3},{0,1},{10,8},{12,10},{14... | collective-permute-start | bytes 2752520 | tf_op jit(solution)/shard_map/ppermute | solution.py:233
  71.9 40.2 %collective-permute-start.9 = (bf16[8,7,64,128]{3,2,1,0:T(8,128)(2,1)S(1)}, bf16[8,7,64,128]{3,2,1,0:T(8,128)(2,1)S(1)}, u32[]{:S(2)}, u32[]{:S(2)}) collective-permute-start(bf16[8,7,64,128]{3,2,1,0:T(8,128)(2,1)S(1)} %add_convert_fusion.11), channel_id=1, source_target_pairs={{0,2},{2,4},{4,6},{6,7},{7,5},{5,3},{3,1},{1,0},{8,10},{10,12},{12... | collective-permute-start | bytes 2752520 | tf_op jit(solution)/shard_map/ppermute | solution.py:233
  92.8 16.6 %copy-start.11 = (bf16[8,7,64,128]{3,2,1,0:T(8,128)(2,1)S(1)}, bf16[8,7,64,128]{3,2,1,0:T(8,128)(2,1)}, u32[]{:S(2)}) copy-start(bf16[8,7,64,128]{3,2,1,0:T(8,128)(2,1)} %get-tuple-element.49) | copy-start | bytes 2752516
  92.8 37.8 %collective-permute-start.16 = (bf16[8,7,64,128]{3,2,1,0:T(8,128)(2,1)S(1)}, bf16[8,7,64,128]{3,2,1,0:T(8,128)(2,1)S(1)}, u32[]{:S(2)}, u32[]{:S(2)}) collective-permute-start(bf16[8,7,64,128]{3,2,1,0:T(8,128)(2,1)S(1)} %add_convert_fusion.5), channel_id=1, source_target_pairs={{0,2},{2,4},{4,6},{6,7},{7,5},{5,3},{3,1},{1,0},{8,10},{10,12},{12... | collective-permute-start | bytes 2752520 | tf_op jit(solution)/shard_map/ppermute | solution.py:233
  93.2 19.0 %copy-start.9 = (bf16[8,7,64,128]{3,2,1,0:T(8,128)(2,1)S(1)}, bf16[8,7,64,128]{3,2,1,0:T(8,128)(2,1)}, u32[]{:S(2)}) copy-start(bf16[8,7,64,128]{3,2,1,0:T(8,128)(2,1)} %get-tuple-element.45) | copy-start | bytes 2752516
  93.2 39.0 %collective-permute-start.20 = (bf16[8,7,64,128]{3,2,1,0:T(8,128)(2,1)S(1)}, bf16[8,7,64,128]{3,2,1,0:T(8,128)(2,1)S(1)}, u32[]{:S(2)}, u32[]{:S(2)}) collective-permute-start(bf16[8,7,64,128]{3,2,1,0:T(8,128)(2,1)S(1)} %add_convert_fusion.2), channel_id=1, source_target_pairs={{2,0},{4,2},{6,4},{7,6},{5,7},{3,5},{1,3},{0,1},{10,8},{12,10},{14... | collective-permute-start | bytes 2752520 | tf_op jit(solution)/shard_map/ppermute | solution.py:233
  109.7 39.0 %collective-permute-start.13 = (bf16[8,7,64,128]{3,2,1,0:T(8,128)(2,1)S(1)}, bf16[8,7,64,128]{3,2,1,0:T(8,128)(2,1)S(1)}, u32[]{:S(2)}, u32[]{:S(2)}) collective-permute-start(bf16[8,7,64,128]{3,2,1,0:T(8,128)(2,1)S(1)} %add_convert_fusion.8), channel_id=1, source_target_pairs={{2,0},{4,2},{6,4},{7,6},{5,7},{3,5},{1,3},{0,1},{10,8},{12,10},{14... | collective-permute-start | bytes 2752520 | tf_op jit(solution)/shard_map/ppermute | solution.py:233
  112.5 39.0 %collective-permute-start.10 = (bf16[8,7,64,128]{3,2,1,0:T(8,128)(2,1)S(1)}, bf16[8,7,64,128]{3,2,1,0:T(8,128)(2,1)S(1)}, u32[]{:S(2)}, u32[]{:S(2)}) collective-permute-start(bf16[8,7,64,128]{3,2,1,0:T(8,128)(2,1)S(1)} %add_convert_fusion.10), channel_id=1, source_target_pairs={{0,2},{2,4},{4,6},{6,7},{7,5},{5,3},{3,1},{1,0},{8,10},{10,12},{12... | collective-permute-start | bytes 2752520 | tf_op jit(solution)/shard_map/ppermute | solution.py:233
  132.1 16.6 %copy-start.12 = (bf16[8,7,64,128]{3,2,1,0:T(8,128)(2,1)S(1)}, bf16[8,7,64,128]{3,2,1,0:T(8,128)(2,1)}, u32[]{:S(2)}) copy-start(bf16[8,7,64,128]{3,2,1,0:T(8,128)(2,1)} %get-tuple-element.48) | copy-start | bytes 2752516
  132.1 37.8 %collective-permute-start.17 = (bf16[8,7,64,128]{3,2,1,0:T(8,128)(2,1)S(1)}, bf16[8,7,64,128]{3,2,1,0:T(8,128)(2,1)S(1)}, u32[]{:S(2)}, u32[]{:S(2)}) collective-permute-start(bf16[8,7,64,128]{3,2,1,0:T(8,128)(2,1)S(1)} %add_convert_fusion.4), channel_id=1, source_target_pairs={{0,2},{2,4},{4,6},{6,7},{7,5},{5,3},{3,1},{1,0},{8,10},{10,12},{12... | collective-permute-start | bytes 2752520 | tf_op jit(solution)/shard_map/ppermute | solution.py:233
  132.5 19.0 %copy-start.10 = (bf16[8,7,64,128]{3,2,1,0:T(8,128)(2,1)S(1)}, bf16[8,7,64,128]{3,2,1,0:T(8,128)(2,1)}, u32[]{:S(2)}) copy-start(bf16[8,7,64,128]{3,2,1,0:T(8,128)(2,1)} %get-tuple-element.44) | copy-start | bytes 2752516
  132.6 37.3 %collective-permute-start.21 = (bf16[8,7,64,128]{3,2,1,0:T(8,128)(2,1)S(1)}, bf16[8,7,64,128]{3,2,1,0:T(8,128)(2,1)S(1)}, u32[]{:S(2)}, u32[]{:S(2)}) collective-permute-start(bf16[8,7,64,128]{3,2,1,0:T(8,128)(2,1)S(1)} %add_convert_fusion.1), channel_id=1, source_target_pairs={{2,0},{4,2},{6,4},{7,6},{5,7},{3,5},{1,3},{0,1},{10,8},{12,10},{14... | collective-permute-start | bytes 2752520 | tf_op jit(solution)/shard_map/ppermute | solution.py:233
  149.1 33.4 %collective-permute-start.14 = (bf16[8,7,64,128]{3,2,1,0:T(8,128)(2,1)S(1)}, bf16[8,7,64,128]{3,2,1,0:T(8,128)(2,1)S(1)}, u32[]{:S(2)}, u32[]{:S(2)}) collective-permute-start(bf16[8,7,64,128]{3,2,1,0:T(8,128)(2,1)S(1)} %add_convert_fusion.7), channel_id=1, source_target_pairs={{2,0},{4,2},{6,4},{7,6},{5,7},{3,5},{1,3},{0,1},{10,8},{12,10},{14... | collective-permute-start | bytes 2752520 | tf_op jit(solution)/shard_map/ppermute | solution.py:233
  151.8 32.8 %collective-permute-start.11 = (bf16[8,7,64,128]{3,2,1,0:T(8,128)(2,1)S(1)}, bf16[8,7,64,128]{3,2,1,0:T(8,128)(2,1)S(1)}, u32[]{:S(2)}, u32[]{:S(2)}) collective-permute-start(bf16[8,7,64,128]{3,2,1,0:T(8,128)(2,1)S(1)} %add_convert_fusion.9), channel_id=1, source_target_pairs={{0,2},{2,4},{4,6},{6,7},{7,5},{5,3},{3,1},{1,0},{8,10},{10,12},{12... | collective-permute-start | bytes 2752520 | tf_op jit(solution)/shard_map/ppermute | solution.py:233
  169.9 14.8 %copy-start.8 = (bf16[8,7,64,128]{3,2,1,0:T(8,128)(2,1)S(1)}, bf16[8,7,64,128]{3,2,1,0:T(8,128)(2,1)}, u32[]{:S(2)}) copy-start(bf16[8,7,64,128]{3,2,1,0:T(8,128)(2,1)} %get-tuple-element.43) | copy-start | bytes 2752516
  (8 other events, 31.7 us)

commit v6 on v5

--- a/solution.py
+++ b/solution.py
@@ -232,8 +232,8 @@
                 terms.append(got[sign, n - 2])
             got[sign, n] = lax.ppermute(terms[0] if n < 2 else add(*terms), "dev", perm)
     last = 2 * far - 2
-    low = add(part(0, 0), got[1, last], got[-1, last - 1])
-    high = add(part(0, 1), got[1, last - 1], got[-1, last])
+    low, high = lax.optimization_barrier((add(part(0, 0), got[-1, last - 1]), add(part(0, 1), got[1, last - 1])))
+    low, high = add(low, got[1, last]), add(high, got[-1, last])
     return jnp.concatenate([low, high], 2)
 
 

time: 187 us -> 187 us (level)
  waiting for transfers between devices: 90.4 us -> 93.2 us
  starting transfers between devices: 39.1 us -> 36.7 us
    ppermute x14, waiting for transfers between devices: 76.3 us -> 79 us  [on_device(): got[sign, n] = lax.ppermute(terms[0] if n < 2 else add(*terms), 'dev', perm)]
    ppermute x14, starting transfers between devices: 17.8 us -> 15.4 us  [on_device(): got[sign, n] = lax.ppermute(terms[0] if n < 2 else add(*terms), 'dev', perm)]
    convert_element_type x12 -> x14, other arithmetic: 7.99 us -> 6.84 us  [add(): return sum((t.astype(jnp.float32) for t in terms)).astype(jnp.bfloat16)]
  transfers between devices with their start and end apart: 22 -> 22, of which waited for: 12 -> 11; matrix products, arithmetic and copies ran while one was open for 5% -> 5% of each run, Pallas kernels for 20% -> 20%
where the time goes in v6:
time: 187 us; the launch traced here: 186 us
  waiting for transfers between devices  93.2 us (50%)
  Pallas kernels  42.6 us (23%)
  starting transfers between devices  36.7 us (20%)
  other arithmetic  8.24 us (4%)
  local copies, waits for them, and re-layouts  4.66 us (2%)
    ppermute x14, waiting for transfers between devices, on_device(): got[sign, n] = lax.ppermute(terms[0] if n < 2 else add(*terms), 'dev', perm)  79 us
    pallas_call x8, Pallas kernels, chunk(): pl.pallas_call(functools.partial(chunk_kernel, distance, cuts), out_shape...  42.6 us
    ppermute x14, starting transfers between devices, on_device(): got[sign, n] = lax.ppermute(terms[0] if n < 2 else add(*terms), 'dev', perm)  15.4 us
    ppermute x3, waiting for transfers between devices, halo_dev(): first.append(lax.ppermute(piece, 'dev', swap))  14.1 us
    ppermute x2, starting transfers between devices, halo_dev(): second.append(lax.ppermute(first[-1], 'dev', relay))  9.54 us
    ppermute x3, starting transfers between devices, halo_dev(): first.append(lax.ppermute(piece, 'dev', swap))  8.29 us
    convert_element_type x14, other arithmetic, add(): return sum((t.astype(jnp.float32) for t in terms)).astype(jnp.bfloat16)  6.84 us
  transfers between devices with their start and end apart: 22, of which 11 were waited for; matrix products, arithmetic and copies ran while one was open for 5% of the time, Pallas kernels for 20%

profile of v6, /device:TPU:0, one launch (start us, length us, event | category | flops | bytes accessed | tf_op | source)
XLA Modules:
  0.0 185.8 jit_solution(10201710162923747748)
XLA Ops:
  1.1 3.0 %collective-permute-start = (bf16[16,128,128]{2,1,0:T(8,128)(2,1)S(1)}, bf16[16,128,128]{2,1,0:T(8,128)(2,1)S(1)}, u32[]{:S(2)}, u32[]{:S(2)}) collective-permute-start(bf16[16,128,128]{2,1,0:T(8,128)(2,1)S(1)} %slice.9), channel_id=1, source_target_pairs={{0,1},{1,0},{2,3},{3,2},{4,5},{5,4},{6,7},{7,6},{8,9},{9,8},{10,11... | collective-permute-start | bytes 1572872 | tf_op jit(solution)/shard_map/ppermute | solution.py:50
  4.1 1.5 collective-permute-start.6
  5.6 1.3 collective-permute-start.7
  7.9 8.1 %collective-permute-done.refs_0_ = bf16[16,128,128]{2,1,0:T(8,128)(2,1)S(1)} collective-permute-done((bf16[16,128,128]{2,1,0:T(8,128)(2,1)S(1)}, bf16[16,128,128]{2,1,0:T(8,128)(2,1)S(1)}, u32[]{:S(2)}, u32[]{:S(2)}) %collective-permute-start) | collective-permute-done | bytes 524320 | tf_op jit(solution)/shard_map/ppermute | solution.py:50
  16.0 1.7 collective-permute-start.1
  17.8 3.5 %collective-permute-start.3 = (bf16[16,128,128]{2,1,0:T(8,128)(2,1)S(1)}, bf16[16,128,128]{2,1,0:T(8,128)(2,1)S(1)}, u32[]{:S(2)}, u32[]{:S(2)}) collective-permute-start(bf16[16,128,128]{2,1,0:T(8,128)(2,1)S(1)} %collective-permute-done.refs_0_), channel_id=1, source_target_pairs={{0,2},{2,4},{4,6},{3,1},{5,3},{7,5},{8,10},{10,12},{12,14},{11,9},... | collective-permute-start | bytes 1572872 | tf_op jit(solution)/shard_map/ppermute | solution.py:52
  22.2 2.0 %collective-permute-done.1.refs_1_ = bf16[9,128,128]{2,1,0:T(8,128)(2,1)S(1)} collective-permute-done((bf16[9,128,128]{2,1,0:T(8,128)(2,1)S(1)}, bf16[9,128,128]{2,1,0:T(8,128)(2,1)S(1)}, u32[]{:S(2)}, u32[]{:S(2)}) %collective-permute-start.1) | collective-permute-done | bytes 294944 | tf_op jit(solution)/shard_map/ppermute | solution.py:50
  24.9 6.0 %collective-permute-start.4 = (bf16[9,128,128]{2,1,0:T(8,128)(2,1)S(1)}, bf16[9,128,128]{2,1,0:T(8,128)(2,1)S(1)}, u32[]{:S(2)}, u32[]{:S(2)}) collective-permute-start(bf16[9,128,128]{2,1,0:T(8,128)(2,1)S(1)} %collective-permute-done.1.refs_1_), channel_id=1, source_target_pairs={{0,2},{2,4},{4,6},{3,1},{5,3},{7,5},{8,10},{10,12},{12,14},{11,9},... | collective-permute-start | bytes 884744 | tf_op jit(solution)/shard_map/ppermute | solution.py:52
  30.9 3.5 %collective-permute-start.2 = (bf16[7,128,128]{2,1,0:T(8,128)(2,1)S(1)}, bf16[7,128,128]{2,1,0:T(8,128)(2,1)S(1)}, u32[]{:S(2)}, u32[]{:S(2)}) collective-permute-start(bf16[7,128,128]{2,1,0:T(8,128)(2,1)S(1)} %slice.11), channel_id=1, source_target_pairs={{0,1},{1,0},{2,3},{3,2},{4,5},{5,4},{6,7},{7,6},{8,9},{9,8},{10,11... | collective-permute-start | bytes 688136 | tf_op jit(solution)/shard_map/ppermute | solution.py:50
  34.5 4.0 %collective-permute-done.2.refs_2_ = bf16[7,128,128]{2,1,0:T(8,128)(2,1)S(1)} collective-permute-done((bf16[7,128,128]{2,1,0:T(8,128)(2,1)S(1)}, bf16[7,128,128]{2,1,0:T(8,128)(2,1)S(1)}, u32[]{:S(2)}, u32[]{:S(2)}) %collective-permute-start.2) | collective-permute-done | bytes 229408 | tf_op jit(solution)/shard_map/ppermute | solution.py:50
  40.2 5.8 %shard_map.80 = (bf16[8,7,64,128]{3,2,1,0:T(8,128)(2,1)}, bf16[8,7,64,128]{3,2,1,0:T(8,128)(2,1)}) custom-call(s32[8]{0:T(128)} %constant.2.clone.places, s32[1,32]{1,0:T(1,128)} %bitcast.19, s32[32]{0:T(128)} %agg.15, s32[6,32]{1,0:T(8,128)} %bitcast.3, s32[7,32]{1,0:T(8,128)} %bitcast.11, bf16[32,7,128,128]{3,2,1,0:T(8,128)(2,1)} %a_ref.15, ...), custom_call_target="tpu_custom_call" | custom-call | flops 234881024 | bytes 12582912 | tf_op jit(solution)/shard_map/pallas_call | solution.py:172
  48.1 4.6 %shard_map.79 = (bf16[8,7,64,128]{3,2,1,0:T(8,128)(2,1)}, bf16[8,7,64,128]{3,2,1,0:T(8,128)(2,1)}) custom-call(s32[8]{0:T(128)} %constant.2.clone.places, s32[1,32]{1,0:T(1,128)} %bitcast.20, s32[32]{0:T(128)} %agg.15, s32[6,32]{1,0:T(8,128)} %bitcast.4, s32[7,32]{1,0:T(8,128)} %bitcast.12, bf16[32,7,128,128]{3,2,1,0:T(8,128)(2,1)} %a_ref.15, ...), custom_call_target="tpu_custom_call" | custom-call | flops 234881024 | bytes 12582912 | tf_op jit(solution)/shard_map/pallas_call | solution.py:172
  52.6 2.4 %collective-permute-start.11 = (bf16[8,7,64,128]{3,2,1,0:T(8,128)(2,1)}, bf16[8,7,64,128]{3,2,1,0:T(8,128)(2,1)S(1)}, u32[]{:S(2)}, u32[]{:S(2)}) collective-permute-start(bf16[8,7,64,128]{3,2,1,0:T(8,128)(2,1)} %get-tuple-element.52), channel_id=1, source_target_pairs={{0,2},{2,4},{4,6},{6,7},{7,5},{5,3},{3,1},{1,0},{8,10},{10,12},{12... | collective-permute-start | bytes 2752520 | tf_op jit(solution)/shard_map/ppermute | solution.py:233
  55.0 4.6 %shard_map.76 = (bf16[8,7,64,128]{3,2,1,0:T(8,128)(2,1)}, bf16[8,7,64,128]{3,2,1,0:T(8,128)(2,1)}) custom-call(s32[8]{0:T(128)} %constant.2.clone.places, s32[1,32]{1,0:T(1,128)} %bitcast.21, s32[32]{0:T(128)} %agg.15, s32[6,32]{1,0:T(8,128)} %bitcast.5, s32[7,32]{1,0:T(8,128)} %bitcast.13, bf16[32,7,128,128]{3,2,1,0:T(8,128)(2,1)} %a_ref.15, ...), custom_call_target="tpu_custom_call" | custom-call | flops 234881024 | bytes 12582912 | tf_op jit(solution)/shard_map/pallas_call | solution.py:172
  60.0 9.6 %collective-permute-done.14 = bf16[8,7,64,128]{3,2,1,0:T(8,128)(2,1)S(1)} collective-permute-done((bf16[8,7,64,128]{3,2,1,0:T(8,128)(2,1)}, bf16[8,7,64,128]{3,2,1,0:T(8,128)(2,1)S(1)}, u32[]{:S(2)}, u32[]{:S(2)}) %collective-permute-start.14) | collective-permute-done | bytes 917536 | tf_op jit(solution)/shard_map/ppermute | solution.py:233
  71.2 1.2 collective-permute-start.19
  72.4 4.6 %shard_map.78 = (bf16[8,7,64,128]{3,2,1,0:T(8,128)(2,1)}, bf16[8,7,64,128]{3,2,1,0:T(8,128)(2,1)}) custom-call(s32[8]{0:T(128)} %constant.2.clone.places, s32[1,32]{1,0:T(1,128)} %bitcast.22, s32[32]{0:T(128)} %agg.15, s32[6,32]{1,0:T(8,128)} %bitcast.6, s32[7,32]{1,0:T(8,128)} %bitcast.14, bf16[32,7,128,128]{3,2,1,0:T(8,128)(2,1)} %a_ref.15, ...), custom_call_target="tpu_custom_call" | custom-call | flops 234881024 | bytes 12582912 | tf_op jit(solution)/shard_map/pallas_call | solution.py:172
  77.0 5.3 %shard_map.75 = (bf16[8,7,64,128]{3,2,1,0:T(8,128)(2,1)}, bf16[8,7,64,128]{3,2,1,0:T(8,128)(2,1)}) custom-call(s32[8]{0:T(128)} %constant.2.clone.places, s32[1,32]{1,0:T(1,128)} %bitcast.23, s32[32]{0:T(128)} %agg.15, s32[6,32]{1,0:T(8,128)} %bitcast.7, s32[7,32]{1,0:T(8,128)} %bitcast.15, bf16[32,7,128,128]{3,2,1,0:T(8,128)(2,1)} %a_ref.15, ...), custom_call_target="tpu_custom_call" | custom-call | flops 234881024 | bytes 12582912 | tf_op jit(solution)/shard_map/pallas_call | solution.py:172
  82.3 6.9 %collective-permute-done.11 = bf16[8,7,64,128]{3,2,1,0:T(8,128)(2,1)S(1)} collective-permute-done((bf16[8,7,64,128]{3,2,1,0:T(8,128)(2,1)}, bf16[8,7,64,128]{3,2,1,0:T(8,128)(2,1)S(1)}, u32[]{:S(2)}, u32[]{:S(2)}) %collective-permute-start.11) | collective-permute-done | bytes 917536 | tf_op jit(solution)/shard_map/ppermute | solution.py:233
  90.9 1.2 collective-permute-start.9
  92.1 16.8 %collective-permute-done.15 = bf16[8,7,64,128]{3,2,1,0:T(8,128)(2,1)S(1)} collective-permute-done((bf16[8,7,64,128]{3,2,1,0:T(8,128)(2,1)S(1)}, bf16[8,7,64,128]{3,2,1,0:T(8,128)(2,1)S(1)}, u32[]{:S(2)}, u32[]{:S(2)}) %collective-permute-start.15) | collective-permute-done | bytes 917536 | tf_op jit(solution)/shard_map/ppermute | solution.py:233
  108.9 1.3 add_convert_fusion.6
  112.6 5.9 %shard_map.77 = (bf16[8,7,64,128]{3,2,1,0:T(8,128)(2,1)}, bf16[8,7,64,128]{3,2,1,0:T(8,128)(2,1)}) custom-call(s32[8]{0:T(128)} %constant.2.clone.places, s32[1,32]{1,0:T(1,128)} %bitcast.24, s32[32]{0:T(128)} %agg.15, s32[6,32]{1,0:T(8,128)} %bitcast.8, s32[7,32]{1,0:T(8,128)} %bitcast.16, bf16[32,7,128,128]{3,2,1,0:T(8,128)(2,1)} %a_ref.15, ...), custom_call_target="tpu_custom_call" | custom-call | flops 234881024 | bytes 12582912 | tf_op jit(solution)/shard_map/pallas_call | solution.py:172
  118.5 6.7 %shard_map.74 = (bf16[8,7,64,128]{3,2,1,0:T(8,128)(2,1)}, bf16[8,7,64,128]{3,2,1,0:T(8,128)(2,1)}) custom-call(s32[8]{0:T(128)} %constant.2.clone.places, s32[1,32]{1,0:T(1,128)} %bitcast.25, s32[32]{0:T(128)} %agg.15, s32[6,32]{1,0:T(8,128)} %bitcast.9, s32[7,32]{1,0:T(8,128)} %bitcast.17, bf16[32,7,128,128]{3,2,1,0:T(8,128)(2,1)} %a_ref.15, ...), custom_call_target="tpu_custom_call" | custom-call | flops 234881024 | bytes 12582912 | tf_op jit(solution)/shard_map/pallas_call | solution.py:172
  125.2 3.3 %collective-permute-done.12 = bf16[8,7,64,128]{3,2,1,0:T(8,128)(2,1)S(1)} collective-permute-done((bf16[8,7,64,128]{3,2,1,0:T(8,128)(2,1)S(1)}, bf16[8,7,64,128]{3,2,1,0:T(8,128)(2,1)S(1)}, u32[]{:S(2)}, u32[]{:S(2)}) %collective-permute-start.12) | collective-permute-done | bytes 917536 | tf_op jit(solution)/shard_map/ppermute | solution.py:233
  130.2 1.2 collective-permute-start.10
  131.4 16.8 %collective-permute-done.16 = bf16[8,7,64,128]{3,2,1,0:T(8,128)(2,1)S(1)} collective-permute-done((bf16[8,7,64,128]{3,2,1,0:T(8,128)(2,1)}, bf16[8,7,64,128]{3,2,1,0:T(8,128)(2,1)S(1)}, u32[]{:S(2)}, u32[]{:S(2)}) %collective-permute-start.16) | collective-permute-done | bytes 917536 | tf_op jit(solution)/shard_map/ppermute | solution.py:233
  151.0 5.1 %shard_map.73 = (bf16[8,7,64,128]{3,2,1,0:T(8,128)(2,1)}, bf16[8,7,64,128]{3,2,1,0:T(8,128)(2,1)}) custom-call(s32[8]{0:T(128)} %constant.2.clone.places, s32[1,32]{1,0:T(1,128)} %bitcast.26, s32[32]{0:T(128)} %agg.15, s32[6,32]{1,0:T(8,128)} %bitcast.10, s32[7,32]{1,0:T(8,128)} %bitcast.18, bf16[32,7,128,128]{3,2,1,0:T(8,128)(2,1)} %a_ref.15, ...), custom_call_target="tpu_custom_call" | custom-call | flops 234881024 | bytes 12582912 | tf_op jit(solution)/shard_map/pallas_call | solution.py:172
  156.2 11.7 %collective-permute-done.13 = bf16[8,7,64,128]{3,2,1,0:T(8,128)(2,1)S(1)} collective-permute-done((bf16[8,7,64,128]{3,2,1,0:T(8,128)(2,1)S(1)}, bf16[8,7,64,128]{3,2,1,0:T(8,128)(2,1)S(1)}, u32[]{:S(2)}, u32[]{:S(2)}) %collective-permute-start.13) | collective-permute-done | bytes 917536 | tf_op jit(solution)/shard_map/ppermute | solution.py:233
  167.8 1.5 add_convert_fusion.8
  169.7 12.8 %collective-permute-done.17 = bf16[8,7,64,128]{3,2,1,0:T(8,128)(2,1)S(1)} collective-permute-done((bf16[8,7,64,128]{3,2,1,0:T(8,128)(2,1)S(1)}, bf16[8,7,64,128]{3,2,1,0:T(8,128)(2,1)S(1)}, u32[]{:S(2)}, u32[]{:S(2)}) %collective-permute-start.17) | collective-permute-done | bytes 917536 | tf_op jit(solution)/shard_map/ppermute | solution.py:233
  184.4 1.4 pad_maximum_fusion
  (76 shorter events, 20.0 us)
Async XLA Ops:
  1.1 14.9 %collective-permute-start = (bf16[16,128,128]{2,1,0:T(8,128)(2,1)S(1)}, bf16[16,128,128]{2,1,0:T(8,128)(2,1)S(1)}, u32[]{:S(2)}, u32[]{:S(2)}) collective-permute-start(bf16[16,128,128]{2,1,0:T(8,128)(2,1)S(1)} %slice.9), channel_id=1, source_target_pairs={{0,1},{1,0},{2,3},{3,2},{4,5},{5,4},{6,7},{7,6},{8,9},{9,8},{10,11... | collective-permute-start | bytes 1572872 | tf_op jit(solution)/shard_map/ppermute | solution.py:50
  4.1 34.4 %collective-permute-start.6 = (bf16[32,128,128]{2,1,0:T(8,128)(2,1)}, bf16[32,128,128]{2,1,0:T(8,128)(2,1)S(1)}, u32[]{:S(2)}, u32[]{:S(2)}) collective-permute-start(bf16[32,128,128]{2,1,0:T(8,128)(2,1)} %own.7), channel_id=1, source_target_pairs={{0,8},{8,16},{16,24},{1,9},{9,17},{17,25},{2,10},{10,18},{18,26},{... | collective-permute-start | bytes 3145736 | tf_op jit(solution)/shard_map/ppermute | solution.py:211
  5.6 32.9 %collective-permute-start.7 = (bf16[32,128,128]{2,1,0:T(8,128)(2,1)}, bf16[32,128,128]{2,1,0:T(8,128)(2,1)S(1)}, u32[]{:S(2)}, u32[]{:S(2)}) collective-permute-start(bf16[32,128,128]{2,1,0:T(8,128)(2,1)} %own.7), channel_id=1, source_target_pairs={{8,0},{16,8},{24,16},{9,1},{17,9},{25,17},{10,2},{18,10},{26,18},{... | collective-permute-start | bytes 3145736 | tf_op jit(solution)/shard_map/ppermute | solution.py:211
  16.0 22.5 %copy-start.2 = (bf16[16,128,128]{2,1,0:T(8,128)(2,1)}, bf16[16,128,128]{2,1,0:T(8,128)(2,1)S(1)}, u32[]{:S(2)}) copy-start(bf16[16,128,128]{2,1,0:T(8,128)(2,1)S(1)} %collective-permute-done.refs_0_) | copy-start | bytes 1572868
  16.0 8.2 %collective-permute-start.1 = (bf16[9,128,128]{2,1,0:T(8,128)(2,1)S(1)}, bf16[9,128,128]{2,1,0:T(8,128)(2,1)S(1)}, u32[]{:S(2)}, u32[]{:S(2)}) collective-permute-start(bf16[9,128,128]{2,1,0:T(8,128)(2,1)S(1)} %slice.10), channel_id=1, source_target_pairs={{0,1},{1,0},{2,3},{3,2},{4,5},{5,4},{6,7},{7,6},{8,9},{9,8},{10,11... | collective-permute-start | bytes 884744 | tf_op jit(solution)/shard_map/ppermute | solution.py:50
  17.8 20.7 %collective-permute-start.3 = (bf16[16,128,128]{2,1,0:T(8,128)(2,1)S(1)}, bf16[16,128,128]{2,1,0:T(8,128)(2,1)S(1)}, u32[]{:S(2)}, u32[]{:S(2)}) collective-permute-start(bf16[16,128,128]{2,1,0:T(8,128)(2,1)S(1)} %collective-permute-done.refs_0_), channel_id=1, source_target_pairs={{0,2},{2,4},{4,6},{3,1},{5,3},{7,5},{8,10},{10,12},{12,14},{11,9},... | collective-permute-start | bytes 1572872 | tf_op jit(solution)/shard_map/ppermute | solution.py:52
  24.2 14.4 %copy-start.4 = (bf16[9,128,128]{2,1,0:T(8,128)(2,1)}, bf16[9,128,128]{2,1,0:T(8,128)(2,1)S(1)}, u32[]{:S(2)}) copy-start(bf16[9,128,128]{2,1,0:T(8,128)(2,1)S(1)} %collective-permute-done.1.refs_1_) | copy-start | bytes 884740
  24.2 6.7 %collective-permute-start.5 = (bf16[7,128,128]{2,1,0:T(8,128)(2,1)S(1)}, bf16[7,128,128]{2,1,0:T(8,128)(2,1)S(1)}, u32[]{:S(2)}, u32[]{:S(2)}) collective-permute-start(bf16[7,128,128]{2,1,0:T(8,128)(2,1)S(1)} %slice.11), channel_id=1, source_target_pairs={{2,1},{4,3},{6,5},{1,2},{3,4},{5,6},{10,9},{12,11},{14,13},{9,10},... | collective-permute-start | bytes 688136 | tf_op jit(solution)/shard_map/ppermute | solution.py:54
  24.9 13.7 %collective-permute-start.4 = (bf16[9,128,128]{2,1,0:T(8,128)(2,1)S(1)}, bf16[9,128,128]{2,1,0:T(8,128)(2,1)S(1)}, u32[]{:S(2)}, u32[]{:S(2)}) collective-permute-start(bf16[9,128,128]{2,1,0:T(8,128)(2,1)S(1)} %collective-permute-done.1.refs_1_), channel_id=1, source_target_pairs={{0,2},{2,4},{4,6},{3,1},{5,3},{7,5},{8,10},{10,12},{12,14},{11,9},... | collective-permute-start | bytes 884744 | tf_op jit(solution)/shard_map/ppermute | solution.py:52
  30.9 7.5 %collective-permute-start.2 = (bf16[7,128,128]{2,1,0:T(8,128)(2,1)S(1)}, bf16[7,128,128]{2,1,0:T(8,128)(2,1)S(1)}, u32[]{:S(2)}, u32[]{:S(2)}) collective-permute-start(bf16[7,128,128]{2,1,0:T(8,128)(2,1)S(1)} %slice.11), channel_id=1, source_target_pairs={{0,1},{1,0},{2,3},{3,2},{4,5},{5,4},{6,7},{7,6},{8,9},{9,8},{10,11... | collective-permute-start | bytes 688136 | tf_op jit(solution)/shard_map/ppermute | solution.py:50
  46.0 23.6 %collective-permute-start.14 = (bf16[8,7,64,128]{3,2,1,0:T(8,128)(2,1)}, bf16[8,7,64,128]{3,2,1,0:T(8,128)(2,1)S(1)}, u32[]{:S(2)}, u32[]{:S(2)}) collective-permute-start(bf16[8,7,64,128]{3,2,1,0:T(8,128)(2,1)} %get-tuple-element.57), channel_id=1, source_target_pairs={{0,2},{2,4},{4,6},{6,7},{7,5},{5,3},{3,1},{1,0},{8,10},{10,12},{12... | collective-permute-start | bytes 2752520 | tf_op jit(solution)/shard_map/ppermute | solution.py:233
  46.9 23.9 %collective-permute-start.18 = (bf16[8,7,64,128]{3,2,1,0:T(8,128)(2,1)}, bf16[8,7,64,128]{3,2,1,0:T(8,128)(2,1)S(1)}, u32[]{:S(2)}, u32[]{:S(2)}) collective-permute-start(bf16[8,7,64,128]{3,2,1,0:T(8,128)(2,1)} %get-tuple-element.62), channel_id=1, source_target_pairs={{2,0},{4,2},{6,4},{7,6},{5,7},{3,5},{1,3},{0,1},{10,8},{12,10},{14... | collective-permute-start | bytes 2752520 | tf_op jit(solution)/shard_map/ppermute | solution.py:233
  52.6 16.9 %copy-start.14 = (bf16[8,7,64,128]{3,2,1,0:T(8,128)(2,1)S(1)}, bf16[8,7,64,128]{3,2,1,0:T(8,128)(2,1)}, u32[]{:S(2)}) copy-start(bf16[8,7,64,128]{3,2,1,0:T(8,128)(2,1)} %get-tuple-element.56) | copy-start | bytes 2752516
  52.6 36.6 %collective-permute-start.11 = (bf16[8,7,64,128]{3,2,1,0:T(8,128)(2,1)}, bf16[8,7,64,128]{3,2,1,0:T(8,128)(2,1)S(1)}, u32[]{:S(2)}, u32[]{:S(2)}) collective-permute-start(bf16[8,7,64,128]{3,2,1,0:T(8,128)(2,1)} %get-tuple-element.52), channel_id=1, source_target_pairs={{0,2},{2,4},{4,6},{6,7},{7,5},{5,3},{3,1},{1,0},{8,10},{10,12},{12... | collective-permute-start | bytes 2752520 | tf_op jit(solution)/shard_map/ppermute | solution.py:233
  59.6 11.2 %copy-start.12 = (bf16[8,7,64,128]{3,2,1,0:T(8,128)(2,1)S(1)}, bf16[8,7,64,128]{3,2,1,0:T(8,128)(2,1)}, u32[]{:S(2)}) copy-start(bf16[8,7,64,128]{3,2,1,0:T(8,128)(2,1)} %get-tuple-element.61) | copy-start | bytes 2752516
  59.6 30.9 %collective-permute-start.8 = (bf16[8,7,64,128]{3,2,1,0:T(8,128)(2,1)}, bf16[8,7,64,128]{3,2,1,0:T(8,128)(2,1)S(1)}, u32[]{:S(2)}, u32[]{:S(2)}) collective-permute-start(bf16[8,7,64,128]{3,2,1,0:T(8,128)(2,1)} %get-tuple-element.48), channel_id=1, source_target_pairs={{2,0},{4,2},{6,4},{7,6},{5,7},{3,5},{1,3},{0,1},{10,8},{12,10},{14... | collective-permute-start | bytes 2752520 | tf_op jit(solution)/shard_map/ppermute | solution.py:233
  69.9 39.0 %collective-permute-start.15 = (bf16[8,7,64,128]{3,2,1,0:T(8,128)(2,1)S(1)}, bf16[8,7,64,128]{3,2,1,0:T(8,128)(2,1)S(1)}, u32[]{:S(2)}, u32[]{:S(2)}) collective-permute-start(bf16[8,7,64,128]{3,2,1,0:T(8,128)(2,1)S(1)} %add_convert_fusion.7), channel_id=1, source_target_pairs={{0,2},{2,4},{4,6},{6,7},{7,5},{5,3},{3,1},{1,0},{8,10},{10,12},{12... | collective-permute-start | bytes 2752520 | tf_op jit(solution)/shard_map/ppermute | solution.py:233
  71.2 39.8 %collective-permute-start.19 = (bf16[8,7,64,128]{3,2,1,0:T(8,128)(2,1)S(1)}, bf16[8,7,64,128]{3,2,1,0:T(8,128)(2,1)S(1)}, u32[]{:S(2)}, u32[]{:S(2)}) collective-permute-start(bf16[8,7,64,128]{3,2,1,0:T(8,128)(2,1)S(1)} %add_convert_fusion.3), channel_id=1, source_target_pairs={{2,0},{4,2},{6,4},{7,6},{5,7},{3,5},{1,3},{0,1},{10,8},{12,10},{14... | collective-permute-start | bytes 2752520 | tf_op jit(solution)/shard_map/ppermute | solution.py:233
  77.0 12.2 %copy-start.17 = (bf16[8,7,64,128]{3,2,1,0:T(8,128)(2,1)S(1)}, bf16[8,7,64,128]{3,2,1,0:T(8,128)(2,1)}, u32[]{:S(2)}) copy-start(bf16[8,7,64,128]{3,2,1,0:T(8,128)(2,1)} %get-tuple-element.51) | copy-start | bytes 2752516
  89.6 19.3 %copy-start.10 = (bf16[8,7,64,128]{3,2,1,0:T(8,128)(2,1)S(1)}, bf16[8,7,64,128]{3,2,1,0:T(8,128)(2,1)}, u32[]{:S(2)}) copy-start(bf16[8,7,64,128]{3,2,1,0:T(8,128)(2,1)} %get-tuple-element.55) | copy-start | bytes 2752516
  89.6 39.0 %collective-permute-start.12 = (bf16[8,7,64,128]{3,2,1,0:T(8,128)(2,1)S(1)}, bf16[8,7,64,128]{3,2,1,0:T(8,128)(2,1)S(1)}, u32[]{:S(2)}, u32[]{:S(2)}) collective-permute-start(bf16[8,7,64,128]{3,2,1,0:T(8,128)(2,1)S(1)} %add_convert_fusion.10), channel_id=1, source_target_pairs={{0,2},{2,4},{4,6},{6,7},{7,5},{5,3},{3,1},{1,0},{8,10},{10,12},{12... | collective-permute-start | bytes 2752520 | tf_op jit(solution)/shard_map/ppermute | solution.py:233
  90.8 20.2 %copy-start.8 = (bf16[8,7,64,128]{3,2,1,0:T(8,128)(2,1)S(1)}, bf16[8,7,64,128]{3,2,1,0:T(8,128)(2,1)}, u32[]{:S(2)}) copy-start(bf16[8,7,64,128]{3,2,1,0:T(8,128)(2,1)} %get-tuple-element.60) | copy-start | bytes 2752516
  90.9 39.0 %collective-permute-start.9 = (bf16[8,7,64,128]{3,2,1,0:T(8,128)(2,1)S(1)}, bf16[8,7,64,128]{3,2,1,0:T(8,128)(2,1)S(1)}, u32[]{:S(2)}, u32[]{:S(2)}) collective-permute-start(bf16[8,7,64,128]{3,2,1,0:T(8,128)(2,1)S(1)} %add_convert_fusion.13), channel_id=1, source_target_pairs={{2,0},{4,2},{6,4},{7,6},{5,7},{3,5},{1,3},{0,1},{10,8},{12,10},{14... | collective-permute-start | bytes 2752520 | tf_op jit(solution)/shard_map/ppermute | solution.py:233
  110.1 38.1 %collective-permute-start.16 = (bf16[8,7,64,128]{3,2,1,0:T(8,128)(2,1)}, bf16[8,7,64,128]{3,2,1,0:T(8,128)(2,1)S(1)}, u32[]{:S(2)}, u32[]{:S(2)}) collective-permute-start(bf16[8,7,64,128]{3,2,1,0:T(8,128)(2,1)} %add_convert_fusion.6), channel_id=1, source_target_pairs={{0,2},{2,4},{4,6},{6,7},{7,5},{5,3},{3,1},{1,0},{8,10},{10,12},{12... | collective-permute-start | bytes 2752520 | tf_op jit(solution)/shard_map/ppermute | solution.py:233
  111.4 38.1 %collective-permute-start.20 = (bf16[8,7,64,128]{3,2,1,0:T(8,128)(2,1)S(1)}, bf16[8,7,64,128]{3,2,1,0:T(8,128)(2,1)S(1)}, u32[]{:S(2)}, u32[]{:S(2)}) collective-permute-start(bf16[8,7,64,128]{3,2,1,0:T(8,128)(2,1)S(1)} %add_convert_fusion.2), channel_id=1, source_target_pairs={{2,0},{4,2},{6,4},{7,6},{5,7},{3,5},{1,3},{0,1},{10,8},{12,10},{14... | collective-permute-start | bytes 2752520 | tf_op jit(solution)/shard_map/ppermute | solution.py:233
  128.9 19.3 %copy-start.11 = (bf16[8,7,64,128]{3,2,1,0:T(8,128)(2,1)S(1)}, bf16[8,7,64,128]{3,2,1,0:T(8,128)(2,1)}, u32[]{:S(2)}) copy-start(bf16[8,7,64,128]{3,2,1,0:T(8,128)(2,1)} %get-tuple-element.54) | copy-start | bytes 2752516
  128.9 39.0 %collective-permute-start.13 = (bf16[8,7,64,128]{3,2,1,0:T(8,128)(2,1)S(1)}, bf16[8,7,64,128]{3,2,1,0:T(8,128)(2,1)S(1)}, u32[]{:S(2)}, u32[]{:S(2)}) collective-permute-start(bf16[8,7,64,128]{3,2,1,0:T(8,128)(2,1)S(1)} %add_convert_fusion.9), channel_id=1, source_target_pairs={{0,2},{2,4},{4,6},{6,7},{7,5},{5,3},{3,1},{1,0},{8,10},{10,12},{12... | collective-permute-start | bytes 2752520 | tf_op jit(solution)/shard_map/ppermute | solution.py:233
  130.2 19.3 %copy-start.9 = (bf16[8,7,64,128]{3,2,1,0:T(8,128)(2,1)S(1)}, bf16[8,7,64,128]{3,2,1,0:T(8,128)(2,1)}, u32[]{:S(2)}) copy-start(bf16[8,7,64,128]{3,2,1,0:T(8,128)(2,1)} %get-tuple-element.59) | copy-start | bytes 2752516
  130.2 39.2 %collective-permute-start.10 = (bf16[8,7,64,128]{3,2,1,0:T(8,128)(2,1)S(1)}, bf16[8,7,64,128]{3,2,1,0:T(8,128)(2,1)S(1)}, u32[]{:S(2)}, u32[]{:S(2)}) collective-permute-start(bf16[8,7,64,128]{3,2,1,0:T(8,128)(2,1)S(1)} %add_convert_fusion.12), channel_id=1, source_target_pairs={{2,0},{4,2},{6,4},{7,6},{5,7},{3,5},{1,3},{0,1},{10,8},{12,10},{14... | collective-permute-start | bytes 2752520 | tf_op jit(solution)/shard_map/ppermute | solution.py:233
  148.5 34.0 %collective-permute-start.17 = (bf16[8,7,64,128]{3,2,1,0:T(8,128)(2,1)S(1)}, bf16[8,7,64,128]{3,2,1,0:T(8,128)(2,1)S(1)}, u32[]{:S(2)}, u32[]{:S(2)}) collective-permute-start(bf16[8,7,64,128]{3,2,1,0:T(8,128)(2,1)S(1)} %add_convert_fusion.5), channel_id=1, source_target_pairs={{0,2},{2,4},{4,6},{6,7},{7,5},{5,3},{3,1},{1,0},{8,10},{10,12},{12... | collective-permute-start | bytes 2752520 | tf_op jit(solution)/shard_map/ppermute | solution.py:233
  149.8 34.2 %collective-permute-start.21 = (bf16[8,7,64,128]{3,2,1,0:T(8,128)(2,1)S(1)}, bf16[8,7,64,128]{3,2,1,0:T(8,128)(2,1)S(1)}, u32[]{:S(2)}, u32[]{:S(2)}) collective-permute-start(bf16[8,7,64,128]{3,2,1,0:T(8,128)(2,1)S(1)} %add_convert_fusion.1), channel_id=1, source_target_pairs={{2,0},{4,2},{6,4},{7,6},{5,7},{3,5},{1,3},{0,1},{10,8},{12,10},{14... | collective-permute-start | bytes 2752520 | tf_op jit(solution)/shard_map/ppermute | solution.py:233
  156.2 13.2 %copy-start.13 = (bf16[8,7,64,128]{3,2,1,0:T(8,128)(2,1)S(1)}, bf16[8,7,64,128]{3,2,1,0:T(8,128)(2,1)}, u32[]{:S(2)}) copy-start(bf16[8,7,64,128]{3,2,1,0:T(8,128)(2,1)} %get-tuple-element.45) | copy-start | bytes 2752516
  (9 other events, 36.5 us)
